TPU v7x, 128 devices: a whole 4x4x4 slice. The times are simulated.
128 devices in a mesh: seq: 32 (over y, z, core), tile: 4 (over x).
Axes of the slice: x: 4, y: 4, z: 4, core: 2. Of those that a mesh axis runs over, the one named last changes fastest.
Arguments:
- tile_features: bfloat16 [16384, 1536], P(('seq', 'tile')), may hold values from -36 to 36
- gate_weight: bfloat16 [1536, 2048], replicated, may hold values from -0.15625 to 0.15625
- up_weight: bfloat16 [1536, 2048], replicated, may hold values from -0.15625 to 0.15625
- down_weight: bfloat16 [2048, 1536], replicated, may hold values from -0.125 to 0.125
- input_projection_weight: bfloat16 [1536, 768], replicated
- query_key_value_weight: bfloat16 [768, 2304], replicated
- positions: int32 [16384], replicated, may hold values from 0 to 16383, as said below
- dilation_shift: int32 [2, 16], replicated, may hold values from 0 to 15, as said below
- slide_output_gradient: bfloat16 [16384, 768], P('seq', 'tile'), may hold values from -6 to 6
Outputs:
- slide_out: bfloat16 [16384, 768], P('seq', 'tile')
- tile_grad: bfloat16 [16384, 1536], P(('seq', 'tile'))
Inputs may be any that keep to these rules, and one draw needn't show every extreme that they name: Each slide position belongs to exactly one tile. Of one device's tiles at most 8 fall in one block of 512 positions, and in every draw some device reaches 8. `dilation_shift`: row 0 lies below 4, row 1 below 16.
All inputs are finite; a program needn't handle non-finite values.
Results may differ from a plain program's by a relative error of at most 0.039.
Values may be sent and summed in bfloat16 or wider, within the bound.
No kernel may reach another device: no remote copies, remote signals or barrier semaphores. Data moves between devices by JAX's collectives and lax.ppermute only.
A program may use at most 128 MiB of HBM per device.

v0:
```python
import jax
import jax.numpy as jnp
from jax import lax
from jax.experimental import pallas as pl
from jax.experimental.pallas import tpu as pltpu
from jax.sharding import PartitionSpec as P

HEADS = 16
HD = 48
EPSILON = 1e-06
SOFT_CAP = 50.0
SCALE = HD**-0.5
BLK = 512
SLOTS = 8
BF = jnp.bfloat16
F32 = jnp.float32
I32 = jnp.int32

NN = (((1,), (0,)), ((), ()))
NT = (((1,), (1,)), ((), ()))
TN = (((0,), (0,)), ((), ()))


def mm(a, b, dims=NN):
    return lax.dot_general(a, b, dims, preferred_element_type=F32)


def iota(shape, dim):
    return lax.broadcasted_iota(I32, shape, dim)


def class_order(row):
    return (row & 3) * 128 + ((row >> 2) & 3) * 32 + (row >> 4)


def order_matrix():
    return jnp.where(class_order(iota((BLK, BLK), 0)) == iota((BLK, BLK), 1), 1.0, 0.0).astype(BF)


def normalize(values):
    centred = values - jnp.mean(values, axis=-1, keepdims=True)
    inv_std = lax.rsqrt(jnp.mean(centred * centred, axis=-1, keepdims=True) + EPSILON)
    return (centred * inv_std, inv_std)


def norm_back(normed, inv_std, grads):
    mean_grad = jnp.mean(grads, axis=-1, keepdims=True)
    mean_cross = jnp.mean(grads * normed, axis=-1, keepdims=True)
    return (grads - mean_grad - normed * mean_cross) * inv_std


def call(kernel, outs, scratch=(), n_smem=0, limit=40):
    def run(*args):
        specs = [pl.BlockSpec(memory_space=pltpu.SMEM)] * n_smem
        specs += [pl.BlockSpec(memory_space=pltpu.VMEM)] * (len(args) - n_smem)
        shapes = [jax.ShapeDtypeStruct(s, d) for s, d in outs]
        out_specs = [pl.BlockSpec(memory_space=pltpu.VMEM)] * len(outs)
        return pl.pallas_call(
            kernel,
            out_shape=shapes,
            in_specs=specs,
            out_specs=out_specs,
            scratch_shapes=list(scratch),
            compiler_params=pltpu.CompilerParams(vmem_limit_bytes=limit * 1024 * 1024),
        )(*args)

    return run


def order_kernel(grad_ref, out_ref):
    out_ref[...] = mm(grad_ref[...], order_matrix(), TN).astype(BF)


def pack_kernel(qkv_ref, x_ref, prow_ref, pcol_ref, out_ref, heads_ref, wide_ref):
    brow = prow_ref[...] >> 9
    bcol = pcol_ref[...] >> 9
    n = prow_ref.shape[1]
    before = iota((n, n), 0) < iota((n, n), 1)
    rank = jnp.sum(jnp.where((bcol == brow) & before, 1, 0), axis=0, keepdims=True)
    code = brow * SLOTS + rank
    width = HEADS * HD
    for h in range(HEADS):
        for part in range(3):
            heads_ref[:, 192 * h + HD * part : 192 * h + HD * part + HD] = qkv_ref[
                :, part * width + h * HD : part * width + h * HD + HD
            ]
        heads_ref[:, 192 * h + 144 : 192 * h + 192] = x_ref[:, h * HD : h * HD + HD]
    seat = iota((64, n), 0)
    heads = heads_ref[...]
    for block in range(4):
        want = ((seat >> 3) * 4 + block) * SLOTS + (seat & 7)
        picker = jnp.where(code == want, 1.0, 0.0).astype(BF)
        rows = mm(picker, heads)
        for h in range(HEADS):
            t, j = h // 4, h % 4
            lane = (j ^ block) * 192
            wide_ref[:, j * 4 + t, :, lane : lane + 192] = rows[:, 192 * h : 192 * h + 192].reshape(
                8, SLOTS, 192
            )
    out_ref[...] = wide_ref[...].reshape(8 * 16 * SLOTS, 768).astype(BF)


def place_kernel(off_ref, recv_ref, tab_ref, y_ref, yt_ref, y2_ref):
    o2 = pl.multiple_of(off_ref[1], 32)
    for d in range(4):
        tab = tab_ref[d : d + 1, :]
        onehot = jnp.where(iota((BLK, tab.shape[1]), 0) == tab, 1.0, 0.0).astype(BF)
        y = mm(onehot, recv_ref[:, 192 * d : 192 * d + 192])
        y_ref[d] = y.astype(BF)
        yt_ref[d] = y.T.astype(BF)
        y2_ref[32 * d : 32 * d + 32, :] = y_ref[d, pl.ds(o2, 32), :]


def score_rows(keys, queries_t, e_store, m_store):
    scores = mm(keys, queries_t)
    count, width = scores.shape
    total = jnp.zeros((8, width), F32)
    step = 64
    for c in range(0, count, step):
        t = jnp.tanh(scores[c : c + step] * (SCALE / SOFT_CAP))
        e = jnp.exp(SOFT_CAP * t)
        total = total + jnp.sum(e.reshape(step // 8, 8, width), axis=0)
        e_store(c, step, e.astype(BF))
        m_store(c, step, (e * (1.0 - t * t) * SCALE).astype(BF))
    return jnp.sum(total, axis=0, keepdims=True)


def forward_kernel(off_ref, y_ref, yt_ref, e0_ref, m0_ref, e1_ref, m1_ref, u_ref, l_ref):
    o1 = pl.multiple_of(off_ref[0], 128)

    def block(d, carry):
        def e_store(c, n, v):
            e0_ref[d, c : c + n, :] = v

        def m_store(c, n, v):
            m0_ref[d, c : c + n, :] = v

        l_ref[d] = score_rows(y_ref[d, :, 48:96], yt_ref[d, 0:48, :], e_store, m_store)
        u_ref[d] = mm(yt_ref[d, 96:144, :], e0_ref[d])
        return carry

    lax.fori_loop(0, 4, block, 0)

    def e_store(c, n, v):
        e1_ref[c : c + n, :] = v

    def m_store(c, n, v):
        m1_ref[c : c + n, :] = v

    keys = jnp.concatenate([y_ref[d, pl.ds(o1, 128), 48:96] for d in range(4)], axis=0)
    queries = jnp.concatenate([yt_ref[d, 0:48, pl.ds(o1, 128)] for d in range(4)], axis=1)
    values = jnp.concatenate([yt_ref[d, 96:144, pl.ds(o1, 128)] for d in range(4)], axis=1)
    l1 = score_rows(keys, queries, e_store, m_store)
    u1 = mm(values, e1_ref[...])
    for d in range(4):
        u_ref[d, :, pl.ds(o1, 128)] += u1[:, 128 * d : 128 * d + 128]
        l_ref[d, :, pl.ds(o1, 128)] += l1[:, 128 * d : 128 * d + 128]


def turned(value, shift):
    return pltpu.roll(value, shift & 127, 1)


def wide_kernel(
    off_ref,
    yt_ref,
    a0_ref,
    a1_ref,
    a2_ref,
    a3_ref,
    u_ref,
    l_ref,
    g0_ref,
    g1_ref,
    g2_ref,
    g3_ref,
    so_ref,
    gs_ref,
    ds_ref,
    own_ref,
    send_ref,
    dq_ref,
    e2_ref,
    m2_ref,
    usum_ref,
    lsum_ref,
):
    o2 = off_ref[1]
    base = pl.multiple_of((o2 >> 7) << 7, 128)
    part = (o2 >> 5) & 3
    y2 = jnp.concatenate([a0_ref[...], a1_ref[...], a2_ref[...], a3_ref[...]], axis=0)
    keys, values = y2[:, 48:96], y2[:, 96:144]
    both_t = y2[:, 48:144].astype(F32).T.astype(BF)
    query_t = a0_ref[:, 0:48].astype(F32).T.astype(BF)

    def e_store(c, n, v):
        e2_ref[c : c + n, :] = v

    def m_store(c, n, v):
        m2_ref[c : c + n, :] = v

    l2 = score_rows(keys, query_t, e_store, m_store)
    u2 = mm(both_t[48:96], e2_ref[...])
    l2w = jnp.broadcast_to(l2, (8, 128))
    lane = iota((1, 128), 1) >> 5
    gs2 = jnp.zeros((48, 128), F32)
    ds2 = jnp.zeros((8, 128), F32)
    for d in range(4):
        grad_ref = (g0_ref, g1_ref, g2_ref, g3_ref)[d]
        here = lane == part
        shift = 32 * (part - d)
        usum_ref[...] = u_ref[d]
        lsum_ref[...] = l_ref[d]
        usum_ref[:, pl.ds(base, 128)] += jnp.where(here, turned(u2, shift), 0.0)
        lsum_ref[:, pl.ds(base, 128)] += jnp.where(here, turned(l2w, shift), 0.0)[0:1]
        inv = 1.0 / lsum_ref[...]
        att = usum_ref[...] * inv
        so_ref[d] = (yt_ref[d, 144:192, :].astype(F32) + att).astype(BF)
        gs = (grad_ref[...].astype(F32) * inv).astype(BF)
        gs_ref[d] = gs
        ds_ref[d] = jnp.sum(gs.astype(F32) * att, axis=0, keepdims=True)
        gs_wide = gs_ref[d, :, pl.ds(base, 128)].astype(F32)
        ds_wide = jnp.broadcast_to(ds_ref[d, :, pl.ds(base, 128)], (8, 128))
        gs2 = jnp.where(lane == d, turned(gs_wide, -shift), gs2)
        ds2 = jnp.where(lane == d, turned(ds_wide, -shift), ds2)
    gs2 = gs2.astype(BF)
    dp = mm(values, gs2)
    dscore = (m2_ref[...].astype(F32) * (dp - ds2[0:1])).astype(BF)
    dq_ref[...] = mm(both_t[0:48], dscore)
    dk = mm(query_t, dscore, NT)
    dv = mm(gs2, e2_ref[...], NT)
    dkv = jnp.concatenate([dk, dv], axis=0)
    own_ref[...] = dkv[:, 0:128]
    for e in range(3):
        send_ref[e] = dkv[:, 128 * e + 128 : 128 * e + 256].astype(BF)


def dscores(values, gs, ds, m_load, store):
    dp = mm(values, gs)
    step = 64
    for c in range(0, dp.shape[0], step):
        store(c, step, (m_load(c, step).astype(F32) * (dp[c : c + step] - ds)).astype(BF))


def backward_kernel(
    off_ref, y_ref, yt_ref, e0_ref, m0_ref, e1_ref, m1_ref, gs_ref, ds_ref, out_ref, tmp_ref
):
    o1 = pl.multiple_of(off_ref[0], 128)

    def store(c, n, v):
        tmp_ref[c : c + n, :] = v

    def block(d, carry):
        gs = gs_ref[d]
        dscores(y_ref[d, :, 96:144], gs, ds_ref[d], lambda c, n: m0_ref[d, c : c + n, :], store)
        dscore = tmp_ref[...]
        out_ref[d, 0:48, :] = mm(yt_ref[d, 48:96, :], dscore)
        out_ref[d, 48:96, :] = mm(yt_ref[d, 0:48, :], dscore, NT)
        out_ref[d, 96:144, :] = mm(gs, e0_ref[d], NT)
        return carry

    lax.fori_loop(0, 4, block, 0)
    values = jnp.concatenate([y_ref[d, pl.ds(o1, 128), 96:144] for d in range(4)], axis=0)
    queries = jnp.concatenate([yt_ref[d, 0:48, pl.ds(o1, 128)] for d in range(4)], axis=1)
    keys = jnp.concatenate([yt_ref[d, 48:96, pl.ds(o1, 128)] for d in range(4)], axis=1)
    gs = jnp.concatenate([gs_ref[d, :, pl.ds(o1, 128)] for d in range(4)], axis=1)
    ds = jnp.concatenate([ds_ref[d, :, pl.ds(o1, 128)] for d in range(4)], axis=1)
    dscores(values, gs, ds, lambda c, n: m1_ref[c : c + n, :], store)
    dscore = tmp_ref[...]
    dq = mm(keys, dscore)
    dk = mm(queries, dscore, NT)
    dv = mm(gs, e1_ref[...], NT)
    dall = jnp.concatenate([dq, dk, dv], axis=0)
    for d in range(4):
        out_ref[d, :, pl.ds(o1, 128)] += dall[:, 128 * d : 128 * d + 128]


def return_kernel(
    off_ref,
    dall_ref,
    own_ref,
    dq_ref,
    r1_ref,
    r2_ref,
    r3_ref,
    g0_ref,
    g1_ref,
    g2_ref,
    g3_ref,
    tab_ref,
    out_ref,
    sum_ref,
):
    o2 = off_ref[1]
    base = pl.multiple_of((o2 >> 7) << 7, 128)
    part = (o2 >> 5) & 3
    dkv = (
        own_ref[...]
        + r1_ref[...].astype(F32)
        + r2_ref[...].astype(F32)
        + r3_ref[...].astype(F32)
    )
    extra = jnp.concatenate([dq_ref[...], dkv], axis=0)
    lane = iota((1, 128), 1) >> 5
    rows = tab_ref.shape[0]
    for d in range(4):
        grad_ref = (g0_ref, g1_ref, g2_ref, g3_ref)[d]
        sum_ref[...] = dall_ref[d]
        sum_ref[:, pl.ds(base, 128)] += jnp.where(
            lane == part, turned(extra, 32 * (part - d)), 0.0
        )
        both = jnp.concatenate([sum_ref[...].astype(BF), grad_ref[...]], axis=0)
        onehot = jnp.where(tab_ref[:, d : d + 1] == iota((rows, BLK), 1), 1.0, 0.0).astype(BF)
        out_ref[:, 192 * d : 192 * d + 192] = mm(onehot, both, NT).astype(BF)


def out_kernel(j_ref, s0_ref, s1_ref, s2_ref, s3_ref, out_ref, tmp_ref):
    j = j_ref[0]
    for d in range(4):
        at = pl.multiple_of((j ^ d) * HD, 16)
        tmp_ref[pl.ds(at, HD), :] = (s0_ref, s1_ref, s2_ref, s3_ref)[d][...]
    out_ref[...] = mm(order_matrix(), tmp_ref[...], NT).astype(BF)


def unpack_kernel(ret_ref, prow_ref, pcol_ref, dqkv_ref, grad_ref, wide_ref):
    brow = prow_ref[...] >> 9
    bcol = pcol_ref[...] >> 9
    n = prow_ref.shape[1]
    before = iota((n, n), 1) < iota((n, n), 0)
    rank = jnp.sum(jnp.where((bcol == brow) & before, 1, 0), axis=1, keepdims=True)
    code = bcol * SLOTS + rank
    seat = iota((n, 256), 1)
    want = (((seat >> 3) & 7) * 4 + (seat >> 6)) * SLOTS + (seat & 7)
    picker = jnp.where(code == want, 1.0, 0.0).astype(BF)
    wide_ref[...] = ret_ref[...].astype(F32).reshape(8, 16, SLOTS, 768)
    width = HEADS * HD
    for h in range(HEADS):
        t, j = h // 4, h % 4
        rows = wide_ref[:, j * 4 + t, :, :].reshape(64, 768)
        stacked = jnp.concatenate(
            [rows[:, (j ^ b) * 192 : (j ^ b) * 192 + 192] for b in range(4)], axis=0
        ).astype(BF)
        got = mm(picker, stacked).astype(BF)
        for part in range(3):
            dqkv_ref[:, part * width + h * HD : part * width + h * HD + HD] = got[
                :, HD * part : HD * part + HD
            ]
        grad_ref[:, h * HD : h * HD + HD] = got[:, 144:192]


def swap(value, distance, count):
    return lax.ppermute(value, "seq", [(i, i ^ distance) for i in range(count)])


def on_device(
    tile_features,
    gate_weight,
    up_weight,
    down_weight,
    input_projection_weight,
    query_key_value_weight,
    positions,
    dilation_shift,
    slide_output_gradient,
):
    seq_count = lax.axis_size("seq")
    tile_count = lax.axis_size("tile")
    s = lax.axis_index("seq")
    t = lax.axis_index("tile")
    j = s % 4
    g = s // 4
    device_count = seq_count * tile_count
    my_device = s * tile_count + t
    tile_rows = tile_features.shape[0]
    head = 4 * t + j
    o1 = dilation_shift[0, head]
    o2 = dilation_shift[1, head]
    offs = jnp.stack([o1 * 128, (o2 & 3) * 128 + (o2 >> 2) * 32]).astype(I32)

    (ordered,) = call(order_kernel, [((192, BLK), BF)])(slide_output_gradient)
    pieces = ordered.reshape(4, HD, BLK)
    grads = [lax.dynamic_index_in_dim(pieces, j ^ d, 0, keepdims=False) for d in range(4)]
    grads = [grads[0]] + [swap(grads[d], d, seq_count) for d in range(1, 4)]

    feats32 = tile_features.astype(F32)
    feat_norm, feat_inv = normalize(feats32)
    feat_bf = feat_norm.astype(BF)
    gate_proj = jnp.dot(feat_bf, gate_weight, preferred_element_type=F32)
    up_proj = jnp.dot(feat_bf, up_weight, preferred_element_type=F32)
    gate_sigmoid = jax.nn.sigmoid(gate_proj)
    hidden = (gate_proj * gate_sigmoid * up_proj).astype(BF)
    embedding = (feats32 + jnp.dot(hidden, down_weight, preferred_element_type=F32)).astype(BF)
    tile_proj = jnp.dot(embedding, input_projection_weight, preferred_element_type=F32).astype(BF)
    slide32 = lax.optimization_barrier(tile_proj).astype(F32)
    slide_norm, slide_inv = normalize(slide32)
    qkv = jnp.dot(
        slide_norm.astype(BF), query_key_value_weight, preferred_element_type=F32
    ).astype(BF)

    all_pos = positions.reshape(device_count, tile_rows)
    own_pos = lax.dynamic_slice_in_dim(all_pos, my_device, 1, 0)
    own_col = own_pos.reshape(tile_rows, 1)
    (outgoing,) = call(
        pack_kernel,
        [((device_count * SLOTS, 768), BF)],
        [pltpu.VMEM((tile_rows, 192 * HEADS), BF), pltpu.VMEM((8, 16, SLOTS, 768), F32)],
    )(qkv, tile_proj, own_pos, own_col)
    arrived = lax.all_to_all(
        outgoing.reshape(device_count, SLOTS, 768),
        ("seq", "tile"),
        split_axis=0,
        concat_axis=0,
        tiled=True,
    ).reshape(device_count * SLOTS, 768)

    block_of = all_pos >> 9
    same = block_of[:, :, None] == block_of[:, None, :]
    before = jnp.arange(tile_rows)[:, None] < jnp.arange(tile_rows)[None, :]
    rank = jnp.sum((same & before[None]).astype(I32), axis=1)
    code = block_of * SLOTS + rank
    place = class_order(all_pos & 511) + 1
    blocks = 4 * g + (j ^ jnp.arange(4, dtype=I32))
    want = (blocks[:, None] * SLOTS + jnp.arange(SLOTS, dtype=I32)[None, :])[:, None, :, None]
    table = (
        jnp.sum(jnp.where(code[None, :, None, :] == want, place[None, :, None, :], 0), axis=3) - 1
    )
    table = table.reshape(4, device_count * SLOTS)
    table_col = table.T

    y, yt, y2 = call(
        place_kernel,
        [((4, BLK, 192), BF), ((4, 192, BLK), BF), ((128, 192), BF)],
        n_smem=1,
    )(offs, arrived, table)
    y2_in = [swap(y2, 4 * e, seq_count) for e in range(1, 4)]
    e0, m0, e1, m1, u, l = call(
        forward_kernel,
        [
            ((4, BLK, BLK), BF),
            ((4, BLK, BLK), BF),
            ((BLK, BLK), BF),
            ((BLK, BLK), BF),
            ((4, HD, BLK), F32),
            ((4, 1, BLK), F32),
        ],
        n_smem=1,
    )(offs, y, yt)
    so, gs, ds, own, send, dq2 = call(
        wide_kernel,
        [
            ((4, HD, BLK), BF),
            ((4, HD, BLK), BF),
            ((4, 1, BLK), F32),
            ((96, 128), F32),
            ((3, 96, 128), BF),
            ((HD, 128), F32),
        ],
        [
            pltpu.VMEM((BLK, 128), BF),
            pltpu.VMEM((BLK, 128), BF),
            pltpu.VMEM((HD, BLK), F32),
            pltpu.VMEM((1, BLK), F32),
        ],
        n_smem=1,
    )(offs, yt, y2, *y2_in, u, l, *grads)
    back = [swap(send[e - 1], 4 * e, seq_count) for e in range(1, 4)]
    (dall,) = call(
        backward_kernel,
        [((4, 144, BLK), F32)],
        [pltpu.VMEM((BLK, BLK), BF)],
        n_smem=1,
    )(offs, y, yt, e0, m0, e1, m1, gs, ds)
    (returning,) = call(
        return_kernel,
        [((device_count * SLOTS, 768), BF)],
        [pltpu.VMEM((144, BLK), F32)],
        n_smem=1,
    )(
        offs, dall, own, dq2, *back, *grads, table_col
    )
    returned = lax.all_to_all(
        returning.reshape(device_count, SLOTS, 768),
        ("seq", "tile"),
        split_axis=0,
        concat_axis=0,
        tiled=True,
    ).reshape(device_count * SLOTS, 768)

    parts = [so[0]] + [swap(so[d], d, seq_count) for d in range(1, 4)]
    (slide_out,) = call(
        out_kernel, [((BLK, 192), BF)], [pltpu.VMEM((192, BLK), BF)], n_smem=1
    )(j.reshape(1).astype(I32), *parts)

    dqkv, grad_rows = call(
        unpack_kernel,
        [((tile_rows, 3 * HEADS * HD), BF), ((tile_rows, HEADS * HD), BF)],
        [pltpu.VMEM((8, 16, SLOTS, 768), F32)],
    )(returned, own_pos, own_col)
    grad_norm = jnp.dot(dqkv, query_key_value_weight.T, preferred_element_type=F32)
    grad_slide = grad_rows.astype(F32) + norm_back(slide_norm, slide_inv, grad_norm)
    grad_embed = jnp.dot(
        grad_slide.astype(BF), input_projection_weight.T, preferred_element_type=F32
    ).astype(BF)
    grad_hidden = jnp.dot(grad_embed, down_weight.T, preferred_element_type=F32)
    grad_gate = (
        grad_hidden * up_proj * gate_sigmoid * (1.0 + gate_proj * (1.0 - gate_sigmoid))
    ).astype(BF)
    grad_up = (grad_hidden * gate_proj * gate_sigmoid).astype(BF)
    grad_feat = jnp.dot(grad_gate, gate_weight.T, preferred_element_type=F32) + jnp.dot(
        grad_up, up_weight.T, preferred_element_type=F32
    )
    embed32 = lax.optimization_barrier(grad_embed).astype(F32)
    tile_grad = (embed32 + norm_back(feat_norm, feat_inv, grad_feat)).astype(BF)
    return (slide_out, tile_grad)


def solution(mesh):
    placed = (P(("seq", "tile"), None), P(), P(), P(), P(), P(), P(), P(), P("seq", "tile"))
    return jax.shard_map(
        on_device,
        mesh=mesh,
        in_specs=placed,
        out_specs=(P("seq", "tile"), P(("seq", "tile"), None)),
        check_vma=False,
    )
```

profile of v0, /device:TPU:1, one launch (start us, length us, event | category | flops | bytes accessed | tf_op | source)
XLA Modules:
  0.0 154.8 jit_solution(8541566672267274485)
XLA Ops:
  3.5 1.2 fusion.11
  4.8 5.1 %fusion.40 = f32[128,2048]{1,0:T(8,128)} fusion(bf16[1536,2048]{1,0:T(8,128)(2,1)} %param.11, bf16[128,1536]{1,0:T(8,128)(2,1)} %param.9, f32[128]{0:T(128)S(1)} %add_rsqrt_fusion.1, f32[128]{0:T(128)S(1)} %broadcast_multiply_fusion.5), kind=kOutput, calls=%fused_computation.81 | convolution fusion | flops 806092800 | bytes 7734272 | tf_op jit(solution)/shard_map/dot_general | solution.py:389
  9.9 2.1 %fusion.42 = f32[128,2048]{1,0:T(8,128)} fusion(bf16[1536,2048]{1,0:T(8,128)(2,1)S(1)} %copy-done.21, bf16[128,1536]{1,0:T(8,128)(2,1)S(1)} %copy-done.19, f32[128]{0:T(128)S(1)} %add_rsqrt_fusion.1, f32[128]{0:T(128)S(1)} %broadcast_multiply_fusion.5), kind=kOutput, calls=%fused_computation.82 | convolution fusion | flops 806092800 | bytes 7734272 | tf_op jit(solution)/shard_map/dot_general | solution.py:388
  12.0 6.4 %convolution_convert_fusion.2.x_ref = bf16[128,768]{1,0:T(8,128)(2,1)} fusion(bf16[1536,768]{1,0:T(8,128)(2,1)} %param.13, bf16[2048,1536]{1,0:T(8,128)(2,1)} %param.12, bf16[128,1536]{1,0:T(8,128)(2,1)} %param.9, f32[128,2048]{1,0:T(8,128)} %fusion.40, f32[128,2048]{1,0:T(8,128)} %fusion.42), kind=kOutput, calls=%fused_computation.9 | convolution fusion | flops 1109557248 | bytes 11337728 | tf_op jit(solution)/shard_map/dot_general | solution.py:393
  21.4 1.7 %convolution_convert_fusion.qkv_ref = bf16[128,2304]{1,0:T(8,128)(2,1)S(1)} fusion(bf16[768,2304]{1,0:T(8,128)(2,1)S(1)} %copy-done, bf16[128,768]{1,0:T(8,128)(2,1)} %convolution_convert_fusion.2.x_ref, f32[128]{0:T(128)S(1)} %add_rsqrt_fusion, f32[128]{0:T(128)S(1)} %broadcast_multiply_fusion.2), kind=kOutput, calls=%fused_computation.1 | convolution fusion | flops 453672960 | bytes 4326400 | tf_op jit(solution)/shard_map/dot_general | solution.py:396
  23.1 2.1 %shard_map.104 = bf16[1024,768]{1,0:T(8,128)(2,1)S(1)} custom-call(bf16[128,2304]{1,0:T(8,128)(2,1)S(1)} %convolution_convert_fusion.qkv_ref, bf16[128,768]{1,0:T(8,128)(2,1)S(1)} %copy-done.1, s32[1,128]{1,0:T(1,128)S(1)} %constant_dynamic-slice_fusion.prow_ref, s32[128,1]{1,0:T(8,128)S(1)} %copy-done.9), custom_call_target="tpu_custom_call" | custom-call | tf_op jit(solution)/shard_map/pallas_call | solution.py:58
  26.3 11.9 %all-to-all-start = ((bf16[128,8,768]{2,1,0:T(8,128)(2,1)}), bf16[128,8,768]{2,1,0:T(8,128)(2,1)}, u32[]{:S(2)}, u32[]{:S(2)}) async-start(bf16[128,8,768]{2,1,0:T(8,128)(2,1)} %bitcast.52), calls=%async_computation | async-start | bytes 3145728 | tf_op jit(solution)/shard_map/all_to_all | solution.py:408
  38.2 1.8 %copy.26.grad_ref = bf16[512,192]{1,0:T(8,128)(2,1)} copy(bf16[512,192]{0,1:T(8,128)(2,1)} %param.17) | data formatting | bytes 393216 | tf_op args[8]
  41.9 1.5 %dynamic-slice_bitcast_fusion = (bf16[48,512]{1,0:T(8,128)(2,1)}, bf16[48,512]{1,0:T(8,128)(2,1)}, bf16[48,512]{1,0:T(8,128)(2,1)}, bf16[48,512]{1,0:T(8,128)(2,1)}) fusion(bf16[4,48,512]{2,1,0:T(8,128)(2,1)} %bitcast.56, s32[]{:T(128)S(6)} %select_n.43, s32[]{:T(128)S(6)} %select_n.42, s32[]{:T(128)S(6)} %select_n.41, s32[]{:T(128)S(6)} %select_n.40), kind=kLoop, calls=%fused_computation.55 | loop fusion | bytes 393232 | tf_op jit(solution)/shard_map/jit(dynamic_index_in_dim)/squeeze | solution.py:382
  46.3 1.3 constant_dynamic-slice_fusion.1
  50.6 2.8 %convert_reduce_fusion = s32[128,128]{1,0:T(8,128)S(1)} fusion(s32[128,128]{1,0:T(8,128)S(1)} %broadcast_shift-right-arithmetic_fusion, pred[128,128]{1,0:T(8,128)(4,1)S(1)} %iota_compare_fusion), kind=kLoop, calls=%fused_computation | loop fusion | flops 8372224 | bytes 147456 | tf_op jit(solution)/shard_map/reduce_sum | solution.py:419
  54.3 9.5 %select_reduce_fusion = s32[4,128,8]{2,1,0:T(8,128)} fusion(s32[128,128]{1,0:T(8,128)S(1)} %get-tuple-element.58, s32[4,8]{1,0:T(4,128)S(1)} %iota_add_fusion, s32[128,128]{1,0:T(8,128)S(1)} %get-tuple-element.57), kind=kLoop, calls=%fused_computation.6 | loop fusion | flops 1568768 | bytes 147584 | tf_op jit(solution)/shard_map/reduce_sum | solution.py:425
  66.1 1.7 %copy.24 = s32[4,128,8]{0,2,1:T(8,128)} copy(s32[4,128,8]{1,2,0:T(8,128)} %broadcast_add_fusion) | data formatting | bytes 32768 | tf_op jit(solution)/shard_map/sub | solution.py:425
  69.7 2.8 %shard_map.105 = (bf16[4,512,192]{2,1,0:T(8,128)(2,1)S(1)}, bf16[4,192,512]{2,1,0:T(8,128)(2,1)S(1)}, bf16[128,192]{1,0:T(8,128)(2,1)S(1)}) custom-call(s32[2]{0:T(128)S(1)} %copy-done.14, bf16[1024,768]{1,0:T(8,128)(2,1)} %bitcast.6.recv_ref, s32[4,1024]{1,0:T(4,128)S(1)} %copy.25.tab_ref), custom_call_target="tpu_custom_call" | custom-call | tf_op jit(solution)/shard_map/pallas_call | solution.py:58
  72.6 2.7 %collective-permute-start = (bf16[128,192]{1,0:T(8,128)(2,1)S(1)}, bf16[128,192]{1,0:T(8,128)(2,1)S(1)}, u32[]{:S(2)}, u32[]{:S(2)}) collective-permute-start(bf16[128,192]{1,0:T(8,128)(2,1)S(1)} %get-tuple-element.20.a0_ref), channel_id=1, source_target_pairs={{0,16},{4,20},{8,24},{12,28},{16,0},{20,4},{24,8},{28,12},{32,48},... | collective-permute-start | bytes 147464 | tf_op jit(solution)/shard_map/ppermute | solution.py:352
  75.3 1.3 collective-permute-start.1
  76.8 4.3 %shard_map.106 = (bf16[4,512,512]{2,1,0:T(8,128)(2,1)S(1)}, bf16[4,512,512]{2,1,0:T(8,128)(2,1)S(1)}, bf16[512,512]{1,0:T(8,128)(2,1)S(1)}, bf16[512,512]{1,0:T(...) custom-call(s32[2]{0:T(128)S(1)} %copy-done.14, bf16[4,512,192]{2,1,0:T(8,128)(2,1)S(1)} %get-tuple-element.21.y_ref, ...), custom_call_target="tpu_custom_call" | custom-call | tf_op jit(solution)/shard_map/pallas_call | solution.py:58
  83.5 1.9 %shard_map.108 = (bf16[4,48,512]{2,1,0:T(8,128)(2,1)S(1)}, bf16[4,48,512]{2,1,0:T(8,128)(2,1)S(1)}, f32[4,1,512]{2,1,0:T(1,128)S(1)}, f32[96,128]{1,0:T(8,128)S(...) custom-call(s32[2]{0:T(128)S(1)} %copy-done.15, bf16[4,192,512]{2,1,0:T(8,128)(2,1)S(1)} %get-tuple-element.19.yt_ref, ...), custom_call_target="tpu_custom_call" | custom-call | tf_op jit(solution)/shard_map/pallas_call | solution.py:58
  86.1 1.7 %collective-permute-start.9 = (bf16[96,128]{1,0:T(8,128)(2,1)S(1)}, bf16[96,128]{1,0:T(8,128)(2,1)S(1)}, u32[]{:S(2)}, u32[]{:S(2)}) collective-permute-start(bf16[96,128]{1,0:T(8,128)(2,1)S(1)} %get-tuple-element.56), channel_id=1, source_target_pairs={{0,16},{4,20},{8,24},{12,28},{16,0},{20,4},{24,8},{28,12},{32,48},... | collective-permute-start | bytes 73736 | tf_op jit(solution)/shard_map/ppermute | solution.py:352
  87.8 1.3 collective-permute-start.10
  90.3 4.4 %shard_map.110.dall_ref = f32[4,144,512]{2,1,0:T(8,128)S(1)} custom-call(s32[2]{0:T(128)S(1)} %copy-done.15, bf16[4,512,192]{2,1,0:T(8,128)(2,1)S(1)} %get-tuple-element.21.y_ref, bf16[4,192,512]{2,1,0:T(8,128)(2,1)S(1)} %get-tuple-element.19.yt_ref, bf16[4,512,512]{2,1,0:T(8,128)(2,1)S(1)} %get-tuple-element.25.e0_ref, ...), custom_call_target="tpu_custom_call" | custom-call | tf_op jit(solution)/shard_map/pallas_call | solution.py:58
  94.8 2.5 %shard_map.111 = bf16[1024,768]{1,0:T(8,128)(2,1)S(1)} custom-call(s32[2]{0:T(128)S(1)} %copy-done.16, f32[4,144,512]{2,1,0:T(8,128)S(1)} %shard_map.110.dall_ref, f32[96,128]{1,0:T(8,128)S(1)} %get-tuple-element.31.own_ref, f32[48,128]{1,0:T(8,128)S(1)} %get-tuple-element.32.dq_ref, bf16[96,128]{1,0:T(8,128)(2,1)S(1)} %collective-permute-done.9.r1_ref, ...), custom_call_target="tpu_custom_call" | custom-call | tf_op jit(solution)/shard_map/pallas_call | solution.py:58
  98.4 10.0 %all-to-all-start.1 = ((bf16[128,8,768]{2,1,0:T(8,128)(2,1)}), bf16[128,8,768]{2,1,0:T(8,128)(2,1)}, u32[]{:S(2)}, u32[]{:S(2)}) async-start(bf16[128,8,768]{2,1,0:T(8,128)(2,1)} %bitcast.53), calls=%async_computation.1 | async-start | bytes 3145728 | tf_op jit(solution)/shard_map/all_to_all | solution.py:481
  112.3 12.4 %collective-permute-done.7.s2_ref = bf16[48,512]{1,0:T(8,128)(2,1)S(1)} collective-permute-done((bf16[48,512]{1,0:T(8,128)(2,1)S(1)}, bf16[48,512]{1,0:T(8,128)(2,1)S(1)}, u32[]{:S(2)}, u32[]{:S(2)}) %collective-permute-start.7) | collective-permute-done | bytes 49184 | tf_op jit(solution)/shard_map/ppermute | solution.py:352
  124.6 4.8 %collective-permute-done.8.s3_ref = bf16[48,512]{1,0:T(8,128)(2,1)S(1)} collective-permute-done((bf16[48,512]{1,0:T(8,128)(2,1)S(1)}, bf16[48,512]{1,0:T(8,128)(2,1)S(1)}, u32[]{:S(2)}, u32[]{:S(2)}) %collective-permute-start.8) | collective-permute-done | bytes 49184 | tf_op jit(solution)/shard_map/ppermute | solution.py:352
  130.5 1.8 %copy.28 = bf16[512,192]{0,1:T(8,128)(2,1)} copy(bf16[512,192]{1,0:T(8,128)(2,1)} %copy-done.7) | data formatting | bytes 393216
  132.2 1.3 all-to-all-done.1
  134.4 5.9 %shard_map.112 = (bf16[128,2304]{1,0:T(8,128)(2,1)S(1)}, bf16[128,768]{1,0:T(8,128)(2,1)S(1)}) custom-call(bf16[1024,768]{1,0:T(8,128)(2,1)} %bitcast.22.ret_ref, s32[1,128]{1,0:T(1,128)S(1)} %copy-done.18, s32[128,1]{1,0:T(8,128)S(1)} %copy-done.10), custom_call_target="tpu_custom_call" | custom-call | tf_op jit(solution)/shard_map/pallas_call | solution.py:58
  140.3 2.5 %fusion.45 = (f32[128]{0:T(128)S(1)}, f32[128]{0:T(128)S(1)}, f32[128,768]{1,0:T(8,128)S(1)}) fusion(f32[128]{0:T(128)S(1)} %copy-done.32, f32[128]{0:T(128)S(1)} %copy-done.28, bf16[128,768]{1,0:T(8,128)(2,1)} %convolution_convert_fusion.2.x_ref, bf16[128,2304]{1,0:T(8,128)(2,1)S(1)} %get-tuple-element.35, bf16[768,2304]{1,0:T(8,128)(2,1)S(1)} %copy-done), kind=kOutput, calls=%fused_computation.84 | convolution fusion | flops 453574400 | bytes 4720640 | tf_op jit(solution)/shard_map/dot_general | solution.py:499
  143.8 5.1 %fusion.46 = f32[128,2048]{1,0:T(8,128)S(1)} fusion(bf16[128,1536]{1,0:T(8,128)(2,1)S(1)} %convolution_convert_fusion.1, bf16[2048,1536]{1,0:T(8,128)(2,1)} %param.12), kind=kOutput, calls=%fused_computation.85 | convolution fusion | flops 805306368 | bytes 7733248 | tf_op jit(solution)/shard_map/dot_general | solution.py:504
  149.0 2.3 %fusion.12 = f32[128,1536]{1,0:T(8,128)S(1)} fusion(bf16[1536,2048]{1,0:T(8,128)(2,1)S(1)} %bitcast.58, f32[128,2048]{1,0:T(8,128)S(1)} %copy-done.23, f32[128,2048]{1,0:T(8,128)S(1)} %fusion.46, f32[128,2048]{1,0:T(8,128)S(1)} %copy-done.24), kind=kOutput, calls=%fused_computation.25 | convolution fusion | flops 807927808 | bytes 10223616 | tf_op jit(solution)/shard_map/dot_general | solution.py:509
  151.3 2.3 %fusion.44 = (f32[128]{0:T(128)S(1)}, f32[128]{0:T(128)S(1)}, f32[128,1536]{1,0:T(8,128)S(1)}) fusion(f32[128]{0:T(128)S(1)} %copy-done.30, f32[128]{0:T(128)S(1)} %copy-done.26, bf16[128,1536]{1,0:T(8,128)(2,1)S(1)} %copy-done.20, f32[128,1536]{1,0:T(8,128)S(1)} %fusion.12, bf16[1536,2048]{1,0:T(8,128)(2,1)S(1)} %bitcast.60, f32[128,2048]{1,0:T(8,128)S(1)} %fusion.46, ...), kind=kOutput, calls=%fused_computation.83 | convolution fusion | flops 808255232 | bytes 10356736 | tf_op jit(solution)/shard_map/dot_general | solution.py:509
  (123 shorter events, 31.4 us)
Async XLA Ops:
  0.6 20.7 %copy-start = (bf16[768,2304]{1,0:T(8,128)(2,1)S(1)}, bf16[768,2304]{1,0:T(8,128)(2,1)}, u32[]{:S(2)}) copy-start(bf16[768,2304]{1,0:T(8,128)(2,1)} %param.14) | copy-start | bytes 10616836
  1.5 21.6 %copy-start.17 = (s32[1,128]{1,0:T(1,128)}, s32[1,128]{1,0:T(1,128)S(1)}, u32[]{:S(2)}) copy-start(s32[1,128]{1,0:T(1,128)S(1)} %constant_dynamic-slice_fusion.prow_ref) | copy-start | bytes 1540
  3.5 6.4 %copy-start.25 = (f32[128]{0:T(128)}, f32[128]{0:T(128)S(1)}, u32[]{:S(2)}) copy-start(f32[128]{0:T(128)S(1)} %broadcast_multiply_fusion.5) | copy-start | bytes 1540
  4.8 5.1 %copy-start.29 = (f32[128]{0:T(128)}, f32[128]{0:T(128)S(1)}, u32[]{:S(2)}) copy-start(f32[128]{0:T(128)S(1)} %add_rsqrt_fusion.1) | copy-start | bytes 1540
  4.8 5.1 %copy-start.19 = (bf16[128,1536]{1,0:T(8,128)(2,1)S(1)}, bf16[128,1536]{1,0:T(8,128)(2,1)}, u32[]{:S(2)}) copy-start(bf16[128,1536]{1,0:T(8,128)(2,1)} %param.9) | copy-start | bytes 1179652
  4.8 5.1 %copy-start.21 = (bf16[1536,2048]{1,0:T(8,128)(2,1)S(1)}, bf16[1536,2048]{1,0:T(8,128)(2,1)}, u32[]{:S(2)}) copy-start(bf16[1536,2048]{1,0:T(8,128)(2,1)} %param.10) | copy-start | bytes 18874372
  19.5 6.8 %copy-start.27 = (f32[128]{0:T(128)}, f32[128]{0:T(128)S(1)}, u32[]{:S(2)}) copy-start(f32[128]{0:T(128)S(1)} %broadcast_multiply_fusion.2) | copy-start | bytes 1540
  20.6 5.7 %copy-start.31 = (f32[128]{0:T(128)}, f32[128]{0:T(128)S(1)}, u32[]{:S(2)}) copy-start(f32[128]{0:T(128)S(1)} %add_rsqrt_fusion) | copy-start | bytes 1540
  26.3 42.7 %all-to-all-start = ((bf16[128,8,768]{2,1,0:T(8,128)(2,1)}), bf16[128,8,768]{2,1,0:T(8,128)(2,1)}, u32[]{:S(2)}, u32[]{:S(2)}) async-start(bf16[128,8,768]{2,1,0:T(8,128)(2,1)} %bitcast.52), calls=%async_computation | async-start | bytes 3145728 | tf_op jit(solution)/shard_map/all_to_all | solution.py:408
  43.5 33.0 %collective-permute-start.3 = (bf16[48,512]{1,0:T(8,128)(2,1)}, bf16[48,512]{1,0:T(8,128)(2,1)}, u32[]{:S(2)}, u32[]{:S(2)}) collective-permute-start(bf16[48,512]{1,0:T(8,128)(2,1)} %get-tuple-element.52), channel_id=1, source_target_pairs={{0,4},{4,0},{8,12},{12,8},{16,20},{20,16},{24,28},{28,24},{32,36},... | collective-permute-start | bytes 147464 | tf_op jit(solution)/shard_map/ppermute | solution.py:352
  44.6 36.4 %collective-permute-start.4 = (bf16[48,512]{1,0:T(8,128)(2,1)}, bf16[48,512]{1,0:T(8,128)(2,1)}, u32[]{:S(2)}, u32[]{:S(2)}) collective-permute-start(bf16[48,512]{1,0:T(8,128)(2,1)} %get-tuple-element.51), channel_id=1, source_target_pairs={{0,8},{4,12},{8,0},{12,4},{16,24},{20,28},{24,16},{28,20},{32,40},... | collective-permute-start | bytes 147464 | tf_op jit(solution)/shard_map/ppermute | solution.py:352
  45.4 35.7 %collective-permute-start.5 = (bf16[48,512]{1,0:T(8,128)(2,1)}, bf16[48,512]{1,0:T(8,128)(2,1)}, u32[]{:S(2)}, u32[]{:S(2)}) collective-permute-start(bf16[48,512]{1,0:T(8,128)(2,1)} %get-tuple-element.50), channel_id=1, source_target_pairs={{0,12},{4,8},{8,4},{12,0},{16,28},{20,24},{24,20},{28,16},{32,44},... | collective-permute-start | bytes 147464 | tf_op jit(solution)/shard_map/ppermute | solution.py:352
  72.6 8.5 %collective-permute-start = (bf16[128,192]{1,0:T(8,128)(2,1)S(1)}, bf16[128,192]{1,0:T(8,128)(2,1)S(1)}, u32[]{:S(2)}, u32[]{:S(2)}) collective-permute-start(bf16[128,192]{1,0:T(8,128)(2,1)S(1)} %get-tuple-element.20.a0_ref), channel_id=1, source_target_pairs={{0,16},{4,20},{8,24},{12,28},{16,0},{20,4},{24,8},{28,12},{32,48},... | collective-permute-start | bytes 147464 | tf_op jit(solution)/shard_map/ppermute | solution.py:352
  75.3 5.8 %collective-permute-start.1 = (bf16[128,192]{1,0:T(8,128)(2,1)S(1)}, bf16[128,192]{1,0:T(8,128)(2,1)S(1)}, u32[]{:S(2)}, u32[]{:S(2)}) collective-permute-start(bf16[128,192]{1,0:T(8,128)(2,1)S(1)} %get-tuple-element.20.a0_ref), channel_id=1, source_target_pairs={{0,32},{4,36},{8,40},{12,44},{16,48},{20,52},{24,56},{28,60},{32,0... | collective-permute-start | bytes 147464 | tf_op jit(solution)/shard_map/ppermute | solution.py:352
  76.5 5.5 %collective-permute-start.2 = (bf16[128,192]{1,0:T(8,128)(2,1)S(1)}, bf16[128,192]{1,0:T(8,128)(2,1)S(1)}, u32[]{:S(2)}, u32[]{:S(2)}) collective-permute-start(bf16[128,192]{1,0:T(8,128)(2,1)S(1)} %get-tuple-element.20.a0_ref), channel_id=1, source_target_pairs={{0,48},{4,52},{8,56},{12,60},{16,32},{20,36},{24,40},{28,44},{32,1... | collective-permute-start | bytes 147464 | tf_op jit(solution)/shard_map/ppermute | solution.py:352
  86.1 8.6 %collective-permute-start.9 = (bf16[96,128]{1,0:T(8,128)(2,1)S(1)}, bf16[96,128]{1,0:T(8,128)(2,1)S(1)}, u32[]{:S(2)}, u32[]{:S(2)}) collective-permute-start(bf16[96,128]{1,0:T(8,128)(2,1)S(1)} %get-tuple-element.56), channel_id=1, source_target_pairs={{0,16},{4,20},{8,24},{12,28},{16,0},{20,4},{24,8},{28,12},{32,48},... | collective-permute-start | bytes 73736 | tf_op jit(solution)/shard_map/ppermute | solution.py:352
  87.8 6.9 %collective-permute-start.10 = (bf16[96,128]{1,0:T(8,128)(2,1)S(1)}, bf16[96,128]{1,0:T(8,128)(2,1)S(1)}, u32[]{:S(2)}, u32[]{:S(2)}) collective-permute-start(bf16[96,128]{1,0:T(8,128)(2,1)S(1)} %get-tuple-element.55), channel_id=1, source_target_pairs={{0,32},{4,36},{8,40},{12,44},{16,48},{20,52},{24,56},{28,60},{32,0... | collective-permute-start | bytes 73736 | tf_op jit(solution)/shard_map/ppermute | solution.py:352
  89.1 5.6 %collective-permute-start.11 = (bf16[96,128]{1,0:T(8,128)(2,1)S(1)}, bf16[96,128]{1,0:T(8,128)(2,1)S(1)}, u32[]{:S(2)}, u32[]{:S(2)}) collective-permute-start(bf16[96,128]{1,0:T(8,128)(2,1)S(1)} %get-tuple-element.54), channel_id=1, source_target_pairs={{0,48},{4,52},{8,56},{12,60},{16,32},{20,36},{24,40},{28,44},{32,1... | collective-permute-start | bytes 73736 | tf_op jit(solution)/shard_map/ppermute | solution.py:352
  94.8 38.8 %copy-start.18 = (s32[1,128]{1,0:T(1,128)S(1)}, s32[1,128]{1,0:T(1,128)}, u32[]{:S(2)}) copy-start(s32[1,128]{1,0:T(1,128)} %copy-done.17) | copy-start | bytes 1540
  98.4 41.9 %copy-start.28 = (f32[128]{0:T(128)S(1)}, f32[128]{0:T(128)}, u32[]{:S(2)}) copy-start(f32[128]{0:T(128)} %copy-done.27) | copy-start | bytes 1540
  98.4 41.9 %copy-start.32 = (f32[128]{0:T(128)S(1)}, f32[128]{0:T(128)}, u32[]{:S(2)}) copy-start(f32[128]{0:T(128)} %copy-done.31) | copy-start | bytes 1540
  98.4 35.1 %all-to-all-start.1 = ((bf16[128,8,768]{2,1,0:T(8,128)(2,1)}), bf16[128,8,768]{2,1,0:T(8,128)(2,1)}, u32[]{:S(2)}, u32[]{:S(2)}) async-start(bf16[128,8,768]{2,1,0:T(8,128)(2,1)} %bitcast.53), calls=%async_computation.1 | async-start | bytes 3145728 | tf_op jit(solution)/shard_map/all_to_all | solution.py:481
  109.3 2.9 %collective-permute-start.6 = (bf16[48,512]{1,0:T(8,128)(2,1)S(1)}, bf16[48,512]{1,0:T(8,128)(2,1)S(1)}, u32[]{:S(2)}, u32[]{:S(2)}) collective-permute-start(bf16[48,512]{1,0:T(8,128)(2,1)S(1)} %get-tuple-element.48), channel_id=1, source_target_pairs={{0,4},{4,0},{8,12},{12,8},{16,20},{20,16},{24,28},{28,24},{32,36},... | collective-permute-start | bytes 147464 | tf_op jit(solution)/shard_map/ppermute | solution.py:352
  110.5 14.1 %collective-permute-start.7 = (bf16[48,512]{1,0:T(8,128)(2,1)S(1)}, bf16[48,512]{1,0:T(8,128)(2,1)S(1)}, u32[]{:S(2)}, u32[]{:S(2)}) collective-permute-start(bf16[48,512]{1,0:T(8,128)(2,1)S(1)} %get-tuple-element.47), channel_id=1, source_target_pairs={{0,8},{4,12},{8,0},{12,4},{16,24},{20,28},{24,16},{28,20},{32,40},... | collective-permute-start | bytes 147464 | tf_op jit(solution)/shard_map/ppermute | solution.py:352
  111.3 18.1 %collective-permute-start.8 = (bf16[48,512]{1,0:T(8,128)(2,1)S(1)}, bf16[48,512]{1,0:T(8,128)(2,1)S(1)}, u32[]{:S(2)}, u32[]{:S(2)}) collective-permute-start(bf16[48,512]{1,0:T(8,128)(2,1)S(1)} %get-tuple-element.46), channel_id=1, source_target_pairs={{0,12},{4,8},{8,4},{12,0},{16,28},{20,24},{24,20},{28,16},{32,44},... | collective-permute-start | bytes 147464 | tf_op jit(solution)/shard_map/ppermute | solution.py:352
  133.5 9.3 %copy-start.2 = (bf16[128,768]{1,0:T(8,128)(2,1)S(1)}, bf16[128,768]{1,0:T(8,128)(2,1)}, u32[]{:S(2)}) copy-start(bf16[128,768]{1,0:T(8,128)(2,1)} %convolution_convert_fusion.2.x_ref) | copy-start | bytes 589828
  134.4 8.4 %copy-start.22 = (bf16[1536,768]{1,0:T(8,128)(2,1)S(1)}, bf16[1536,768]{1,0:T(8,128)(2,1)}, u32[]{:S(2)}) copy-start(bf16[1536,768]{1,0:T(8,128)(2,1)} %param.13) | copy-start | bytes 7077892
  140.3 8.6 %slice-start = ((s8[6291456]{0:T(1024)(128)(4,1)}), s8[4194304]{0:T(1024)(128)(4,1)S(1)}, s32[]{:S(2)}) async-start(s8[6291456]{0:T(1024)(128)(4,1)} %bitcast.57), calls=%async_computation.2 | async-start | bytes 8388608
  142.8 6.1 %slice-start.1 = ((s8[6291456]{0:T(1024)(128)(4,1)}), s8[2097152]{0:T(1024)(128)(4,1)S(1)}, s32[]{:S(2)}) async-start(s8[6291456]{0:T(1024)(128)(4,1)} %bitcast.57), calls=%async_computation.3 | async-start | bytes 4194304
  143.8 5.1 %copy-start.23 = (f32[128,2048]{1,0:T(8,128)S(1)}, f32[128,2048]{1,0:T(8,128)}, u32[]{:S(2)}) copy-start(f32[128,2048]{1,0:T(8,128)} %fusion.42) | copy-start | bytes 3145732
  143.8 5.1 %copy-start.24 = (f32[128,2048]{1,0:T(8,128)S(1)}, f32[128,2048]{1,0:T(8,128)}, u32[]{:S(2)}) copy-start(f32[128,2048]{1,0:T(8,128)} %fusion.40) | copy-start | bytes 3145732
  143.8 7.4 %slice-start.2 = ((s8[6291456]{0:T(1024)(128)(4,1)}), s8[4194304]{0:T(1024)(128)(4,1)S(1)}, s32[]{:S(2)}) async-start(s8[6291456]{0:T(1024)(128)(4,1)} %bitcast.59), calls=%async_computation.4 | async-start | bytes 8388608
  (19 other events, 34.5 us)
where the time goes:
time: 156 us; the launch traced here: 155 us
  starting transfers between devices  36 us (23%)
  matrix products  28.3 us (18%)
  Pallas kernels  24.5 us (16%)
  local copies, waits for them, and re-layouts  22.2 us (14%)
  other arithmetic  21.1 us (14%)
  waiting for transfers between devices  19.4 us (12%)
  between operations  3.25 us (2%)
    pallas_call x9, Pallas kernels, run(): pl.pallas_call(kernel, out_shape=shapes, in_specs=specs, out_specs=out_sp...  24.5 us
    ppermute x12, waiting for transfers between devices, swap(): return lax.ppermute(value, 'seq', [(i, i ^ distance) for i in range(count)])  18.1 us
    ppermute x12, starting transfers between devices, swap(): return lax.ppermute(value, 'seq', [(i, i ^ distance) for i in range(count)])  14.1 us
    unnamed x76, local copies, waits for them, and re-layouts  12 us
    all_to_all x1, starting transfers between devices, on_device(): lax.all_to_all(outgoing.reshape(device_count, SLOTS, 768), ('seq', 'tile'...  11.9 us
    all_to_all x1, starting transfers between devices, on_device(): lax.all_to_all(returning.reshape(device_count, SLOTS, 768), ('seq', 'tile...  10 us
    reduce_sum x1, other arithmetic, on_device(): jnp.sum(jnp.where(code[None, :, None, :] == want, place[None, :, None, :]...  9.47 us
    dot_general x1, matrix products, on_device(): jnp.dot(embedding, input_projection_weight, preferred_element_type=F32)  6.43 us
  transfers between devices with their start and end apart: 14, of which 4 were waited for; matrix products, arithmetic and copies ran while one was open for 17% of the time, Pallas kernels for 8%

commit v1 on v0

--- a/solution.py
+++ b/solution.py
@@ -49,10 +49,11 @@
     return (grads - mean_grad - normed * mean_cross) * inv_std
 
 
-def call(kernel, outs, scratch=(), n_smem=0, limit=40):
+def call(kernel, outs, scratch=(), n_smem=0, n_any=0, limit=24):
     def run(*args):
         specs = [pl.BlockSpec(memory_space=pltpu.SMEM)] * n_smem
-        specs += [pl.BlockSpec(memory_space=pltpu.VMEM)] * (len(args) - n_smem)
+        specs += [pl.BlockSpec(memory_space=pltpu.VMEM)] * (len(args) - n_smem - n_any)
+        specs += [pl.BlockSpec(memory_space=pl.ANY)] * n_any
         shapes = [jax.ShapeDtypeStruct(s, d) for s, d in outs]
         out_specs = [pl.BlockSpec(memory_space=pltpu.VMEM)] * len(outs)
         return pl.pallas_call(
@@ -67,17 +68,123 @@
     return run
 
 
-def order_kernel(grad_ref, out_ref):
-    out_ref[...] = mm(grad_ref[...], order_matrix(), TN).astype(BF)
-
-
-def pack_kernel(qkv_ref, x_ref, prow_ref, pcol_ref, out_ref, heads_ref, wide_ref):
-    brow = prow_ref[...] >> 9
-    bcol = pcol_ref[...] >> 9
-    n = prow_ref.shape[1]
+def order_kernel(grad_ref, g0_ref, g1_ref, g2_ref, g3_ref, tmp_ref):
+    j = lax.axis_index("seq") & 3
+    tmp_ref[...] = mm(grad_ref[...], order_matrix(), TN).astype(BF)
+    for d, out_ref in enumerate((g0_ref, g1_ref, g2_ref, g3_ref)):
+        out_ref[...] = tmp_ref[pl.ds(pl.multiple_of((j ^ d) * HD, 16), HD), :]
+
+
+def offsets(shift_ref):
+    head = 4 * lax.axis_index("tile") + (lax.axis_index("seq") & 3)
+    o1 = shift_ref[0, head]
+    o2 = shift_ref[1, head]
+    return (o1 * 128, (o2 & 3) * 128, o2 >> 2)
+
+
+def table_kernel(pos_ref, row_ref, col_ref):
+    s = lax.axis_index("seq")
+    pos = pos_ref[...].T
+    n = pos.shape[0]
+    block = pos >> 9
+    seat = class_order(pos & (BLK - 1)) + 1
+    lower = jnp.where(iota((n, n), 1) < iota((n, n), 0), 1.0, 0.0).astype(BF)
+    high, low = [], []
+    for d in range(4):
+        owned = block == (s ^ d)
+        rank = mm(lower, jnp.where(owned, 1.0, 0.0).astype(BF)).astype(I32)
+        held = jnp.where(owned, seat, 0)
+        for k in range(SLOTS):
+            found = jnp.sum(jnp.where(rank == k, held, 0), axis=0, keepdims=True)
+            high.append(found >> 4)
+            low.append(found & 15)
+    digits = jnp.concatenate(high + low, axis=0).astype(F32).astype(BF)
+    lanes = n * SLOTS
+    spread = jnp.where(iota((n, lanes), 0) == iota((n, lanes), 1) >> 3, 1.0, 0.0).astype(BF)
+    wide = mm(digits, spread)
+    wide = 16.0 * wide[0:32] + wide[32:64]
+    own = iota((8, lanes), 0) == (iota((8, lanes), 1) & 7)
+    rows = [
+        jnp.sum(jnp.where(own, wide[8 * d : 8 * d + 8], 0.0), axis=0, keepdims=True)
+        for d in range(4)
+    ]
+    table = jnp.concatenate(rows + rows, axis=0) - 1.0
+    row_ref[...] = table.astype(I32)
+    col_ref[...] = table.T.astype(I32)
+
+
+def forward_mlp_kernel(
+    feat_ref,
+    pos_ref,
+    gate_hbm,
+    up_hbm,
+    down_hbm,
+    proj_hbm,
+    qkvw_hbm,
+    out_ref,
+    x_ref,
+    gate_ref,
+    up_ref,
+    wg_ref,
+    wu_ref,
+    wd_ref,
+    wp_ref,
+    wq_ref,
+    qkv_ref,
+    heads_ref,
+    wide_ref,
+    sems,
+):
+    ff = gate_hbm.shape[1]
+    step = 512
+    chunks = ff // step
+    waits = []
+    for c in range(chunks):
+        at = pl.ds(c * step, step)
+        trio = [
+            pltpu.make_async_copy(gate_hbm.at[:, at], wg_ref.at[:, at], sems.at[3 * c]),
+            pltpu.make_async_copy(up_hbm.at[:, at], wu_ref.at[:, at], sems.at[3 * c + 1]),
+            pltpu.make_async_copy(down_hbm.at[at, :], wd_ref.at[at, :], sems.at[3 * c + 2]),
+        ]
+        for copy in trio:
+            copy.start()
+        waits.append(trio)
+    last = [
+        pltpu.make_async_copy(proj_hbm, wp_ref, sems.at[3 * chunks]),
+        pltpu.make_async_copy(qkvw_hbm, wq_ref, sems.at[3 * chunks + 1]),
+    ]
+    for copy in last:
+        copy.start()
+
+    me = lax.axis_index("seq") * 4 + lax.axis_index("tile")
+    brow = pos_ref[pl.ds(me, 1), :] >> 9
+    n = brow.shape[1]
+    bcol = jnp.broadcast_to(brow, (n, n)).T
     before = iota((n, n), 0) < iota((n, n), 1)
     rank = jnp.sum(jnp.where((bcol == brow) & before, 1, 0), axis=0, keepdims=True)
     code = brow * SLOTS + rank
+
+    feats = feat_ref[...].astype(F32)
+    normed = normalize(feats)[0].astype(BF)
+    total = feats
+    for c in range(chunks):
+        at = slice(c * step, c * step + step)
+        waits[c][0].wait()
+        gate = mm(normed, wg_ref[:, at])
+        gate_ref[:, at] = gate
+        waits[c][1].wait()
+        up = mm(normed, wu_ref[:, at])
+        up_ref[:, at] = up
+        hidden = (gate * jax.nn.sigmoid(gate) * up).astype(BF)
+        waits[c][2].wait()
+        total = total + mm(hidden, wd_ref[at, :])
+    last[0].wait()
+    x = mm(total.astype(BF), wp_ref[...]).astype(BF)
+    x_ref[...] = x
+    slide_norm = normalize(x.astype(F32))[0].astype(BF)
+    last[1].wait()
+    qkv_ref[...] = mm(slide_norm, wq_ref[...]).astype(BF)
+
     width = HEADS * HD
     for h in range(HEADS):
         for part in range(3):
@@ -100,8 +207,69 @@
     out_ref[...] = wide_ref[...].reshape(8 * 16 * SLOTS, 768).astype(BF)
 
 
-def place_kernel(off_ref, recv_ref, tab_ref, y_ref, yt_ref, y2_ref):
-    o2 = pl.multiple_of(off_ref[1], 32)
+def backward_mlp_kernel(
+    ret_ref,
+    pos_ref,
+    feat_ref,
+    x_ref,
+    gate_ref,
+    up_ref,
+    wg_ref,
+    wu_ref,
+    wd_ref,
+    wp_ref,
+    wq_ref,
+    out_ref,
+    dqkv_ref,
+    grad_ref,
+    wide_ref,
+):
+    me = lax.axis_index("seq") * 4 + lax.axis_index("tile")
+    brow = pos_ref[pl.ds(me, 1), :] >> 9
+    n = brow.shape[1]
+    bcol = jnp.broadcast_to(brow, (n, n)).T
+    before = iota((n, n), 1) < iota((n, n), 0)
+    rank = jnp.sum(jnp.where((bcol == brow) & before, 1, 0), axis=1, keepdims=True)
+    code = bcol[:, 0:1] * SLOTS + rank
+    seat = iota((n, 256), 1)
+    want = (((seat >> 3) & 7) * 4 + (seat >> 6)) * SLOTS + (seat & 7)
+    picker = jnp.where(code == want, 1.0, 0.0).astype(BF)
+    wide_ref[...] = ret_ref[...].astype(F32).reshape(8, 16, SLOTS, 768)
+    width = HEADS * HD
+    for h in range(HEADS):
+        t, j = h // 4, h % 4
+        rows = wide_ref[:, j * 4 + t, :, :].reshape(64, 768)
+        stacked = jnp.concatenate(
+            [rows[:, (j ^ b) * 192 : (j ^ b) * 192 + 192] for b in range(4)], axis=0
+        ).astype(BF)
+        got = mm(picker, stacked)
+        for part in range(3):
+            dqkv_ref[:, part * width + h * HD : part * width + h * HD + HD] = got[
+                :, HD * part : HD * part + HD
+            ].astype(BF)
+        grad_ref[:, h * HD : h * HD + HD] = got[:, 144:192]
+    dnorm = mm(dqkv_ref[...], wq_ref[...], NT)
+    slide_norm, slide_inv = normalize(x_ref[...].astype(F32))
+    dslide = (grad_ref[...] + norm_back(slide_norm, slide_inv, dnorm)).astype(BF)
+    dembed = mm(dslide, wp_ref[...], NT).astype(BF)
+    ff = gate_ref.shape[1]
+    step = 512
+    dfeat = jnp.zeros(feat_ref.shape, F32)
+    for c in range(ff // step):
+        at = slice(c * step, c * step + step)
+        dhidden = mm(dembed, wd_ref[at, :], NT)
+        gate = gate_ref[:, at]
+        sig = jax.nn.sigmoid(gate)
+        dgate = (dhidden * up_ref[:, at] * sig * (1.0 + gate * (1.0 - sig))).astype(BF)
+        dup = (dhidden * gate * sig).astype(BF)
+        dfeat = dfeat + mm(dgate, wg_ref[:, at], NT) + mm(dup, wu_ref[:, at], NT)
+    normed, inv = normalize(feat_ref[...].astype(F32))
+    out_ref[...] = (dembed.astype(F32) + norm_back(normed, inv, dfeat)).astype(BF)
+
+
+def place_kernel(shift_ref, recv_ref, tab_ref, y_ref, yt_ref, y2_ref):
+    _, base, part = offsets(shift_ref)
+    o2 = pl.multiple_of(base + 32 * part, 32)
     for d in range(4):
         tab = tab_ref[d : d + 1, :]
         onehot = jnp.where(iota((BLK, tab.shape[1]), 0) == tab, 1.0, 0.0).astype(BF)
@@ -125,8 +293,8 @@
     return jnp.sum(total, axis=0, keepdims=True)
 
 
-def forward_kernel(off_ref, y_ref, yt_ref, e0_ref, m0_ref, e1_ref, m1_ref, u_ref, l_ref):
-    o1 = pl.multiple_of(off_ref[0], 128)
+def forward_kernel(shift_ref, y_ref, yt_ref, e0_ref, m0_ref, e1_ref, m1_ref, u_ref, l_ref):
+    o1 = pl.multiple_of(offsets(shift_ref)[0], 128)
 
     def block(d, carry):
         def e_store(c, n, v):
@@ -162,7 +330,7 @@
 
 
 def wide_kernel(
-    off_ref,
+    shift_ref,
     yt_ref,
     a0_ref,
     a1_ref,
@@ -174,7 +342,10 @@
     g1_ref,
     g2_ref,
     g3_ref,
-    so_ref,
+    so0_ref,
+    so1_ref,
+    so2_ref,
+    so3_ref,
     gs_ref,
     ds_ref,
     own_ref,
@@ -185,9 +356,8 @@
     usum_ref,
     lsum_ref,
 ):
-    o2 = off_ref[1]
-    base = pl.multiple_of((o2 >> 7) << 7, 128)
-    part = (o2 >> 5) & 3
+    _, base, part = offsets(shift_ref)
+    base = pl.multiple_of(base, 128)
     y2 = jnp.concatenate([a0_ref[...], a1_ref[...], a2_ref[...], a3_ref[...]], axis=0)
     keys, values = y2[:, 48:96], y2[:, 96:144]
     both_t = y2[:, 48:144].astype(F32).T.astype(BF)
@@ -215,7 +385,7 @@
         lsum_ref[:, pl.ds(base, 128)] += jnp.where(here, turned(l2w, shift), 0.0)[0:1]
         inv = 1.0 / lsum_ref[...]
         att = usum_ref[...] * inv
-        so_ref[d] = (yt_ref[d, 144:192, :].astype(F32) + att).astype(BF)
+        (so0_ref, so1_ref, so2_ref, so3_ref)[d][...] = (yt_ref[d, 144:192, :].astype(F32) + att).astype(BF)
         gs = (grad_ref[...].astype(F32) * inv).astype(BF)
         gs_ref[d] = gs
         ds_ref[d] = jnp.sum(gs.astype(F32) * att, axis=0, keepdims=True)
@@ -243,9 +413,9 @@
 
 
 def backward_kernel(
-    off_ref, y_ref, yt_ref, e0_ref, m0_ref, e1_ref, m1_ref, gs_ref, ds_ref, out_ref, tmp_ref
+    shift_ref, y_ref, yt_ref, e0_ref, m0_ref, e1_ref, m1_ref, gs_ref, ds_ref, out_ref, tmp_ref
 ):
-    o1 = pl.multiple_of(off_ref[0], 128)
+    o1 = pl.multiple_of(offsets(shift_ref)[0], 128)
 
     def store(c, n, v):
         tmp_ref[c : c + n, :] = v
@@ -276,7 +446,7 @@
 
 
 def return_kernel(
-    off_ref,
+    shift_ref,
     dall_ref,
     own_ref,
     dq_ref,
@@ -291,9 +461,8 @@
     out_ref,
     sum_ref,
 ):
-    o2 = off_ref[1]
-    base = pl.multiple_of((o2 >> 7) << 7, 128)
-    part = (o2 >> 5) & 3
+    _, base, part = offsets(shift_ref)
+    base = pl.multiple_of(base, 128)
     dkv = (
         own_ref[...]
         + r1_ref[...].astype(F32)
@@ -314,38 +483,12 @@
         out_ref[:, 192 * d : 192 * d + 192] = mm(onehot, both, NT).astype(BF)
 
 
-def out_kernel(j_ref, s0_ref, s1_ref, s2_ref, s3_ref, out_ref, tmp_ref):
-    j = j_ref[0]
+def out_kernel(s0_ref, s1_ref, s2_ref, s3_ref, out_ref, tmp_ref):
+    j = lax.axis_index("seq") & 3
     for d in range(4):
         at = pl.multiple_of((j ^ d) * HD, 16)
         tmp_ref[pl.ds(at, HD), :] = (s0_ref, s1_ref, s2_ref, s3_ref)[d][...]
     out_ref[...] = mm(order_matrix(), tmp_ref[...], NT).astype(BF)
-
-
-def unpack_kernel(ret_ref, prow_ref, pcol_ref, dqkv_ref, grad_ref, wide_ref):
-    brow = prow_ref[...] >> 9
-    bcol = pcol_ref[...] >> 9
-    n = prow_ref.shape[1]
-    before = iota((n, n), 1) < iota((n, n), 0)
-    rank = jnp.sum(jnp.where((bcol == brow) & before, 1, 0), axis=1, keepdims=True)
-    code = bcol * SLOTS + rank
-    seat = iota((n, 256), 1)
-    want = (((seat >> 3) & 7) * 4 + (seat >> 6)) * SLOTS + (seat & 7)
-    picker = jnp.where(code == want, 1.0, 0.0).astype(BF)
-    wide_ref[...] = ret_ref[...].astype(F32).reshape(8, 16, SLOTS, 768)
-    width = HEADS * HD
-    for h in range(HEADS):
-        t, j = h // 4, h % 4
-        rows = wide_ref[:, j * 4 + t, :, :].reshape(64, 768)
-        stacked = jnp.concatenate(
-            [rows[:, (j ^ b) * 192 : (j ^ b) * 192 + 192] for b in range(4)], axis=0
-        ).astype(BF)
-        got = mm(picker, stacked).astype(BF)
-        for part in range(3):
-            dqkv_ref[:, part * width + h * HD : part * width + h * HD + HD] = got[
-                :, HD * part : HD * part + HD
-            ]
-        grad_ref[:, h * HD : h * HD + HD] = got[:, 144:192]
 
 
 def swap(value, distance, count):
@@ -364,74 +507,56 @@
     slide_output_gradient,
 ):
     seq_count = lax.axis_size("seq")
-    tile_count = lax.axis_size("tile")
-    s = lax.axis_index("seq")
-    t = lax.axis_index("tile")
-    j = s % 4
-    g = s // 4
-    device_count = seq_count * tile_count
-    my_device = s * tile_count + t
-    tile_rows = tile_features.shape[0]
-    head = 4 * t + j
-    o1 = dilation_shift[0, head]
-    o2 = dilation_shift[1, head]
-    offs = jnp.stack([o1 * 128, (o2 & 3) * 128 + (o2 >> 2) * 32]).astype(I32)
-
-    (ordered,) = call(order_kernel, [((192, BLK), BF)])(slide_output_gradient)
-    pieces = ordered.reshape(4, HD, BLK)
-    grads = [lax.dynamic_index_in_dim(pieces, j ^ d, 0, keepdims=False) for d in range(4)]
+    device_count = seq_count * lax.axis_size("tile")
+    rows, width = tile_features.shape
+    ff = gate_weight.shape[1]
+    slide_width = input_projection_weight.shape[1]
+    all_pos = positions.reshape(device_count, rows)
+    routed = ((device_count * SLOTS, slide_width), BF)
+    weights = (gate_weight, up_weight, down_weight, input_projection_weight, query_key_value_weight)
+
+    def exchange(block):
+        return lax.all_to_all(
+            block.reshape(device_count, SLOTS, slide_width),
+            ("seq", "tile"),
+            split_axis=0,
+            concat_axis=0,
+            tiled=True,
+        ).reshape(device_count * SLOTS, slide_width)
+
+    outgoing, x, gate_proj, up_proj = call(
+        forward_mlp_kernel,
+        [routed, ((rows, slide_width), BF), ((rows, ff), F32), ((rows, ff), F32)],
+        [
+            pltpu.VMEM((width, ff), BF),
+            pltpu.VMEM((width, ff), BF),
+            pltpu.VMEM((ff, width), BF),
+            pltpu.VMEM((width, slide_width), BF),
+            pltpu.VMEM((slide_width, 3 * slide_width), BF),
+            pltpu.VMEM((rows, 3 * slide_width), BF),
+            pltpu.VMEM((rows, 4 * slide_width), BF),
+            pltpu.VMEM((8, 16, SLOTS, slide_width), F32),
+            pltpu.SemaphoreType.DMA((14,)),
+        ],
+        n_any=5,
+        limit=48,
+    )(tile_features, all_pos, *weights)
+    arrived = exchange(outgoing)
+
+    grads = call(order_kernel, [((HD, BLK), BF)] * 4, [pltpu.VMEM((192, BLK), BF)])(
+        slide_output_gradient
+    )
     grads = [grads[0]] + [swap(grads[d], d, seq_count) for d in range(1, 4)]
-
-    feats32 = tile_features.astype(F32)
-    feat_norm, feat_inv = normalize(feats32)
-    feat_bf = feat_norm.astype(BF)
-    gate_proj = jnp.dot(feat_bf, gate_weight, preferred_element_type=F32)
-    up_proj = jnp.dot(feat_bf, up_weight, preferred_element_type=F32)
-    gate_sigmoid = jax.nn.sigmoid(gate_proj)
-    hidden = (gate_proj * gate_sigmoid * up_proj).astype(BF)
-    embedding = (feats32 + jnp.dot(hidden, down_weight, preferred_element_type=F32)).astype(BF)
-    tile_proj = jnp.dot(embedding, input_projection_weight, preferred_element_type=F32).astype(BF)
-    slide32 = lax.optimization_barrier(tile_proj).astype(F32)
-    slide_norm, slide_inv = normalize(slide32)
-    qkv = jnp.dot(
-        slide_norm.astype(BF), query_key_value_weight, preferred_element_type=F32
-    ).astype(BF)
-
-    all_pos = positions.reshape(device_count, tile_rows)
-    own_pos = lax.dynamic_slice_in_dim(all_pos, my_device, 1, 0)
-    own_col = own_pos.reshape(tile_rows, 1)
-    (outgoing,) = call(
-        pack_kernel,
-        [((device_count * SLOTS, 768), BF)],
-        [pltpu.VMEM((tile_rows, 192 * HEADS), BF), pltpu.VMEM((8, 16, SLOTS, 768), F32)],
-    )(qkv, tile_proj, own_pos, own_col)
-    arrived = lax.all_to_all(
-        outgoing.reshape(device_count, SLOTS, 768),
-        ("seq", "tile"),
-        split_axis=0,
-        concat_axis=0,
-        tiled=True,
-    ).reshape(device_count * SLOTS, 768)
-
-    block_of = all_pos >> 9
-    same = block_of[:, :, None] == block_of[:, None, :]
-    before = jnp.arange(tile_rows)[:, None] < jnp.arange(tile_rows)[None, :]
-    rank = jnp.sum((same & before[None]).astype(I32), axis=1)
-    code = block_of * SLOTS + rank
-    place = class_order(all_pos & 511) + 1
-    blocks = 4 * g + (j ^ jnp.arange(4, dtype=I32))
-    want = (blocks[:, None] * SLOTS + jnp.arange(SLOTS, dtype=I32)[None, :])[:, None, :, None]
-    table = (
-        jnp.sum(jnp.where(code[None, :, None, :] == want, place[None, :, None, :], 0), axis=3) - 1
-    )
-    table = table.reshape(4, device_count * SLOTS)
-    table_col = table.T
+    table, table_col = call(
+        table_kernel,
+        [((8, device_count * SLOTS), I32), ((device_count * SLOTS, 8), I32)],
+    )(all_pos)
 
     y, yt, y2 = call(
         place_kernel,
         [((4, BLK, 192), BF), ((4, 192, BLK), BF), ((128, 192), BF)],
         n_smem=1,
-    )(offs, arrived, table)
+    )(dilation_shift, arrived, table)
     y2_in = [swap(y2, 4 * e, seq_count) for e in range(1, 4)]
     e0, m0, e1, m1, u, l = call(
         forward_kernel,
@@ -444,11 +569,11 @@
             ((4, 1, BLK), F32),
         ],
         n_smem=1,
-    )(offs, y, yt)
-    so, gs, ds, own, send, dq2 = call(
+    )(dilation_shift, y, yt)
+    *parts, gs, ds, own, send, dq2 = call(
         wide_kernel,
-        [
-            ((4, HD, BLK), BF),
+        [((HD, BLK), BF)] * 4
+        + [
             ((4, HD, BLK), BF),
             ((4, 1, BLK), F32),
             ((96, 128), F32),
@@ -462,55 +587,34 @@
             pltpu.VMEM((1, BLK), F32),
         ],
         n_smem=1,
-    )(offs, yt, y2, *y2_in, u, l, *grads)
+    )(dilation_shift, yt, y2, *y2_in, u, l, *grads)
     back = [swap(send[e - 1], 4 * e, seq_count) for e in range(1, 4)]
+    parts = [parts[0]] + [swap(parts[d], d, seq_count) for d in range(1, 4)]
     (dall,) = call(
         backward_kernel,
         [((4, 144, BLK), F32)],
         [pltpu.VMEM((BLK, BLK), BF)],
         n_smem=1,
-    )(offs, y, yt, e0, m0, e1, m1, gs, ds)
+    )(dilation_shift, y, yt, e0, m0, e1, m1, gs, ds)
+    dall, parts = lax.optimization_barrier((dall, parts))
     (returning,) = call(
         return_kernel,
-        [((device_count * SLOTS, 768), BF)],
+        [routed],
         [pltpu.VMEM((144, BLK), F32)],
         n_smem=1,
-    )(
-        offs, dall, own, dq2, *back, *grads, table_col
-    )
-    returned = lax.all_to_all(
-        returning.reshape(device_count, SLOTS, 768),
-        ("seq", "tile"),
-        split_axis=0,
-        concat_axis=0,
-        tiled=True,
-    ).reshape(device_count * SLOTS, 768)
-
-    parts = [so[0]] + [swap(so[d], d, seq_count) for d in range(1, 4)]
-    (slide_out,) = call(
-        out_kernel, [((BLK, 192), BF)], [pltpu.VMEM((192, BLK), BF)], n_smem=1
-    )(j.reshape(1).astype(I32), *parts)
-
-    dqkv, grad_rows = call(
-        unpack_kernel,
-        [((tile_rows, 3 * HEADS * HD), BF), ((tile_rows, HEADS * HD), BF)],
-        [pltpu.VMEM((8, 16, SLOTS, 768), F32)],
-    )(returned, own_pos, own_col)
-    grad_norm = jnp.dot(dqkv, query_key_value_weight.T, preferred_element_type=F32)
-    grad_slide = grad_rows.astype(F32) + norm_back(slide_norm, slide_inv, grad_norm)
-    grad_embed = jnp.dot(
-        grad_slide.astype(BF), input_projection_weight.T, preferred_element_type=F32
-    ).astype(BF)
-    grad_hidden = jnp.dot(grad_embed, down_weight.T, preferred_element_type=F32)
-    grad_gate = (
-        grad_hidden * up_proj * gate_sigmoid * (1.0 + gate_proj * (1.0 - gate_sigmoid))
-    ).astype(BF)
-    grad_up = (grad_hidden * gate_proj * gate_sigmoid).astype(BF)
-    grad_feat = jnp.dot(grad_gate, gate_weight.T, preferred_element_type=F32) + jnp.dot(
-        grad_up, up_weight.T, preferred_element_type=F32
-    )
-    embed32 = lax.optimization_barrier(grad_embed).astype(F32)
-    tile_grad = (embed32 + norm_back(feat_norm, feat_inv, grad_feat)).astype(BF)
+    )(dilation_shift, dall, own, dq2, *back, *grads, table_col)
+    returned = exchange(returning)
+    (slide_out,) = call(out_kernel, [((BLK, 192), BF)], [pltpu.VMEM((192, BLK), BF)])(*parts)
+    (tile_grad,) = call(
+        backward_mlp_kernel,
+        [((rows, width), BF)],
+        [
+            pltpu.VMEM((rows, 3 * slide_width), BF),
+            pltpu.VMEM((rows, slide_width), F32),
+            pltpu.VMEM((8, 16, SLOTS, slide_width), F32),
+        ],
+        limit=40,
+    )(returned, all_pos, tile_features, x, gate_proj, up_proj, *weights)
     return (slide_out, tile_grad)
 
 

time: 156 us -> 139 us (0.89)
  matrix products: 28.3 us -> 0 us
  Pallas kernels: 24.5 us -> 45.9 us
  other arithmetic: 21.1 us -> 0 us
  waiting for transfers between devices: 19.4 us -> 40.3 us
  starting transfers between devices: 36 us -> 31.5 us
  local copies, waits for them, and re-layouts: 22.2 us -> 19.5 us
  between operations: 3.25 us -> 0.88 us
    all_to_all x2, waiting for transfers between devices: 1.27 us -> 40.3 us  [exchange(): lax.all_to_all(block.reshape(device_count, SLOTS, slide_width), ('seq', '...]
    dot_general x9 -> x0, matrix products: 28.3 us -> none  [the longest x1 6.43 us: on_device(): jnp.dot(embedding, input_projection_weight, preferred_element_type=F32)]
    pallas_call x9 -> x10, Pallas kernels: 24.5 us -> 45.9 us  [run(): pl.pallas_call(kernel, out_shape=shapes, in_specs=specs, out_specs=out_sp...]
    ppermute x12, waiting for transfers between devices: 18.1 us -> 0.03 us  [swap(): return lax.ppermute(value, 'seq', [(i, i ^ distance) for i in range(count)])]
    reduce_sum x6 -> x0, other arithmetic: 16.8 us -> none  [the longest x1 9.47 us: on_device(): jnp.sum(jnp.where(code[None, :, None, :] == want, place[None, :, None, :]...]
    unnamed x76 -> x52, local copies, waits for them, and re-layouts: 12 us -> 19.5 us
    all_to_all x2, starting transfers between devices: 21.9 us -> 17.4 us  [exchange(): lax.all_to_all(block.reshape(device_count, SLOTS, slide_width), ('seq', '...]
    sub x2 -> x0, local copies, waits for them, and re-layouts: 2.96 us -> none  [on_device(): jnp.sum(jnp.where(code[None, :, None, :] == want, place[None, :, None, :]...]
  transfers between devices with their start and end apart: 14 -> 14, of which waited for: 4 -> 2; matrix products, arithmetic and copies ran while one was open for 17% -> 1% of each run, Pallas kernels for 8% -> 9%
where the time goes in v1:
time: 139 us; the launch traced here: 138 us
  Pallas kernels  45.9 us (33%)
  waiting for transfers between devices  40.3 us (29%)
  starting transfers between devices  31.5 us (23%)
  local copies, waits for them, and re-layouts  19.5 us (14%)
    pallas_call x10, Pallas kernels, run(): pl.pallas_call(kernel, out_shape=shapes, in_specs=specs, out_specs=out_sp...  45.9 us
    all_to_all x2, waiting for transfers between devices, exchange(): lax.all_to_all(block.reshape(device_count, SLOTS, slide_width), ('seq', '...  40.3 us
    unnamed x52, local copies, waits for them, and re-layouts  19.5 us
    all_to_all x2, starting transfers between devices, exchange(): lax.all_to_all(block.reshape(device_count, SLOTS, slide_width), ('seq', '...  17.4 us
    ppermute x12, starting transfers between devices, swap(): return lax.ppermute(value, 'seq', [(i, i ^ distance) for i in range(count)])  14.1 us
  transfers between devices with their start and end apart: 14, of which 2 were waited for; matrix products, arithmetic and copies ran while one was open for 1% of the time, Pallas kernels for 9%

profile of v1, /device:TPU:1, one launch (start us, length us, event | category | flops | bytes accessed | tf_op | source)
XLA Modules:
  0.0 138.1 jit_solution(7411049917293088648)
XLA Ops:
  0.6 1.0 copy-done.3
  2.5 11.8 %shard_map.104 = (bf16[1024,768]{1,0:T(8,128)(2,1)}, bf16[128,768]{1,0:T(8,128)(2,1)S(1)}, f32[128,2048]{1,0:T(8,128)S(1)}, f32[128,2048]{1,0:T(8,128)S(1)}) custom-call(bf16[128,1536]{1,0:T(8,128)(2,1)S(1)} %copy-done.3, s32[128,128]{1,0:T(8,128)S(1)} %bitcast.13, bf16[1536,2048]{1,0:T(8,128)(2,1)} %wg_ref.1, bf16[1536,2048]{1,0:T(8,128)(2,1)} %wu_ref.1, ...), custom_call_target="tpu_custom_call" | custom-call | tf_op jit(solution)/shard_map/pallas_call | solution.py:59
  14.3 1.0 copy-done.5
  15.3 1.0 copy-done.7
  16.9 11.5 %all-to-all-start = ((bf16[128,8,768]{2,1,0:T(8,128)(2,1)}), bf16[128,8,768]{2,1,0:T(8,128)(2,1)S(1)}, u32[]{:S(2)}, u32[]{:S(2)}) async-start(bf16[128,8,768]{2,1,0:T(8,128)(2,1)} %bitcast.1), calls=%async_computation | async-start | bytes 3145728 | tf_op jit(solution)/shard_map/all_to_all | solution.py:519
  28.9 1.1 collective-permute-start.3
  30.9 0.9 collective-permute-start.5
  31.8 0.9 shard_map.105
  32.7 21.1 %all-to-all-done = bf16[128,8,768]{2,1,0:T(8,128)(2,1)S(1)} async-done(((bf16[128,8,768]{2,1,0:T(8,128)(2,1)}), bf16[128,8,768]{2,1,0:T(8,128)(2,1)S(1)}, u32[]{:S(2)}, u32[]{:S(2)}) %all-to-all-start) | async-done | bytes 1572896 | tf_op jit(solution)/shard_map/all_to_all | solution.py:519
  53.8 2.0 %shard_map.106 = (bf16[4,512,192]{2,1,0:T(8,128)(2,1)S(1)}, bf16[4,192,512]{2,1,0:T(8,128)(2,1)S(1)}, bf16[128,192]{1,0:T(8,128)(2,1)S(1)}) custom-call(s32[2,16]{1,0:T(2,128)S(1)} %copy-done.23, bf16[1024,768]{1,0:T(8,128)(2,1)S(1)} %bitcast.11, s32[8,1024]{1,0:T(8,128)S(1)} %get-tuple-element.36.tab_ref), custom_call_target="tpu_custom_call" | custom-call | tf_op jit(solution)/shard_map/pallas_call | solution.py:59
  55.9 1.0 collective-permute-start.1
  56.9 3.2 %collective-permute-start = (bf16[128,192]{1,0:T(8,128)(2,1)S(1)}, bf16[128,192]{1,0:T(8,128)(2,1)S(1)}, u32[]{:S(2)}, u32[]{:S(2)}) collective-permute-start(bf16[128,192]{1,0:T(8,128)(2,1)S(1)} %get-tuple-element.43.a0_ref), channel_id=1, source_target_pairs={{0,16},{4,20},{8,24},{12,28},{16,0},{20,4},{24,8},{28,12},{32,48},... | collective-permute-start | bytes 147464 | tf_op jit(solution)/shard_map/ppermute | solution.py:495
  60.0 4.3 %shard_map.107 = (bf16[4,512,512]{2,1,0:T(8,128)(2,1)S(1)}, bf16[4,512,512]{2,1,0:T(8,128)(2,1)S(1)}, bf16[512,512]{1,0:T(8,128)(2,1)S(1)}, bf16[512,512]{1,0:T(...) custom-call(s32[2,16]{1,0:T(2,128)S(1)} %copy-done.23, ...), custom_call_target="tpu_custom_call" | custom-call | tf_op jit(solution)/shard_map/pallas_call | solution.py:59
  64.4 1.7 %shard_map.109 = (bf16[48,512]{1,0:T(8,128)(2,1)S(1)}, bf16[48,512]{1,0:T(8,128)(2,1)S(1)}, bf16[48,512]{1,0:T(8,128)(2,1)S(1)}, bf16[48,512]{1,0:T(8,128)(2,1)S...) custom-call(s32[2,16]{1,0:T(2,128)S(1)} %copy-done.23, ...), custom_call_target="tpu_custom_call" | custom-call | tf_op jit(solution)/shard_map/pallas_call | solution.py:59
  66.0 1.1 collective-permute-start.6
  67.8 1.2 collective-permute-start.8
  68.9 1.2 collective-permute-start.11
  70.1 1.1 collective-permute-start.10
  71.3 1.8 %collective-permute-start.9 = (bf16[96,128]{1,0:T(8,128)(2,1)S(1)}, bf16[96,128]{1,0:T(8,128)(2,1)S(1)}, u32[]{:S(2)}, u32[]{:S(2)}) collective-permute-start(bf16[96,128]{1,0:T(8,128)(2,1)S(1)} %get-tuple-element.72), channel_id=1, source_target_pairs={{0,16},{4,20},{8,24},{12,28},{16,0},{20,4},{24,8},{28,12},{32,48},... | collective-permute-start | bytes 73736 | tf_op jit(solution)/shard_map/ppermute | solution.py:495
  73.1 4.4 %shard_map.110.dall_ref = f32[4,144,512]{2,1,0:T(8,128)S(1)} custom-call(s32[2,16]{1,0:T(2,128)S(1)} %copy-done.23, bf16[4,512,192]{2,1,0:T(8,128)(2,1)S(1)} %get-tuple-element.37.y_ref, bf16[4,192,512]{2,1,0:T(8,128)(2,1)S(1)} %get-tuple-element.38.yt_ref, bf16[4,512,512]{2,1,0:T(8,128)(2,1)S(1)} %get-tuple-element.39.e0_ref, ...), custom_call_target="tpu_custom_call" | custom-call | tf_op jit(solution)/shard_map/pallas_call | solution.py:59
  78.8 2.3 %shard_map.112 = bf16[1024,768]{1,0:T(8,128)(2,1)S(1)} custom-call(s32[2,16]{1,0:T(2,128)S(1)} %copy-done.23, f32[4,144,512]{2,1,0:T(8,128)S(1)} %shard_map.110.dall_ref, f32[96,128]{1,0:T(8,128)S(1)} %get-tuple-element.61.own_ref, f32[48,128]{1,0:T(8,128)S(1)} %get-tuple-element.62.dq_ref, bf16[96,128]{1,0:T(8,128)(2,1)S(1)} %collective-permute-done.9.r1_ref, ...), custom_call_target="tpu_custom_call" | custom-call | tf_op jit(solution)/shard_map/pallas_call | solution.py:59
  81.1 1.2 copy-done.2
  82.2 5.9 %all-to-all-start.1 = ((bf16[128,8,768]{2,1,0:T(8,128)(2,1)}), bf16[128,8,768]{2,1,0:T(8,128)(2,1)}, u32[]{:S(2)}, u32[]{:S(2)}) async-start(bf16[128,8,768]{2,1,0:T(8,128)(2,1)} %bitcast.12), calls=%async_computation.1 | async-start | bytes 3145728 | tf_op jit(solution)/shard_map/all_to_all | solution.py:519
  92.4 1.8 %copy.12 = bf16[512,192]{0,1:T(8,128)(2,1)} copy(bf16[512,192]{1,0:T(8,128)(2,1)} %copy-done.9) | data formatting | bytes 393216
  94.1 19.2 %all-to-all-done.1 = bf16[128,8,768]{2,1,0:T(8,128)(2,1)} async-done(((bf16[128,8,768]{2,1,0:T(8,128)(2,1)}), bf16[128,8,768]{2,1,0:T(8,128)(2,1)}, u32[]{:S(2)}, u32[]{:S(2)}) %all-to-all-start.1) | async-done | bytes 1572896 | tf_op jit(solution)/shard_map/all_to_all | solution.py:519
  113.3 1.7 %copy-done.1 = bf16[1536,768]{1,0:T(8,128)(2,1)S(1)} copy-done((bf16[1536,768]{1,0:T(8,128)(2,1)S(1)}, bf16[1536,768]{1,0:T(8,128)(2,1)}, u32[]{:S(2)}) %copy-start.1) | copy-done | bytes 2359320
  115.0 1.0 copy-done.4
  116.0 1.2 copy-done.6
  117.2 1.2 copy-done.8
  118.4 0.8 copy-done.12
  119.3 0.9 copy-done.14
  120.2 17.9 %shard_map.113 = bf16[128,1536]{1,0:T(8,128)(2,1)} custom-call(bf16[1024,768]{1,0:T(8,128)(2,1)} %bitcast.7.ret_ref, s32[128,128]{1,0:T(8,128)S(1)} %bitcast.15, bf16[128,1536]{1,0:T(8,128)(2,1)S(1)} %copy-done.4, bf16[128,768]{1,0:T(8,128)(2,1)S(1)} %copy-done.14, f32[128,2048]{1,0:T(8,128)S(1)} %copy-done.6, f32[128,2048]{1,0:T(8,128)S(1)} %copy-done.8, ...), custom_call_target="tpu_custom_call" | custom-call | tf_op jit(solution)/shard_map/pallas_call | solution.py:59
  (59 shorter events, 9.0 us)
Async XLA Ops:
  0.6 1.0 copy-start.3
  1.6 0.8 copy-start.10
  14.3 1.0 copy-start.5
  15.2 1.0 copy-start.7
  16.9 11.5 %copy-start.24 = (bf16[512,192]{0,1:T(8,128)(2,1)S(1)}, bf16[512,192]{0,1:T(8,128)(2,1)}, u32[]{:S(2)}) copy-start(bf16[512,192]{0,1:T(8,128)(2,1)} %param.17) | copy-start | bytes 589828
  16.9 14.9 %copy-start.11 = (s32[16384]{0:T(1024)S(1)}, s32[16384]{0:T(1024)}, u32[]{:S(2)}) copy-start(s32[16384]{0:T(1024)} %param.15) | copy-start | bytes 196612
  16.9 36.9 %copy-start.23 = (s32[2,16]{1,0:T(2,128)S(1)}, s32[2,16]{1,0:T(2,128)}, u32[]{:S(2)}) copy-start(s32[2,16]{1,0:T(2,128)} %shift_ref.9) | copy-start | bytes 388
  16.9 36.9 %all-to-all-start = ((bf16[128,8,768]{2,1,0:T(8,128)(2,1)}), bf16[128,8,768]{2,1,0:T(8,128)(2,1)S(1)}, u32[]{:S(2)}, u32[]{:S(2)}) async-start(bf16[128,8,768]{2,1,0:T(8,128)(2,1)} %bitcast.1), calls=%async_computation | async-start | bytes 3145728 | tf_op jit(solution)/shard_map/all_to_all | solution.py:519
  28.9 27.9 %collective-permute-start.3 = (bf16[48,512]{1,0:T(8,128)(2,1)S(1)}, bf16[48,512]{1,0:T(8,128)(2,1)S(1)}, u32[]{:S(2)}, u32[]{:S(2)}) collective-permute-start(bf16[48,512]{1,0:T(8,128)(2,1)S(1)} %get-tuple-element.47), channel_id=1, source_target_pairs={{0,4},{4,0},{8,12},{12,8},{16,20},{20,16},{24,28},{28,24},{32,36},... | collective-permute-start | bytes 147464 | tf_op jit(solution)/shard_map/ppermute | solution.py:495
  30.1 34.2 %collective-permute-start.4 = (bf16[48,512]{1,0:T(8,128)(2,1)S(1)}, bf16[48,512]{1,0:T(8,128)(2,1)S(1)}, u32[]{:S(2)}, u32[]{:S(2)}) collective-permute-start(bf16[48,512]{1,0:T(8,128)(2,1)S(1)} %get-tuple-element.48), channel_id=1, source_target_pairs={{0,8},{4,12},{8,0},{12,4},{16,24},{20,28},{24,16},{28,20},{32,40},... | collective-permute-start | bytes 147464 | tf_op jit(solution)/shard_map/ppermute | solution.py:495
  30.9 33.5 %collective-permute-start.5 = (bf16[48,512]{1,0:T(8,128)(2,1)S(1)}, bf16[48,512]{1,0:T(8,128)(2,1)S(1)}, u32[]{:S(2)}, u32[]{:S(2)}) collective-permute-start(bf16[48,512]{1,0:T(8,128)(2,1)S(1)} %get-tuple-element.49), channel_id=1, source_target_pairs={{0,12},{4,8},{8,4},{12,0},{16,28},{20,24},{24,20},{28,16},{32,44},... | collective-permute-start | bytes 147464 | tf_op jit(solution)/shard_map/ppermute | solution.py:495
  55.8 8.5 %collective-permute-start.2 = (bf16[128,192]{1,0:T(8,128)(2,1)S(1)}, bf16[128,192]{1,0:T(8,128)(2,1)S(1)}, u32[]{:S(2)}, u32[]{:S(2)}) collective-permute-start(bf16[128,192]{1,0:T(8,128)(2,1)S(1)} %get-tuple-element.43.a0_ref), channel_id=1, source_target_pairs={{0,48},{4,52},{8,56},{12,60},{16,32},{20,36},{24,40},{28,44},{32,1... | collective-permute-start | bytes 147464 | tf_op jit(solution)/shard_map/ppermute | solution.py:495
  55.9 8.5 %collective-permute-start.1 = (bf16[128,192]{1,0:T(8,128)(2,1)S(1)}, bf16[128,192]{1,0:T(8,128)(2,1)S(1)}, u32[]{:S(2)}, u32[]{:S(2)}) collective-permute-start(bf16[128,192]{1,0:T(8,128)(2,1)S(1)} %get-tuple-element.43.a0_ref), channel_id=1, source_target_pairs={{0,32},{4,36},{8,40},{12,44},{16,48},{20,52},{24,56},{28,60},{32,0... | collective-permute-start | bytes 147464 | tf_op jit(solution)/shard_map/ppermute | solution.py:495
  56.9 7.5 %collective-permute-start = (bf16[128,192]{1,0:T(8,128)(2,1)S(1)}, bf16[128,192]{1,0:T(8,128)(2,1)S(1)}, u32[]{:S(2)}, u32[]{:S(2)}) collective-permute-start(bf16[128,192]{1,0:T(8,128)(2,1)S(1)} %get-tuple-element.43.a0_ref), channel_id=1, source_target_pairs={{0,16},{4,20},{8,24},{12,28},{16,0},{20,4},{24,8},{28,12},{32,48},... | collective-permute-start | bytes 147464 | tf_op jit(solution)/shard_map/ppermute | solution.py:495
  66.0 7.0 %copy-start.15 = (bf16[48,512]{1,0:T(8,128)(2,1)}, bf16[48,512]{1,0:T(8,128)(2,1)S(1)}, u32[]{:S(2)}) copy-start(bf16[48,512]{1,0:T(8,128)(2,1)S(1)} %get-tuple-element.56.s0_ref) | copy-start | bytes 147460
  66.0 5.2 %collective-permute-start.6 = (bf16[48,512]{1,0:T(8,128)(2,1)S(1)}, bf16[48,512]{1,0:T(8,128)(2,1)S(1)}, u32[]{:S(2)}, u32[]{:S(2)}) collective-permute-start(bf16[48,512]{1,0:T(8,128)(2,1)S(1)} %get-tuple-element.53), channel_id=1, source_target_pairs={{0,4},{4,0},{8,12},{12,8},{16,20},{20,16},{24,28},{28,24},{32,36},... | collective-permute-start | bytes 147464 | tf_op jit(solution)/shard_map/ppermute | solution.py:495
  67.2 10.4 %collective-permute-start.7 = (bf16[48,512]{1,0:T(8,128)(2,1)S(1)}, bf16[48,512]{1,0:T(8,128)(2,1)S(1)}, u32[]{:S(2)}, u32[]{:S(2)}) collective-permute-start(bf16[48,512]{1,0:T(8,128)(2,1)S(1)} %get-tuple-element.54), channel_id=1, source_target_pairs={{0,8},{4,12},{8,0},{12,4},{16,24},{20,28},{24,16},{28,20},{32,40},... | collective-permute-start | bytes 147464 | tf_op jit(solution)/shard_map/ppermute | solution.py:495
  67.8 10.4 %collective-permute-start.8 = (bf16[48,512]{1,0:T(8,128)(2,1)S(1)}, bf16[48,512]{1,0:T(8,128)(2,1)S(1)}, u32[]{:S(2)}, u32[]{:S(2)}) collective-permute-start(bf16[48,512]{1,0:T(8,128)(2,1)S(1)} %get-tuple-element.55), channel_id=1, source_target_pairs={{0,12},{4,8},{8,4},{12,0},{16,28},{20,24},{24,20},{28,16},{32,44},... | collective-permute-start | bytes 147464 | tf_op jit(solution)/shard_map/ppermute | solution.py:495
  68.9 9.9 %collective-permute-start.11 = (bf16[96,128]{1,0:T(8,128)(2,1)S(1)}, bf16[96,128]{1,0:T(8,128)(2,1)S(1)}, u32[]{:S(2)}, u32[]{:S(2)}) collective-permute-start(bf16[96,128]{1,0:T(8,128)(2,1)S(1)} %get-tuple-element.70), channel_id=1, source_target_pairs={{0,48},{4,52},{8,56},{12,60},{16,32},{20,36},{24,40},{28,44},{32,1... | collective-permute-start | bytes 73736 | tf_op jit(solution)/shard_map/ppermute | solution.py:495
  70.1 8.7 %collective-permute-start.10 = (bf16[96,128]{1,0:T(8,128)(2,1)S(1)}, bf16[96,128]{1,0:T(8,128)(2,1)S(1)}, u32[]{:S(2)}, u32[]{:S(2)}) collective-permute-start(bf16[96,128]{1,0:T(8,128)(2,1)S(1)} %get-tuple-element.71), channel_id=1, source_target_pairs={{0,32},{4,36},{8,40},{12,44},{16,48},{20,52},{24,56},{28,60},{32,0... | collective-permute-start | bytes 73736 | tf_op jit(solution)/shard_map/ppermute | solution.py:495
  71.3 6.3 %copy-start.17 = (bf16[48,512]{1,0:T(8,128)(2,1)}, bf16[48,512]{1,0:T(8,128)(2,1)S(1)}, u32[]{:S(2)}) copy-start(bf16[48,512]{1,0:T(8,128)(2,1)S(1)} %collective-permute-done.6.s1_ref) | copy-start | bytes 147460
  71.3 7.5 %collective-permute-start.9 = (bf16[96,128]{1,0:T(8,128)(2,1)S(1)}, bf16[96,128]{1,0:T(8,128)(2,1)S(1)}, u32[]{:S(2)}, u32[]{:S(2)}) collective-permute-start(bf16[96,128]{1,0:T(8,128)(2,1)S(1)} %get-tuple-element.72), channel_id=1, source_target_pairs={{0,16},{4,20},{8,24},{12,28},{16,0},{20,4},{24,8},{28,12},{32,48},... | collective-permute-start | bytes 73736 | tf_op jit(solution)/shard_map/ppermute | solution.py:495
  81.1 1.2 copy-start.2
  82.2 31.1 %copy-start = (bf16[768,2304]{1,0:T(8,128)(2,1)S(1)}, bf16[768,2304]{1,0:T(8,128)(2,1)}, u32[]{:S(2)}) copy-start(bf16[768,2304]{1,0:T(8,128)(2,1)} %wq_ref.1) | copy-start | bytes 10616836
  82.2 31.1 %all-to-all-start.1 = ((bf16[128,8,768]{2,1,0:T(8,128)(2,1)}), bf16[128,8,768]{2,1,0:T(8,128)(2,1)}, u32[]{:S(2)}, u32[]{:S(2)}) async-start(bf16[128,8,768]{2,1,0:T(8,128)(2,1)} %bitcast.12), calls=%async_computation.1 | async-start | bytes 3145728 | tf_op jit(solution)/shard_map/all_to_all | solution.py:519
  88.1 0.8 copy-start.16
  113.3 1.7 %copy-start.1 = (bf16[1536,768]{1,0:T(8,128)(2,1)S(1)}, bf16[1536,768]{1,0:T(8,128)(2,1)}, u32[]{:S(2)}) copy-start(bf16[1536,768]{1,0:T(8,128)(2,1)} %wp_ref.1) | copy-start | bytes 7077892
  115.0 1.0 copy-start.4
  116.0 1.2 copy-start.6
  117.2 1.2 copy-start.8
  118.4 0.8 copy-start.12
  119.3 0.9 copy-start.14
  (7 other events, 5.0 us)

commit v2 on v1

--- a/solution.py
+++ b/solution.py
@@ -49,13 +49,15 @@
     return (grads - mean_grad - normed * mean_cross) * inv_std
 
 
-def call(kernel, outs, scratch=(), n_smem=0, n_any=0, limit=24):
+def call(kernel, outs, scratch=(), n_smem=0, n_any=0, n_any_out=0, n_after=0, limit=4):
     def run(*args):
         specs = [pl.BlockSpec(memory_space=pltpu.SMEM)] * n_smem
-        specs += [pl.BlockSpec(memory_space=pltpu.VMEM)] * (len(args) - n_smem - n_any)
-        specs += [pl.BlockSpec(memory_space=pl.ANY)] * n_any
+        specs += [pl.BlockSpec(memory_space=pltpu.VMEM)] * (len(args) - n_smem - n_any - n_after)
+        specs += [pl.BlockSpec(memory_space=pltpu.HBM)] * n_any
+        specs += [pl.BlockSpec(memory_space=pl.ANY)] * n_after
         shapes = [jax.ShapeDtypeStruct(s, d) for s, d in outs]
-        out_specs = [pl.BlockSpec(memory_space=pltpu.VMEM)] * len(outs)
+        out_specs = [pl.BlockSpec(memory_space=pltpu.HBM)] * n_any_out
+        out_specs += [pl.BlockSpec(memory_space=pltpu.VMEM)] * (len(outs) - n_any_out)
         return pl.pallas_call(
             kernel,
             out_shape=shapes,
@@ -70,7 +72,7 @@
 
 def order_kernel(grad_ref, g0_ref, g1_ref, g2_ref, g3_ref, tmp_ref):
     j = lax.axis_index("seq") & 3
-    tmp_ref[...] = mm(grad_ref[...], order_matrix(), TN).astype(BF)
+    tmp_ref[...] = mm(grad_ref[...], order_matrix()).astype(BF)
     for d, out_ref in enumerate((g0_ref, g1_ref, g2_ref, g3_ref)):
         out_ref[...] = tmp_ref[pl.ds(pl.multiple_of((j ^ d) * HD, 16), HD), :]
 
@@ -121,7 +123,7 @@
     down_hbm,
     proj_hbm,
     qkvw_hbm,
-    out_ref,
+    out_hbm,
     x_ref,
     gate_ref,
     up_ref,
@@ -132,7 +134,8 @@
     wq_ref,
     qkv_ref,
     heads_ref,
-    wide_ref,
+    picker_ref,
+    tmp_ref,
     sems,
 ):
     ff = gate_hbm.shape[1]
@@ -163,6 +166,10 @@
     before = iota((n, n), 0) < iota((n, n), 1)
     rank = jnp.sum(jnp.where((bcol == brow) & before, 1, 0), axis=0, keepdims=True)
     code = brow * SLOTS + rank
+    code = jnp.concatenate([code, code + 4096], axis=1)
+    seat = iota((BLK, 2 * n), 0)
+    want = (((seat >> 4) & 7) * 4 + (seat >> 7)) * SLOTS + (seat & 7) + 4096 * ((seat >> 3) & 1)
+    picker_ref[...] = jnp.where(code == want, 1.0, 0.0).astype(BF)
 
     feats = feat_ref[...].astype(F32)
     normed = normalize(feats)[0].astype(BF)
@@ -186,25 +193,43 @@
     qkv_ref[...] = mm(slide_norm, wq_ref[...]).astype(BF)
 
     width = HEADS * HD
+    outs = []
+    for pair in range(HEADS // 2):
+        j, t = pair // 2, 2 * (pair % 2)
+        for tp in range(2):
+            h = 4 * (t + tp) + j
+            for part in range(3):
+                heads_ref[n * tp : n * tp + n, HD * part : HD * part + HD] = qkv_ref[
+                    :, part * width + h * HD : part * width + h * HD + HD
+                ]
+            heads_ref[n * tp : n * tp + n, 144:192] = x_ref[:, h * HD : h * HD + HD]
+        rows = mm(picker_ref[...], heads_ref[...]).astype(BF)
+        at = slice(16 * pair, 16 * pair + 16)
+        for block in range(4):
+            lane = (j ^ block) * 192
+            tmp_ref[:, at, lane : lane + 192] = rows[128 * block : 128 * block + 128].reshape(
+                8, 16, 192
+            )
+        copy = pltpu.make_async_copy(tmp_ref.at[:, at, :], out_hbm.at[:, at, :], sems.at[14 + pair])
+        copy.start()
+        outs.append(copy)
+    for copy in outs:
+        copy.wait()
+
+
+def between_kernel(gate_ref, up_ref, wq_ref, a1_ref, a2_ref, wqp_ref):
+    gate = gate_ref[...]
+    sig = jax.nn.sigmoid(gate)
+    a1_ref[...] = up_ref[...] * sig * (1.0 + gate * (1.0 - sig))
+    a2_ref[...] = gate * sig
+    width = HEADS * HD
+    zeros = jnp.zeros((width, HD), BF)
     for h in range(HEADS):
         for part in range(3):
-            heads_ref[:, 192 * h + HD * part : 192 * h + HD * part + HD] = qkv_ref[
+            wqp_ref[:, 192 * h + HD * part : 192 * h + HD * part + HD] = wq_ref[
                 :, part * width + h * HD : part * width + h * HD + HD
             ]
-        heads_ref[:, 192 * h + 144 : 192 * h + 192] = x_ref[:, h * HD : h * HD + HD]
-    seat = iota((64, n), 0)
-    heads = heads_ref[...]
-    for block in range(4):
-        want = ((seat >> 3) * 4 + block) * SLOTS + (seat & 7)
-        picker = jnp.where(code == want, 1.0, 0.0).astype(BF)
-        rows = mm(picker, heads)
-        for h in range(HEADS):
-            t, j = h // 4, h % 4
-            lane = (j ^ block) * 192
-            wide_ref[:, j * 4 + t, :, lane : lane + 192] = rows[:, 192 * h : 192 * h + 192].reshape(
-                8, SLOTS, 192
-            )
-    out_ref[...] = wide_ref[...].reshape(8 * 16 * SLOTS, 768).astype(BF)
+        wqp_ref[:, 192 * h + 144 : 192 * h + 192] = zeros
 
 
 def backward_mlp_kernel(
@@ -212,18 +237,38 @@
     pos_ref,
     feat_ref,
     x_ref,
-    gate_ref,
-    up_ref,
+    a1_ref,
+    a2_ref,
+    wqp_ref,
+    gate_hbm,
+    up_hbm,
+    down_hbm,
+    proj_hbm,
+    out_ref,
     wg_ref,
     wu_ref,
     wd_ref,
     wp_ref,
-    wq_ref,
-    out_ref,
-    dqkv_ref,
+    got_ref,
     grad_ref,
-    wide_ref,
+    sems,
 ):
+    ff = a1_ref.shape[1]
+    step = 512
+    chunks = ff // step
+    first = pltpu.make_async_copy(proj_hbm, wp_ref, sems.at[3 * chunks])
+    first.start()
+    waits = []
+    for c in range(chunks):
+        at = pl.ds(c * step, step)
+        trio = [
+            pltpu.make_async_copy(down_hbm.at[at, :], wd_ref.at[at, :], sems.at[3 * c]),
+            pltpu.make_async_copy(gate_hbm.at[:, at], wg_ref.at[:, at], sems.at[3 * c + 1]),
+            pltpu.make_async_copy(up_hbm.at[:, at], wu_ref.at[:, at], sems.at[3 * c + 2]),
+        ]
+        for copy in trio:
+            copy.start()
+        waits.append(trio)
     me = lax.axis_index("seq") * 4 + lax.axis_index("tile")
     brow = pos_ref[pl.ds(me, 1), :] >> 9
     n = brow.shape[1]
@@ -231,43 +276,42 @@
     before = iota((n, n), 1) < iota((n, n), 0)
     rank = jnp.sum(jnp.where((bcol == brow) & before, 1, 0), axis=1, keepdims=True)
     code = bcol[:, 0:1] * SLOTS + rank
-    seat = iota((n, 256), 1)
-    want = (((seat >> 3) & 7) * 4 + (seat >> 6)) * SLOTS + (seat & 7)
+    code = jnp.concatenate([code, code + 4096], axis=0)
+    seat = iota((2 * n, BLK), 1)
+    want = (((seat >> 4) & 7) * 4 + (seat >> 7)) * SLOTS + (seat & 7) + 4096 * ((seat >> 3) & 1)
     picker = jnp.where(code == want, 1.0, 0.0).astype(BF)
-    wide_ref[...] = ret_ref[...].astype(F32).reshape(8, 16, SLOTS, 768)
-    width = HEADS * HD
-    for h in range(HEADS):
-        t, j = h // 4, h % 4
-        rows = wide_ref[:, j * 4 + t, :, :].reshape(64, 768)
+    for pair in range(HEADS // 2):
+        j, t = pair // 2, 2 * (pair % 2)
+        tile = ret_ref[:, 16 * pair : 16 * pair + 16, :].reshape(128, 768)
         stacked = jnp.concatenate(
-            [rows[:, (j ^ b) * 192 : (j ^ b) * 192 + 192] for b in range(4)], axis=0
-        ).astype(BF)
-        got = mm(picker, stacked)
-        for part in range(3):
-            dqkv_ref[:, part * width + h * HD : part * width + h * HD + HD] = got[
-                :, HD * part : HD * part + HD
-            ].astype(BF)
-        grad_ref[:, h * HD : h * HD + HD] = got[:, 144:192]
-    dnorm = mm(dqkv_ref[...], wq_ref[...], NT)
+            [tile[:, (j ^ b) * 192 : (j ^ b) * 192 + 192] for b in range(4)], axis=0
+        )
+        got = mm(picker, stacked).astype(BF)
+        for tp in range(2):
+            h = 4 * (t + tp) + j
+            got_ref[:, 192 * h : 192 * h + 192] = got[n * tp : n * tp + n]
+            grad_ref[:, h * HD : h * HD + HD] = got[n * tp : n * tp + n, 144:192]
+    dnorm = mm(got_ref[...], wqp_ref[...], NT)
     slide_norm, slide_inv = normalize(x_ref[...].astype(F32))
-    dslide = (grad_ref[...] + norm_back(slide_norm, slide_inv, dnorm)).astype(BF)
+    dslide = (grad_ref[...].astype(F32) + norm_back(slide_norm, slide_inv, dnorm)).astype(BF)
+    first.wait()
     dembed = mm(dslide, wp_ref[...], NT).astype(BF)
-    ff = gate_ref.shape[1]
-    step = 512
     dfeat = jnp.zeros(feat_ref.shape, F32)
-    for c in range(ff // step):
+    for c in range(chunks):
         at = slice(c * step, c * step + step)
+        waits[c][0].wait()
         dhidden = mm(dembed, wd_ref[at, :], NT)
-        gate = gate_ref[:, at]
-        sig = jax.nn.sigmoid(gate)
-        dgate = (dhidden * up_ref[:, at] * sig * (1.0 + gate * (1.0 - sig))).astype(BF)
-        dup = (dhidden * gate * sig).astype(BF)
-        dfeat = dfeat + mm(dgate, wg_ref[:, at], NT) + mm(dup, wu_ref[:, at], NT)
+        dgate = (dhidden * a1_ref[:, at]).astype(BF)
+        dup = (dhidden * a2_ref[:, at]).astype(BF)
+        waits[c][1].wait()
+        dfeat = dfeat + mm(dgate, wg_ref[:, at], NT)
+        waits[c][2].wait()
+        dfeat = dfeat + mm(dup, wu_ref[:, at], NT)
     normed, inv = normalize(feat_ref[...].astype(F32))
     out_ref[...] = (dembed.astype(F32) + norm_back(normed, inv, dfeat)).astype(BF)
 
 
-def place_kernel(shift_ref, recv_ref, tab_ref, y_ref, yt_ref, y2_ref):
+def place_kernel(shift_ref, recv_ref, tab_ref, _after_ref, y_ref, yt_ref, y2_ref):
     _, base, part = offsets(shift_ref)
     o2 = pl.multiple_of(base + 32 * part, 32)
     for d in range(4):
@@ -458,8 +502,10 @@
     g2_ref,
     g3_ref,
     tab_ref,
+    out_hbm,
+    sum_ref,
     out_ref,
-    sum_ref,
+    sems,
 ):
     _, base, part = offsets(shift_ref)
     base = pl.multiple_of(base, 128)
@@ -472,6 +518,7 @@
     extra = jnp.concatenate([dq_ref[...], dkv], axis=0)
     lane = iota((1, 128), 1) >> 5
     rows = tab_ref.shape[0]
+    outs = []
     for d in range(4):
         grad_ref = (g0_ref, g1_ref, g2_ref, g3_ref)[d]
         sum_ref[...] = dall_ref[d]
@@ -481,14 +528,21 @@
         both = jnp.concatenate([sum_ref[...].astype(BF), grad_ref[...]], axis=0)
         onehot = jnp.where(tab_ref[:, d : d + 1] == iota((rows, BLK), 1), 1.0, 0.0).astype(BF)
         out_ref[:, 192 * d : 192 * d + 192] = mm(onehot, both, NT).astype(BF)
-
-
-def out_kernel(s0_ref, s1_ref, s2_ref, s3_ref, out_ref, tmp_ref):
+        if d % 2:
+            at = pl.ds(384 * (d // 2), 384)
+            copy = pltpu.make_async_copy(out_ref.at[:, at], out_hbm.at[:, at], sems.at[d // 2])
+            copy.start()
+            outs.append(copy)
+    for copy in outs:
+        copy.wait()
+
+
+def out_kernel(s0_ref, s1_ref, s2_ref, s3_ref, _after_ref, out_ref, tmp_ref):
     j = lax.axis_index("seq") & 3
     for d in range(4):
         at = pl.multiple_of((j ^ d) * HD, 16)
         tmp_ref[pl.ds(at, HD), :] = (s0_ref, s1_ref, s2_ref, s3_ref)[d][...]
-    out_ref[...] = mm(order_matrix(), tmp_ref[...], NT).astype(BF)
+    out_ref[...] = mm(tmp_ref[...], order_matrix(), NT).astype(BF)
 
 
 def swap(value, distance, count):
@@ -512,7 +566,7 @@
     ff = gate_weight.shape[1]
     slide_width = input_projection_weight.shape[1]
     all_pos = positions.reshape(device_count, rows)
-    routed = ((device_count * SLOTS, slide_width), BF)
+    routed = ((8, 16 * SLOTS, slide_width), BF)
     weights = (gate_weight, up_weight, down_weight, input_projection_weight, query_key_value_weight)
 
     def exchange(block):
@@ -534,17 +588,19 @@
             pltpu.VMEM((width, slide_width), BF),
             pltpu.VMEM((slide_width, 3 * slide_width), BF),
             pltpu.VMEM((rows, 3 * slide_width), BF),
-            pltpu.VMEM((rows, 4 * slide_width), BF),
-            pltpu.VMEM((8, 16, SLOTS, slide_width), F32),
-            pltpu.SemaphoreType.DMA((14,)),
+            pltpu.VMEM((2 * rows, 192), BF),
+            pltpu.VMEM((BLK, 2 * rows), BF),
+            pltpu.VMEM((8, 16 * SLOTS, slide_width), BF),
+            pltpu.SemaphoreType.DMA((14 + HEADS // 2,)),
         ],
         n_any=5,
-        limit=48,
+        n_any_out=1,
+        limit=34,
     )(tile_features, all_pos, *weights)
     arrived = exchange(outgoing)
 
     grads = call(order_kernel, [((HD, BLK), BF)] * 4, [pltpu.VMEM((192, BLK), BF)])(
-        slide_output_gradient
+        slide_output_gradient.T
     )
     grads = [grads[0]] + [swap(grads[d], d, seq_count) for d in range(1, 4)]
     table, table_col = call(
@@ -552,11 +608,17 @@
         [((8, device_count * SLOTS), I32), ((device_count * SLOTS, 8), I32)],
     )(all_pos)
 
+    a1, a2, wqp = call(
+        between_kernel,
+        [((rows, ff), F32), ((rows, ff), F32), ((slide_width, 4 * slide_width), BF)],
+    )(gate_proj, up_proj, query_key_value_weight)
+
     y, yt, y2 = call(
         place_kernel,
         [((4, BLK, 192), BF), ((4, 192, BLK), BF), ((128, 192), BF)],
         n_smem=1,
-    )(dilation_shift, arrived, table)
+        n_after=1,
+    )(dilation_shift, arrived, table, a1)
     y2_in = [swap(y2, 4 * e, seq_count) for e in range(1, 4)]
     e0, m0, e1, m1, u, l = call(
         forward_kernel,
@@ -596,26 +658,47 @@
         [pltpu.VMEM((BLK, BLK), BF)],
         n_smem=1,
     )(dilation_shift, y, yt, e0, m0, e1, m1, gs, ds)
-    dall, parts = lax.optimization_barrier((dall, parts))
     (returning,) = call(
         return_kernel,
-        [routed],
-        [pltpu.VMEM((144, BLK), F32)],
+        [((device_count * SLOTS, slide_width), BF)],
+        [
+            pltpu.VMEM((144, BLK), F32),
+            pltpu.VMEM((device_count * SLOTS, slide_width), BF),
+            pltpu.SemaphoreType.DMA((2,)),
+        ],
         n_smem=1,
+        n_any_out=1,
+        limit=6,
     )(dilation_shift, dall, own, dq2, *back, *grads, table_col)
     returned = exchange(returning)
-    (slide_out,) = call(out_kernel, [((BLK, 192), BF)], [pltpu.VMEM((192, BLK), BF)])(*parts)
     (tile_grad,) = call(
         backward_mlp_kernel,
         [((rows, width), BF)],
         [
-            pltpu.VMEM((rows, 3 * slide_width), BF),
-            pltpu.VMEM((rows, slide_width), F32),
-            pltpu.VMEM((8, 16, SLOTS, slide_width), F32),
+            pltpu.VMEM((width, ff), BF),
+            pltpu.VMEM((width, ff), BF),
+            pltpu.VMEM((ff, width), BF),
+            pltpu.VMEM((width, slide_width), BF),
+            pltpu.VMEM((rows, 4 * slide_width), BF),
+            pltpu.VMEM((rows, slide_width), BF),
+            pltpu.SemaphoreType.DMA((13,)),
         ],
-        limit=40,
-    )(returned, all_pos, tile_features, x, gate_proj, up_proj, *weights)
-    return (slide_out, tile_grad)
+        n_any=4,
+        limit=32,
+    )(
+        returned.reshape(8, 16 * SLOTS, slide_width),
+        all_pos,
+        tile_features,
+        x,
+        a1,
+        a2,
+        wqp,
+        *weights[:4],
+    )
+    (slide_out,) = call(
+        out_kernel, [((192, BLK), BF)], [pltpu.VMEM((192, BLK), BF)], n_after=1
+    )(*parts, tile_grad)
+    return (slide_out.T, tile_grad)
 
 
 def solution(mesh):

time: 139 us -> 152 us (1.094)
  local copies, waits for them, and re-layouts: 19.5 us -> 36.9 us
  waiting for transfers between devices: 40.3 us -> 26.8 us
  Pallas kernels: 45.9 us -> 53.9 us
    unnamed x52 -> x76, local copies, waits for them, and re-layouts: 19.5 us -> 36.9 us
    all_to_all x2, waiting for transfers between devices: 40.3 us -> 26.7 us  [exchange(): lax.all_to_all(block.reshape(device_count, SLOTS, slide_width), ('seq', '...]
    pallas_call x10 -> x11, Pallas kernels: 45.9 us -> 53.9 us  [run(): pl.pallas_call(kernel, out_shape=shapes, in_specs=specs, out_specs=out_sp...]
  transfers between devices with their start and end apart: 14 -> 14, of which waited for: 2 -> 2; matrix products, arithmetic and copies ran while one was open for 1% -> 0% of each run, Pallas kernels for 9% -> 23%
where the time goes in v2:
time: 152 us; the launch traced here: 151 us
  Pallas kernels  53.9 us (35%)
  local copies, waits for them, and re-layouts  36.9 us (24%)
  starting transfers between devices  32.6 us (21%)
  waiting for transfers between devices  26.8 us (18%)
    pallas_call x11, Pallas kernels, run(): pl.pallas_call(kernel, out_shape=shapes, in_specs=specs, out_specs=out_sp...  53.9 us
    unnamed x76, local copies, waits for them, and re-layouts  36.9 us
    all_to_all x2, waiting for transfers between devices, exchange(): lax.all_to_all(block.reshape(device_count, SLOTS, slide_width), ('seq', '...  26.7 us
    all_to_all x2, starting transfers between devices, exchange(): lax.all_to_all(block.reshape(device_count, SLOTS, slide_width), ('seq', '...  18.4 us
    ppermute x12, starting transfers between devices, swap(): return lax.ppermute(value, 'seq', [(i, i ^ distance) for i in range(count)])  14.2 us
  transfers between devices with their start and end apart: 14, of which 2 were waited for; matrix products, arithmetic and copies ran while one was open for 0% of the time, Pallas kernels for 23%

profile of v2, /device:TPU:1, one launch (start us, length us, event | category | flops | bytes accessed | tf_op | source)
XLA Modules:
  0.0 151.1 jit_solution(13634716901466189234)
XLA Ops:
  0.6 2.8 %copy-done = bf16[1536,2048]{1,0:T(8,128)(2,1)S(1)} copy-done((bf16[1536,2048]{1,0:T(8,128)(2,1)S(1)}, bf16[1536,2048]{1,0:T(8,128)(2,1)}, u32[]{:S(2)}) %copy-start) | copy-done | bytes 6291480
  3.4 2.0 %copy-done.2 = bf16[768,2304]{1,0:T(8,128)(2,1)S(1)} copy-done((bf16[768,2304]{1,0:T(8,128)(2,1)S(1)}, bf16[768,2304]{1,0:T(8,128)(2,1)}, u32[]{:S(2)}) %copy-start.2) | copy-done | bytes 3538968
  5.4 1.7 %copy-done.4 = bf16[1536,768]{1,0:T(8,128)(2,1)S(1)} copy-done((bf16[1536,768]{1,0:T(8,128)(2,1)S(1)}, bf16[1536,768]{1,0:T(8,128)(2,1)}, u32[]{:S(2)}) %copy-start.4) | copy-done | bytes 2359320
  8.9 12.6 %shard_map.104 = (bf16[8,128,768]{2,1,0:T(8,128)(2,1)S(1)}, bf16[128,768]{1,0:T(8,128)(2,1)S(1)}, f32[128,2048]{1,0:T(8,128)S(1)}, f32[128,2048]{1,0:T(8,128)S(1)}) custom-call(bf16[128,1536]{1,0:T(8,128)(2,1)S(1)} %copy-done.13, s32[128,128]{1,0:T(8,128)S(1)} %bitcast.15, bf16[1536,2048]{1,0:T(8,128)(2,1)S(1)} %copy-done, bf16[1536,2048]{1,0:T(8,128)(2,1)} %up_hbm.3, ...), custom_call_target="tpu_custom_call" | custom-call | tf_op jit(solution)/shard_map/pallas_call | solution.py:61
  21.6 1.2 copy-done.15
  22.8 1.0 copy-done.16
  25.4 11.9 %all-to-all-start = ((bf16[128,8,768]{2,1,0:T(8,128)(2,1)}), bf16[128,8,768]{2,1,0:T(8,128)(2,1)}, u32[]{:S(2)}, u32[]{:S(2)}) async-start(bf16[128,8,768]{2,1,0:T(8,128)(2,1)} %bitcast.14), calls=%async_computation | async-start | bytes 3145728 | tf_op jit(solution)/shard_map/all_to_all | solution.py:573
  39.8 1.1 collective-permute-start.3
  45.8 1.2 copy-done.17
  47.0 1.2 copy-done.19
  48.2 5.3 %shard_map.106 = (f32[128,2048]{1,0:T(8,128)S(1)}, f32[128,2048]{1,0:T(8,128)S(1)}, bf16[768,3072]{1,0:T(8,128)(2,1)S(1)}) custom-call(f32[128,2048]{1,0:T(8,128)S(1)} %copy-done.17, f32[128,2048]{1,0:T(8,128)S(1)} %copy-done.19, bf16[768,2304]{1,0:T(8,128)(2,1)S(1)} %copy-done.3), custom_call_target="tpu_custom_call" | custom-call | tf_op jit(solution)/shard_map/pallas_call | solution.py:61
  53.6 2.2 %copy-done.7 = bf16[768,3072]{1,0:T(8,128)(2,1)} copy-done((bf16[768,3072]{1,0:T(8,128)(2,1)}, bf16[768,3072]{1,0:T(8,128)(2,1)S(1)}, u32[]{:S(2)}) %copy-start.7) | copy-done | bytes 4718616
  56.7 1.0 copy-done.20
  57.8 4.6 %all-to-all-done = bf16[128,8,768]{2,1,0:T(8,128)(2,1)} async-done(((bf16[128,8,768]{2,1,0:T(8,128)(2,1)}), bf16[128,8,768]{2,1,0:T(8,128)(2,1)}, u32[]{:S(2)}, u32[]{:S(2)}) %all-to-all-start) | async-done | bytes 1572896 | tf_op jit(solution)/shard_map/all_to_all | solution.py:573
  62.4 1.2 copy-done.10
  64.4 2.8 %shard_map.107 = (bf16[4,512,192]{2,1,0:T(8,128)(2,1)S(1)}, bf16[4,192,512]{2,1,0:T(8,128)(2,1)S(1)}, bf16[128,192]{1,0:T(8,128)(2,1)S(1)}) custom-call(s32[2,16]{1,0:T(2,128)S(1)} %copy-done.34, bf16[1024,768]{1,0:T(8,128)(2,1)} %bitcast.2.recv_ref, s32[8,1024]{1,0:T(8,128)S(1)} %copy-done.33, f32[128,2048]{1,0:T(8,128)S(1)} %copy-done.10), custom_call_target="tpu_custom_call" | custom-call | tf_op jit(solution)/shard_map/pallas_call | solution.py:61
  68.3 3.2 %collective-permute-start = (bf16[128,192]{1,0:T(8,128)(2,1)S(1)}, bf16[128,192]{1,0:T(8,128)(2,1)S(1)}, u32[]{:S(2)}, u32[]{:S(2)}) collective-permute-start(bf16[128,192]{1,0:T(8,128)(2,1)S(1)} %get-tuple-element.39.a0_ref), channel_id=1, source_target_pairs={{0,16},{4,20},{8,24},{12,28},{16,0},{20,4},{24,8},{28,12},{32,48},... | collective-permute-start | bytes 147464 | tf_op jit(solution)/shard_map/ppermute | solution.py:549
  71.5 4.3 %shard_map.108 = (bf16[4,512,512]{2,1,0:T(8,128)(2,1)S(1)}, bf16[4,512,512]{2,1,0:T(8,128)(2,1)S(1)}, bf16[512,512]{1,0:T(8,128)(2,1)S(1)}, bf16[512,512]{1,0:T(...) custom-call(s32[2,16]{1,0:T(2,128)S(1)} %copy-done.34, ...), custom_call_target="tpu_custom_call" | custom-call | tf_op jit(solution)/shard_map/pallas_call | solution.py:61
  75.8 2.0 %shard_map.110 = (bf16[48,512]{1,0:T(8,128)(2,1)S(1)}, bf16[48,512]{1,0:T(8,128)(2,1)S(1)}, bf16[48,512]{1,0:T(8,128)(2,1)S(1)}, bf16[48,512]{1,0:T(8,128)(2,1)S...) custom-call(s32[2,16]{1,0:T(2,128)S(1)} %copy-done.34, ...), custom_call_target="tpu_custom_call" | custom-call | tf_op jit(solution)/shard_map/pallas_call | solution.py:61
  80.0 1.1 collective-permute-start.10
  81.1 2.7 %collective-permute-start.9 = (bf16[96,128]{1,0:T(8,128)(2,1)S(1)}, bf16[96,128]{1,0:T(8,128)(2,1)S(1)}, u32[]{:S(2)}, u32[]{:S(2)}) collective-permute-start(bf16[96,128]{1,0:T(8,128)(2,1)S(1)} %get-tuple-element.66), channel_id=1, source_target_pairs={{0,16},{4,20},{8,24},{12,28},{16,0},{20,4},{24,8},{28,12},{32,48},... | collective-permute-start | bytes 73736 | tf_op jit(solution)/shard_map/ppermute | solution.py:549
  83.8 4.4 %shard_map.111.dall_ref = f32[4,144,512]{2,1,0:T(8,128)S(1)} custom-call(s32[2,16]{1,0:T(2,128)S(1)} %copy-done.34, bf16[4,512,192]{2,1,0:T(8,128)(2,1)S(1)} %get-tuple-element.40.y_ref, bf16[4,192,512]{2,1,0:T(8,128)(2,1)S(1)} %get-tuple-element.38.yt_ref, bf16[4,512,512]{2,1,0:T(8,128)(2,1)S(1)} %get-tuple-element.51.e0_ref, ...), custom_call_target="tpu_custom_call" | custom-call | tf_op jit(solution)/shard_map/pallas_call | solution.py:61
  88.3 3.2 %shard_map.112 = bf16[1024,768]{1,0:T(8,128)(2,1)S(1)} custom-call(s32[2,16]{1,0:T(2,128)S(1)} %copy-done.34, f32[4,144,512]{2,1,0:T(8,128)S(1)} %shard_map.111.dall_ref, f32[96,128]{1,0:T(8,128)S(1)} %get-tuple-element.57.own_ref, f32[48,128]{1,0:T(8,128)S(1)} %get-tuple-element.58.dq_ref, bf16[96,128]{1,0:T(8,128)(2,1)S(1)} %collective-permute-done.9.r1_ref, ...), custom_call_target="tpu_custom_call" | custom-call | tf_op jit(solution)/shard_map/pallas_call | solution.py:61
  91.5 1.2 copy-done.6
  92.8 6.5 %all-to-all-start.1 = ((bf16[128,8,768]{2,1,0:T(8,128)(2,1)}), bf16[128,8,768]{2,1,0:T(8,128)(2,1)}, u32[]{:S(2)}, u32[]{:S(2)}) async-start(bf16[128,8,768]{2,1,0:T(8,128)(2,1)} %bitcast.13), calls=%async_computation.1 | async-start | bytes 3145728 | tf_op jit(solution)/shard_map/all_to_all | solution.py:573
  99.2 1.4 collective-permute-start.6
  102.3 22.1 %all-to-all-done.1 = bf16[128,8,768]{2,1,0:T(8,128)(2,1)} async-done(((bf16[128,8,768]{2,1,0:T(8,128)(2,1)}), bf16[128,8,768]{2,1,0:T(8,128)(2,1)}, u32[]{:S(2)}, u32[]{:S(2)}) %all-to-all-start.1) | async-done | bytes 1572896 | tf_op jit(solution)/shard_map/all_to_all | solution.py:573
  124.5 2.8 %copy-done.1 = bf16[1536,2048]{1,0:T(8,128)(2,1)S(1)} copy-done((bf16[1536,2048]{1,0:T(8,128)(2,1)S(1)}, bf16[1536,2048]{1,0:T(8,128)(2,1)}, u32[]{:S(2)}) %copy-start.1) | copy-done | bytes 6291480
  127.3 2.3 %copy-done.8 = bf16[768,3072]{1,0:T(8,128)(2,1)S(1)} copy-done((bf16[768,3072]{1,0:T(8,128)(2,1)S(1)}, bf16[768,3072]{1,0:T(8,128)(2,1)}, u32[]{:S(2)}) %copy-start.8) | copy-done | bytes 4718616
  130.6 1.2 copy-done.21
  132.7 15.4 %shard_map.113._after_ref = bf16[128,1536]{1,0:T(8,128)(2,1)} custom-call(bf16[8,128,768]{2,1,0:T(8,128)(2,1)} %bitcast.8.ret_ref, s32[128,128]{1,0:T(8,128)S(1)} %bitcast.17, bf16[128,1536]{1,0:T(8,128)(2,1)S(1)} %copy-done.14, bf16[128,768]{1,0:T(8,128)(2,1)S(1)} %copy-done.28, f32[128,2048]{1,0:T(8,128)S(1)} %copy-done.11, f32[128,2048]{1,0:T(8,128)S(1)} %copy-done.21, ...), custom_call_target="tpu_custom_call" | custom-call | tf_op jit(solution)/shard_map/pallas_call | solution.py:61
  149.2 1.9 %shard_map.114 = bf16[192,512]{1,0:T(8,128)(2,1)} custom-call(bf16[48,512]{1,0:T(8,128)(2,1)S(1)} %get-tuple-element.47.s0_ref, bf16[48,512]{1,0:T(8,128)(2,1)} %collective-permute-done.6.s1_ref, bf16[48,512]{1,0:T(8,128)(2,1)} %collective-permute-done.7.s2_ref, bf16[48,512]{1,0:T(8,128)(2,1)} %collective-permute-done.8.s3_ref, bf16[128,1536]{1,0:T(8,128)(2,1)S(1)} %copy-done.12), custom_call_target="tpu_custom_call" | custom-call | tf_op jit(solution)/shard_map/pallas_call | solution.py:61
  (84 shorter events, 20.5 us)
Async XLA Ops:
  0.6 2.8 %copy-start = (bf16[1536,2048]{1,0:T(8,128)(2,1)S(1)}, bf16[1536,2048]{1,0:T(8,128)(2,1)}, u32[]{:S(2)}) copy-start(bf16[1536,2048]{1,0:T(8,128)(2,1)} %gate_hbm.3) | copy-start | bytes 18874372
  3.4 2.0 %copy-start.2 = (bf16[768,2304]{1,0:T(8,128)(2,1)S(1)}, bf16[768,2304]{1,0:T(8,128)(2,1)}, u32[]{:S(2)}) copy-start(bf16[768,2304]{1,0:T(8,128)(2,1)} %wq_ref.1) | copy-start | bytes 10616836
  5.4 1.7 %copy-start.4 = (bf16[1536,768]{1,0:T(8,128)(2,1)S(1)}, bf16[1536,768]{1,0:T(8,128)(2,1)}, u32[]{:S(2)}) copy-start(bf16[1536,768]{1,0:T(8,128)(2,1)} %proj_hbm.3) | copy-start | bytes 7077892
  8.9 36.9 %copy-start.3 = (bf16[768,2304]{1,0:T(8,128)(2,1)S(1)}, bf16[768,2304]{1,0:T(8,128)(2,1)}, u32[]{:S(2)}) copy-start(bf16[768,2304]{1,0:T(8,128)(2,1)} %wq_ref.1) | copy-start | bytes 10616836
  25.4 37.0 %all-to-all-start = ((bf16[128,8,768]{2,1,0:T(8,128)(2,1)}), bf16[128,8,768]{2,1,0:T(8,128)(2,1)}, u32[]{:S(2)}, u32[]{:S(2)}) async-start(bf16[128,8,768]{2,1,0:T(8,128)(2,1)} %bitcast.14), calls=%async_computation | async-start | bytes 3145728 | tf_op jit(solution)/shard_map/all_to_all | solution.py:573
  39.8 28.5 %collective-permute-start.3 = (bf16[48,512]{1,0:T(8,128)(2,1)}, bf16[48,512]{1,0:T(8,128)(2,1)}, u32[]{:S(2)}, u32[]{:S(2)}) collective-permute-start(bf16[48,512]{1,0:T(8,128)(2,1)} %get-tuple-element.44), channel_id=1, source_target_pairs={{0,4},{4,0},{8,12},{12,8},{16,20},{20,16},{24,28},{28,24},{32,36},... | collective-permute-start | bytes 147464 | tf_op jit(solution)/shard_map/ppermute | solution.py:549
  41.0 34.8 %collective-permute-start.4 = (bf16[48,512]{1,0:T(8,128)(2,1)}, bf16[48,512]{1,0:T(8,128)(2,1)}, u32[]{:S(2)}, u32[]{:S(2)}) collective-permute-start(bf16[48,512]{1,0:T(8,128)(2,1)} %get-tuple-element.45), channel_id=1, source_target_pairs={{0,8},{4,12},{8,0},{12,4},{16,24},{20,28},{24,16},{28,20},{32,40},... | collective-permute-start | bytes 147464 | tf_op jit(solution)/shard_map/ppermute | solution.py:549
  41.7 34.1 %collective-permute-start.5 = (bf16[48,512]{1,0:T(8,128)(2,1)}, bf16[48,512]{1,0:T(8,128)(2,1)}, u32[]{:S(2)}, u32[]{:S(2)}) collective-permute-start(bf16[48,512]{1,0:T(8,128)(2,1)} %get-tuple-element.46), channel_id=1, source_target_pairs={{0,12},{4,8},{8,4},{12,0},{16,28},{20,24},{24,20},{28,16},{32,44},... | collective-permute-start | bytes 147464 | tf_op jit(solution)/shard_map/ppermute | solution.py:549
  45.8 1.2 copy-start.17
  47.0 1.2 copy-start.19
  48.2 14.2 %copy-start.34 = (s32[2,16]{1,0:T(2,128)S(1)}, s32[2,16]{1,0:T(2,128)}, u32[]{:S(2)}) copy-start(s32[2,16]{1,0:T(2,128)} %shift_ref.9) | copy-start | bytes 388
  53.6 2.2 %copy-start.7 = (bf16[768,3072]{1,0:T(8,128)(2,1)}, bf16[768,3072]{1,0:T(8,128)(2,1)S(1)}, u32[]{:S(2)}) copy-start(bf16[768,3072]{1,0:T(8,128)(2,1)S(1)} %get-tuple-element.63.wqp_ref) | copy-start | bytes 14155780
  62.4 1.2 copy-start.10
  64.4 11.4 %copy-start.30 = (bf16[48,512]{1,0:T(8,128)(2,1)S(1)}, bf16[48,512]{1,0:T(8,128)(2,1)}, u32[]{:S(2)}) copy-start(bf16[48,512]{1,0:T(8,128)(2,1)} %copy-done.29) | copy-start | bytes 147460
  67.2 8.6 %collective-permute-start.2 = (bf16[128,192]{1,0:T(8,128)(2,1)S(1)}, bf16[128,192]{1,0:T(8,128)(2,1)S(1)}, u32[]{:S(2)}, u32[]{:S(2)}) collective-permute-start(bf16[128,192]{1,0:T(8,128)(2,1)S(1)} %get-tuple-element.39.a0_ref), channel_id=1, source_target_pairs={{0,48},{4,52},{8,56},{12,60},{16,32},{20,36},{24,40},{28,44},{32,1... | collective-permute-start | bytes 147464 | tf_op jit(solution)/shard_map/ppermute | solution.py:549
  67.3 8.5 %collective-permute-start.1 = (bf16[128,192]{1,0:T(8,128)(2,1)S(1)}, bf16[128,192]{1,0:T(8,128)(2,1)S(1)}, u32[]{:S(2)}, u32[]{:S(2)}) collective-permute-start(bf16[128,192]{1,0:T(8,128)(2,1)S(1)} %get-tuple-element.39.a0_ref), channel_id=1, source_target_pairs={{0,32},{4,36},{8,40},{12,44},{16,48},{20,52},{24,56},{28,60},{32,0... | collective-permute-start | bytes 147464 | tf_op jit(solution)/shard_map/ppermute | solution.py:549
  68.3 7.5 %collective-permute-start = (bf16[128,192]{1,0:T(8,128)(2,1)S(1)}, bf16[128,192]{1,0:T(8,128)(2,1)S(1)}, u32[]{:S(2)}, u32[]{:S(2)}) collective-permute-start(bf16[128,192]{1,0:T(8,128)(2,1)S(1)} %get-tuple-element.39.a0_ref), channel_id=1, source_target_pairs={{0,16},{4,20},{8,24},{12,28},{16,0},{20,4},{24,8},{28,12},{32,48},... | collective-permute-start | bytes 147464 | tf_op jit(solution)/shard_map/ppermute | solution.py:549
  79.7 8.6 %collective-permute-start.11 = (bf16[96,128]{1,0:T(8,128)(2,1)S(1)}, bf16[96,128]{1,0:T(8,128)(2,1)S(1)}, u32[]{:S(2)}, u32[]{:S(2)}) collective-permute-start(bf16[96,128]{1,0:T(8,128)(2,1)S(1)} %get-tuple-element.64), channel_id=1, source_target_pairs={{0,48},{4,52},{8,56},{12,60},{16,32},{20,36},{24,40},{28,44},{32,1... | collective-permute-start | bytes 73736 | tf_op jit(solution)/shard_map/ppermute | solution.py:549
  80.0 8.3 %collective-permute-start.10 = (bf16[96,128]{1,0:T(8,128)(2,1)S(1)}, bf16[96,128]{1,0:T(8,128)(2,1)S(1)}, u32[]{:S(2)}, u32[]{:S(2)}) collective-permute-start(bf16[96,128]{1,0:T(8,128)(2,1)S(1)} %get-tuple-element.65), channel_id=1, source_target_pairs={{0,32},{4,36},{8,40},{12,44},{16,48},{20,52},{24,56},{28,60},{32,0... | collective-permute-start | bytes 73736 | tf_op jit(solution)/shard_map/ppermute | solution.py:549
  81.1 7.2 %collective-permute-start.9 = (bf16[96,128]{1,0:T(8,128)(2,1)S(1)}, bf16[96,128]{1,0:T(8,128)(2,1)S(1)}, u32[]{:S(2)}, u32[]{:S(2)}) collective-permute-start(bf16[96,128]{1,0:T(8,128)(2,1)S(1)} %get-tuple-element.66), channel_id=1, source_target_pairs={{0,16},{4,20},{8,24},{12,28},{16,0},{20,4},{24,8},{28,12},{32,48},... | collective-permute-start | bytes 73736 | tf_op jit(solution)/shard_map/ppermute | solution.py:549
  83.8 4.5 %copy-start.26 = (s32[1024,8]{1,0:T(8,128)S(1)}, s32[1024,8]{1,0:T(8,128)}, u32[]{:S(2)}) copy-start(s32[1024,8]{1,0:T(8,128)} %copy-done.25) | copy-start | bytes 98308
  88.3 36.1 %copy-start.11 = (f32[128,2048]{1,0:T(8,128)S(1)}, f32[128,2048]{1,0:T(8,128)}, u32[]{:S(2)}) copy-start(f32[128,2048]{1,0:T(8,128)} %copy-done.9) | copy-start | bytes 3145732
  91.5 1.2 copy-start.6
  92.7 31.7 %copy-start.5 = (bf16[1536,768]{1,0:T(8,128)(2,1)S(1)}, bf16[1536,768]{1,0:T(8,128)(2,1)}, u32[]{:S(2)}) copy-start(bf16[1536,768]{1,0:T(8,128)(2,1)} %proj_hbm.3) | copy-start | bytes 7077892
  92.7 31.7 %copy-start.24 = (s32[16384]{0:T(1024)S(1)}, s32[16384]{0:T(1024)}, u32[]{:S(2)}) copy-start(s32[16384]{0:T(1024)} %param.15) | copy-start | bytes 196612
  92.8 31.7 %all-to-all-start.1 = ((bf16[128,8,768]{2,1,0:T(8,128)(2,1)}), bf16[128,8,768]{2,1,0:T(8,128)(2,1)}, u32[]{:S(2)}, u32[]{:S(2)}) async-start(bf16[128,8,768]{2,1,0:T(8,128)(2,1)} %bitcast.13), calls=%async_computation.1 | async-start | bytes 3145728 | tf_op jit(solution)/shard_map/all_to_all | solution.py:573
  99.2 49.0 %collective-permute-start.6 = (bf16[48,512]{1,0:T(8,128)(2,1)}, bf16[48,512]{1,0:T(8,128)(2,1)}, u32[]{:S(2)}, u32[]{:S(2)}) collective-permute-start(bf16[48,512]{1,0:T(8,128)(2,1)} %copy-done.37), channel_id=1, source_target_pairs={{0,4},{4,0},{8,12},{12,8},{16,20},{20,16},{24,28},{28,24},{32,36},... | collective-permute-start | bytes 147464 | tf_op jit(solution)/shard_map/ppermute | solution.py:549
  100.6 47.6 %collective-permute-start.7 = (bf16[48,512]{1,0:T(8,128)(2,1)}, bf16[48,512]{1,0:T(8,128)(2,1)}, u32[]{:S(2)}, u32[]{:S(2)}) collective-permute-start(bf16[48,512]{1,0:T(8,128)(2,1)} %copy-done.36), channel_id=1, source_target_pairs={{0,8},{4,12},{8,0},{12,4},{16,24},{20,28},{24,16},{28,20},{32,40},... | collective-permute-start | bytes 147464 | tf_op jit(solution)/shard_map/ppermute | solution.py:549
  101.3 46.9 %collective-permute-start.8 = (bf16[48,512]{1,0:T(8,128)(2,1)}, bf16[48,512]{1,0:T(8,128)(2,1)}, u32[]{:S(2)}, u32[]{:S(2)}) collective-permute-start(bf16[48,512]{1,0:T(8,128)(2,1)} %copy-done.35), channel_id=1, source_target_pairs={{0,12},{4,8},{8,4},{12,0},{16,28},{20,24},{24,20},{28,16},{32,44},... | collective-permute-start | bytes 147464 | tf_op jit(solution)/shard_map/ppermute | solution.py:549
  124.5 2.8 %copy-start.1 = (bf16[1536,2048]{1,0:T(8,128)(2,1)S(1)}, bf16[1536,2048]{1,0:T(8,128)(2,1)}, u32[]{:S(2)}) copy-start(bf16[1536,2048]{1,0:T(8,128)(2,1)} %gate_hbm.3) | copy-start | bytes 18874372
  127.3 2.3 %copy-start.8 = (bf16[768,3072]{1,0:T(8,128)(2,1)S(1)}, bf16[768,3072]{1,0:T(8,128)(2,1)}, u32[]{:S(2)}) copy-start(bf16[768,3072]{1,0:T(8,128)(2,1)} %copy-done.7) | copy-start | bytes 14155780
  130.6 1.2 copy-start.21
  (20 other events, 17.1 us)

commit v3 on v2

--- a/solution.py
+++ b/solution.py
@@ -49,15 +49,19 @@
     return (grads - mean_grad - normed * mean_cross) * inv_std
 
 
-def call(kernel, outs, scratch=(), n_smem=0, n_any=0, n_any_out=0, n_after=0, limit=4):
+def call(kernel, outs, scratch=(), n_smem=0, n_any=0, n_hbm=0, n_hbm_out=0, limit=4):
     def run(*args):
+        n_vmem = len(args) - n_smem - n_any - n_hbm
         specs = [pl.BlockSpec(memory_space=pltpu.SMEM)] * n_smem
-        specs += [pl.BlockSpec(memory_space=pltpu.VMEM)] * (len(args) - n_smem - n_any - n_after)
-        specs += [pl.BlockSpec(memory_space=pltpu.HBM)] * n_any
-        specs += [pl.BlockSpec(memory_space=pl.ANY)] * n_after
-        shapes = [jax.ShapeDtypeStruct(s, d) for s, d in outs]
-        out_specs = [pl.BlockSpec(memory_space=pltpu.HBM)] * n_any_out
-        out_specs += [pl.BlockSpec(memory_space=pltpu.VMEM)] * (len(outs) - n_any_out)
+        specs += [pl.BlockSpec(memory_space=pltpu.VMEM)] * n_vmem
+        specs += [pl.BlockSpec(memory_space=pl.ANY)] * n_any
+        specs += [pl.BlockSpec(memory_space=pltpu.HBM)] * n_hbm
+        out_specs = [pl.BlockSpec(memory_space=pltpu.HBM)] * n_hbm_out
+        out_specs += [pl.BlockSpec(memory_space=pltpu.VMEM)] * (len(outs) - n_hbm_out)
+        shapes = [pltpu.HBM(shape, kind) for shape, kind in outs[:n_hbm_out]]
+        shapes += [jax.ShapeDtypeStruct(shape, kind) for shape, kind in outs[n_hbm_out:]]
+        cut = len(args) - n_hbm
+        held = [pltpu.with_memory_space_constraint(x, pltpu.HBM) for x in args[cut:]]
         return pl.pallas_call(
             kernel,
             out_shape=shapes,
@@ -65,16 +69,35 @@
             out_specs=out_specs,
             scratch_shapes=list(scratch),
             compiler_params=pltpu.CompilerParams(vmem_limit_bytes=limit * 1024 * 1024),
-        )(*args)
+        )(*args[:cut], *held)
 
     return run
 
 
-def order_kernel(grad_ref, g0_ref, g1_ref, g2_ref, g3_ref, tmp_ref):
+def started(copies):
+    for copy in copies:
+        copy.start()
+    return copies
+
+
+def finish(copies):
+    for copy in copies:
+        copy.wait()
+
+
+def order_kernel(grad_ref, g0_hbm, g1_hbm, g2_hbm, g3_hbm, tmp_ref, sems):
     j = lax.axis_index("seq") & 3
     tmp_ref[...] = mm(grad_ref[...], order_matrix()).astype(BF)
-    for d, out_ref in enumerate((g0_ref, g1_ref, g2_ref, g3_ref)):
-        out_ref[...] = tmp_ref[pl.ds(pl.multiple_of((j ^ d) * HD, 16), HD), :]
+    finish(
+        started(
+            [
+                pltpu.make_async_copy(
+                    tmp_ref.at[pl.ds(pl.multiple_of((j ^ d) * HD, 16), HD), :], out, sems.at[d]
+                )
+                for d, out in enumerate((g0_hbm, g1_hbm, g2_hbm, g3_hbm))
+            ]
+        )
+    )
 
 
 def offsets(shift_ref):
@@ -84,7 +107,7 @@
     return (o1 * 128, (o2 & 3) * 128, o2 >> 2)
 
 
-def table_kernel(pos_ref, row_ref, col_ref):
+def table_kernel(pos_ref, row_hbm, col_hbm, row_ref, col_ref, sems):
     s = lax.axis_index("seq")
     pos = pos_ref[...].T
     n = pos.shape[0]
@@ -113,51 +136,73 @@
     table = jnp.concatenate(rows + rows, axis=0) - 1.0
     row_ref[...] = table.astype(I32)
     col_ref[...] = table.T.astype(I32)
+    finish(
+        started(
+            [
+                pltpu.make_async_copy(row_ref, row_hbm, sems.at[0]),
+                pltpu.make_async_copy(col_ref, col_hbm, sems.at[1]),
+            ]
+        )
+    )
 
 
 def forward_mlp_kernel(
-    feat_ref,
-    pos_ref,
+    feat_hbm,
+    pos_hbm,
     gate_hbm,
     up_hbm,
     down_hbm,
     proj_hbm,
     qkvw_hbm,
     out_hbm,
-    x_ref,
-    gate_ref,
-    up_ref,
+    x_hbm,
+    a1_hbm,
+    a2_hbm,
+    feat_ref,
+    pos_ref,
     wg_ref,
     wu_ref,
     wd_ref,
     wp_ref,
     wq_ref,
+    x_ref,
+    a1_ref,
+    a2_ref,
     qkv_ref,
     heads_ref,
     picker_ref,
     tmp_ref,
     sems,
+    out_sems,
 ):
     ff = gate_hbm.shape[1]
     step = 512
     chunks = ff // step
+    first = started(
+        [
+            pltpu.make_async_copy(feat_hbm, feat_ref, sems.at[3 * chunks]),
+            pltpu.make_async_copy(pos_hbm, pos_ref, sems.at[3 * chunks + 1]),
+        ]
+    )
     waits = []
     for c in range(chunks):
         at = pl.ds(c * step, step)
-        trio = [
-            pltpu.make_async_copy(gate_hbm.at[:, at], wg_ref.at[:, at], sems.at[3 * c]),
-            pltpu.make_async_copy(up_hbm.at[:, at], wu_ref.at[:, at], sems.at[3 * c + 1]),
-            pltpu.make_async_copy(down_hbm.at[at, :], wd_ref.at[at, :], sems.at[3 * c + 2]),
+        waits.append(
+            started(
+                [
+                    pltpu.make_async_copy(gate_hbm.at[:, at], wg_ref.at[:, at], sems.at[3 * c]),
+                    pltpu.make_async_copy(up_hbm.at[:, at], wu_ref.at[:, at], sems.at[3 * c + 1]),
+                    pltpu.make_async_copy(down_hbm.at[at, :], wd_ref.at[at, :], sems.at[3 * c + 2]),
+                ]
+            )
+        )
+    last = started(
+        [
+            pltpu.make_async_copy(proj_hbm, wp_ref, sems.at[3 * chunks + 2]),
+            pltpu.make_async_copy(qkvw_hbm, wq_ref, sems.at[3 * chunks + 3]),
         ]
-        for copy in trio:
-            copy.start()
-        waits.append(trio)
-    last = [
-        pltpu.make_async_copy(proj_hbm, wp_ref, sems.at[3 * chunks]),
-        pltpu.make_async_copy(qkvw_hbm, wq_ref, sems.at[3 * chunks + 1]),
-    ]
-    for copy in last:
-        copy.start()
+    )
+    finish(first)
 
     me = lax.axis_index("seq") * 4 + lax.axis_index("tile")
     brow = pos_ref[pl.ds(me, 1), :] >> 9
@@ -174,26 +219,35 @@
     feats = feat_ref[...].astype(F32)
     normed = normalize(feats)[0].astype(BF)
     total = feats
+    outs = []
     for c in range(chunks):
         at = slice(c * step, c * step + step)
         waits[c][0].wait()
         gate = mm(normed, wg_ref[:, at])
-        gate_ref[:, at] = gate
         waits[c][1].wait()
         up = mm(normed, wu_ref[:, at])
-        up_ref[:, at] = up
-        hidden = (gate * jax.nn.sigmoid(gate) * up).astype(BF)
+        sig = jax.nn.sigmoid(gate)
+        silu = gate * sig
+        hidden = (silu * up).astype(BF)
+        a1_ref[:, at] = (up * (sig + silu * (1.0 - sig))).astype(BF)
+        a2_ref[:, at] = silu.astype(BF)
         waits[c][2].wait()
         total = total + mm(hidden, wd_ref[at, :])
+    outs += started(
+        [
+            pltpu.make_async_copy(a1_ref, a1_hbm, out_sems.at[0]),
+            pltpu.make_async_copy(a2_ref, a2_hbm, out_sems.at[1]),
+        ]
+    )
     last[0].wait()
     x = mm(total.astype(BF), wp_ref[...]).astype(BF)
     x_ref[...] = x
+    outs += started([pltpu.make_async_copy(x_ref, x_hbm, out_sems.at[2])])
     slide_norm = normalize(x.astype(F32))[0].astype(BF)
     last[1].wait()
     qkv_ref[...] = mm(slide_norm, wq_ref[...]).astype(BF)
 
     width = HEADS * HD
-    outs = []
     for pair in range(HEADS // 2):
         j, t = pair // 2, 2 * (pair % 2)
         for tp in range(2):
@@ -210,65 +264,74 @@
             tmp_ref[:, at, lane : lane + 192] = rows[128 * block : 128 * block + 128].reshape(
                 8, 16, 192
             )
-        copy = pltpu.make_async_copy(tmp_ref.at[:, at, :], out_hbm.at[:, at, :], sems.at[14 + pair])
-        copy.start()
-        outs.append(copy)
-    for copy in outs:
-        copy.wait()
-
-
-def between_kernel(gate_ref, up_ref, wq_ref, a1_ref, a2_ref, wqp_ref):
-    gate = gate_ref[...]
-    sig = jax.nn.sigmoid(gate)
-    a1_ref[...] = up_ref[...] * sig * (1.0 + gate * (1.0 - sig))
-    a2_ref[...] = gate * sig
-    width = HEADS * HD
-    zeros = jnp.zeros((width, HD), BF)
-    for h in range(HEADS):
-        for part in range(3):
-            wqp_ref[:, 192 * h + HD * part : 192 * h + HD * part + HD] = wq_ref[
-                :, part * width + h * HD : part * width + h * HD + HD
+        outs += started(
+            [
+                pltpu.make_async_copy(
+                    tmp_ref.at[:, at, :], out_hbm.at[:, at, :], out_sems.at[3 + pair]
+                )
             ]
-        wqp_ref[:, 192 * h + 144 : 192 * h + 192] = zeros
+        )
+    finish(outs)
 
 
 def backward_mlp_kernel(
     ret_ref,
+    pos_hbm,
+    feat_hbm,
+    x_hbm,
+    a1_hbm,
+    a2_hbm,
+    gate_hbm,
+    up_hbm,
+    down_hbm,
+    proj_hbm,
+    qkvw_hbm,
+    out_ref,
     pos_ref,
     feat_ref,
     x_ref,
     a1_ref,
     a2_ref,
-    wqp_ref,
-    gate_hbm,
-    up_hbm,
-    down_hbm,
-    proj_hbm,
-    out_ref,
     wg_ref,
     wu_ref,
     wd_ref,
     wp_ref,
-    got_ref,
+    wq_ref,
+    dqkv_ref,
     grad_ref,
     sems,
 ):
-    ff = a1_ref.shape[1]
+    ff = gate_hbm.shape[1]
     step = 512
     chunks = ff // step
-    first = pltpu.make_async_copy(proj_hbm, wp_ref, sems.at[3 * chunks])
-    first.start()
+    pairs = (
+        (pos_hbm, pos_ref),
+        (x_hbm, x_ref),
+        (qkvw_hbm, wq_ref),
+        (proj_hbm, wp_ref),
+        (a1_hbm, a1_ref),
+        (a2_hbm, a2_ref),
+        (feat_hbm, feat_ref),
+    )
+    first = started(
+        [
+            pltpu.make_async_copy(here, there, sems.at[3 * chunks + i])
+            for i, (here, there) in enumerate(pairs)
+        ]
+    )
     waits = []
     for c in range(chunks):
         at = pl.ds(c * step, step)
-        trio = [
-            pltpu.make_async_copy(down_hbm.at[at, :], wd_ref.at[at, :], sems.at[3 * c]),
-            pltpu.make_async_copy(gate_hbm.at[:, at], wg_ref.at[:, at], sems.at[3 * c + 1]),
-            pltpu.make_async_copy(up_hbm.at[:, at], wu_ref.at[:, at], sems.at[3 * c + 2]),
-        ]
-        for copy in trio:
-            copy.start()
-        waits.append(trio)
+        waits.append(
+            started(
+                [
+                    pltpu.make_async_copy(down_hbm.at[at, :], wd_ref.at[at, :], sems.at[3 * c]),
+                    pltpu.make_async_copy(gate_hbm.at[:, at], wg_ref.at[:, at], sems.at[3 * c + 1]),
+                    pltpu.make_async_copy(up_hbm.at[:, at], wu_ref.at[:, at], sems.at[3 * c + 2]),
+                ]
+            )
+        )
+    first[0].wait()
     me = lax.axis_index("seq") * 4 + lax.axis_index("tile")
     brow = pos_ref[pl.ds(me, 1), :] >> 9
     n = brow.shape[1]
@@ -280,6 +343,7 @@
     seat = iota((2 * n, BLK), 1)
     want = (((seat >> 4) & 7) * 4 + (seat >> 7)) * SLOTS + (seat & 7) + 4096 * ((seat >> 3) & 1)
     picker = jnp.where(code == want, 1.0, 0.0).astype(BF)
+    width = HEADS * HD
     for pair in range(HEADS // 2):
         j, t = pair // 2, 2 * (pair % 2)
         tile = ret_ref[:, 16 * pair : 16 * pair + 16, :].reshape(128, 768)
@@ -289,29 +353,39 @@
         got = mm(picker, stacked).astype(BF)
         for tp in range(2):
             h = 4 * (t + tp) + j
-            got_ref[:, 192 * h : 192 * h + 192] = got[n * tp : n * tp + n]
-            grad_ref[:, h * HD : h * HD + HD] = got[n * tp : n * tp + n, 144:192]
-    dnorm = mm(got_ref[...], wqp_ref[...], NT)
+            mine = got[n * tp : n * tp + n]
+            for part in range(3):
+                dqkv_ref[:, part * width + h * HD : part * width + h * HD + HD] = mine[
+                    :, HD * part : HD * part + HD
+                ]
+            grad_ref[:, h * HD : h * HD + HD] = mine[:, 144:192]
+    first[1].wait()
     slide_norm, slide_inv = normalize(x_ref[...].astype(F32))
+    first[2].wait()
+    dnorm = mm(dqkv_ref[...], wq_ref[...], NT)
     dslide = (grad_ref[...].astype(F32) + norm_back(slide_norm, slide_inv, dnorm)).astype(BF)
-    first.wait()
+    first[3].wait()
     dembed = mm(dslide, wp_ref[...], NT).astype(BF)
+    finish(first[4:])
+    normed, inv = normalize(feat_ref[...].astype(F32))
     dfeat = jnp.zeros(feat_ref.shape, F32)
     for c in range(chunks):
         at = slice(c * step, c * step + step)
         waits[c][0].wait()
         dhidden = mm(dembed, wd_ref[at, :], NT)
-        dgate = (dhidden * a1_ref[:, at]).astype(BF)
-        dup = (dhidden * a2_ref[:, at]).astype(BF)
+        dgate = (dhidden * a1_ref[:, at].astype(F32)).astype(BF)
+        dup = (dhidden * a2_ref[:, at].astype(F32)).astype(BF)
         waits[c][1].wait()
         dfeat = dfeat + mm(dgate, wg_ref[:, at], NT)
         waits[c][2].wait()
         dfeat = dfeat + mm(dup, wu_ref[:, at], NT)
-    normed, inv = normalize(feat_ref[...].astype(F32))
     out_ref[...] = (dembed.astype(F32) + norm_back(normed, inv, dfeat)).astype(BF)
 
 
-def place_kernel(shift_ref, recv_ref, tab_ref, _after_ref, y_ref, yt_ref, y2_ref):
+def place_kernel(shift_ref, recv_ref, tab_hbm, y_ref, yt_ref, y2_ref, tab_ref, sem):
+    copy = pltpu.make_async_copy(tab_hbm, tab_ref, sem)
+    copy.start()
+    copy.wait()
     _, base, part = offsets(shift_ref)
     o2 = pl.multiple_of(base + 32 * part, 32)
     for d in range(4):
@@ -382,24 +456,37 @@
     a3_ref,
     u_ref,
     l_ref,
-    g0_ref,
-    g1_ref,
-    g2_ref,
-    g3_ref,
-    so0_ref,
-    so1_ref,
-    so2_ref,
-    so3_ref,
+    g0_hbm,
+    g1_hbm,
+    g2_hbm,
+    g3_hbm,
+    so0_hbm,
+    so1_hbm,
+    so2_hbm,
+    so3_hbm,
     gs_ref,
     ds_ref,
     own_ref,
-    send_ref,
+    send1_ref,
+    send2_ref,
+    send3_ref,
     dq_ref,
     e2_ref,
     m2_ref,
     usum_ref,
     lsum_ref,
+    g_ref,
+    so_ref,
+    sems,
+    so_sems,
 ):
+    grads = started(
+        [
+            pltpu.make_async_copy(g, g_ref.at[d], sems.at[d])
+            for d, g in enumerate((g0_hbm, g1_hbm, g2_hbm, g3_hbm))
+        ]
+    )
+    outs = []
     _, base, part = offsets(shift_ref)
     base = pl.multiple_of(base, 128)
     y2 = jnp.concatenate([a0_ref[...], a1_ref[...], a2_ref[...], a3_ref[...]], axis=0)
@@ -420,7 +507,6 @@
     gs2 = jnp.zeros((48, 128), F32)
     ds2 = jnp.zeros((8, 128), F32)
     for d in range(4):
-        grad_ref = (g0_ref, g1_ref, g2_ref, g3_ref)[d]
         here = lane == part
         shift = 32 * (part - d)
         usum_ref[...] = u_ref[d]
@@ -429,8 +515,11 @@
         lsum_ref[:, pl.ds(base, 128)] += jnp.where(here, turned(l2w, shift), 0.0)[0:1]
         inv = 1.0 / lsum_ref[...]
         att = usum_ref[...] * inv
-        (so0_ref, so1_ref, so2_ref, so3_ref)[d][...] = (yt_ref[d, 144:192, :].astype(F32) + att).astype(BF)
-        gs = (grad_ref[...].astype(F32) * inv).astype(BF)
+        so_ref[d] = (yt_ref[d, 144:192, :].astype(F32) + att).astype(BF)
+        so = (so0_hbm, so1_hbm, so2_hbm, so3_hbm)[d]
+        outs += started([pltpu.make_async_copy(so_ref.at[d], so, so_sems.at[d])])
+        grads[d].wait()
+        gs = (g_ref[d].astype(F32) * inv).astype(BF)
         gs_ref[d] = gs
         ds_ref[d] = jnp.sum(gs.astype(F32) * att, axis=0, keepdims=True)
         gs_wide = gs_ref[d, :, pl.ds(base, 128)].astype(F32)
@@ -445,8 +534,9 @@
     dv = mm(gs2, e2_ref[...], NT)
     dkv = jnp.concatenate([dk, dv], axis=0)
     own_ref[...] = dkv[:, 0:128]
-    for e in range(3):
-        send_ref[e] = dkv[:, 128 * e + 128 : 128 * e + 256].astype(BF)
+    for e, send_ref in enumerate((send1_ref, send2_ref, send3_ref)):
+        send_ref[...] = dkv[:, 128 * e + 128 : 128 * e + 256].astype(BF)
+    finish(outs)
 
 
 def dscores(values, gs, ds, m_load, store):
@@ -497,16 +587,26 @@
     r1_ref,
     r2_ref,
     r3_ref,
-    g0_ref,
-    g1_ref,
-    g2_ref,
-    g3_ref,
-    tab_ref,
+    g0_hbm,
+    g1_hbm,
+    g2_hbm,
+    g3_hbm,
+    tab_hbm,
     out_hbm,
     sum_ref,
     out_ref,
+    g_ref,
+    tab_ref,
     sems,
+    in_sems,
 ):
+    loads = started(
+        [pltpu.make_async_copy(tab_hbm, tab_ref, in_sems.at[4])]
+        + [
+            pltpu.make_async_copy(g, g_ref.at[d], in_sems.at[d])
+            for d, g in enumerate((g0_hbm, g1_hbm, g2_hbm, g3_hbm))
+        ]
+    )
     _, base, part = offsets(shift_ref)
     base = pl.multiple_of(base, 128)
     dkv = (
@@ -519,29 +619,35 @@
     lane = iota((1, 128), 1) >> 5
     rows = tab_ref.shape[0]
     outs = []
+    finish(loads)
     for d in range(4):
-        grad_ref = (g0_ref, g1_ref, g2_ref, g3_ref)[d]
         sum_ref[...] = dall_ref[d]
         sum_ref[:, pl.ds(base, 128)] += jnp.where(
             lane == part, turned(extra, 32 * (part - d)), 0.0
         )
-        both = jnp.concatenate([sum_ref[...].astype(BF), grad_ref[...]], axis=0)
+        both = jnp.concatenate([sum_ref[...].astype(BF), g_ref[d]], axis=0)
         onehot = jnp.where(tab_ref[:, d : d + 1] == iota((rows, BLK), 1), 1.0, 0.0).astype(BF)
         out_ref[:, 192 * d : 192 * d + 192] = mm(onehot, both, NT).astype(BF)
         if d % 2:
             at = pl.ds(384 * (d // 2), 384)
-            copy = pltpu.make_async_copy(out_ref.at[:, at], out_hbm.at[:, at], sems.at[d // 2])
-            copy.start()
-            outs.append(copy)
-    for copy in outs:
-        copy.wait()
-
-
-def out_kernel(s0_ref, s1_ref, s2_ref, s3_ref, _after_ref, out_ref, tmp_ref):
+            outs += started(
+                [pltpu.make_async_copy(out_ref.at[:, at], out_hbm.at[:, at], sems.at[d // 2])]
+            )
+    finish(outs)
+
+
+def out_kernel(s0_hbm, s1_hbm, s2_hbm, s3_hbm, _after_hbm, out_ref, tmp_ref, sems):
     j = lax.axis_index("seq") & 3
-    for d in range(4):
-        at = pl.multiple_of((j ^ d) * HD, 16)
-        tmp_ref[pl.ds(at, HD), :] = (s0_ref, s1_ref, s2_ref, s3_ref)[d][...]
+    finish(
+        started(
+            [
+                pltpu.make_async_copy(
+                    so, tmp_ref.at[pl.ds(pl.multiple_of((j ^ d) * HD, 16), HD), :], sems.at[d]
+                )
+                for d, so in enumerate((s0_hbm, s1_hbm, s2_hbm, s3_hbm))
+            ]
+        )
+    )
     out_ref[...] = mm(tmp_ref[...], order_matrix(), NT).astype(BF)
 
 
@@ -578,47 +684,58 @@
             tiled=True,
         ).reshape(device_count * SLOTS, slide_width)
 
-    outgoing, x, gate_proj, up_proj = call(
+    stored = [
+        pltpu.VMEM((width, ff), BF),
+        pltpu.VMEM((width, ff), BF),
+        pltpu.VMEM((ff, width), BF),
+        pltpu.VMEM((width, slide_width), BF),
+        pltpu.VMEM((slide_width, 3 * slide_width), BF),
+    ]
+    dma = pltpu.SemaphoreType.DMA
+    outgoing, x, a1, a2 = call(
         forward_mlp_kernel,
-        [routed, ((rows, slide_width), BF), ((rows, ff), F32), ((rows, ff), F32)],
-        [
-            pltpu.VMEM((width, ff), BF),
-            pltpu.VMEM((width, ff), BF),
-            pltpu.VMEM((ff, width), BF),
-            pltpu.VMEM((width, slide_width), BF),
-            pltpu.VMEM((slide_width, 3 * slide_width), BF),
+        [routed, ((rows, slide_width), BF), ((rows, ff), BF), ((rows, ff), BF)],
+        [pltpu.VMEM((rows, width), BF), pltpu.VMEM((device_count, rows), I32)]
+        + stored
+        + [
+            pltpu.VMEM((rows, slide_width), BF),
+            pltpu.VMEM((rows, ff), BF),
+            pltpu.VMEM((rows, ff), BF),
             pltpu.VMEM((rows, 3 * slide_width), BF),
             pltpu.VMEM((2 * rows, 192), BF),
             pltpu.VMEM((BLK, 2 * rows), BF),
             pltpu.VMEM((8, 16 * SLOTS, slide_width), BF),
-            pltpu.SemaphoreType.DMA((14 + HEADS // 2,)),
+            dma((16,)),
+            dma((3 + HEADS // 2,)),
         ],
-        n_any=5,
-        n_any_out=1,
-        limit=34,
+        n_hbm=7,
+        n_hbm_out=4,
+        limit=48,
     )(tile_features, all_pos, *weights)
     arrived = exchange(outgoing)
 
-    grads = call(order_kernel, [((HD, BLK), BF)] * 4, [pltpu.VMEM((192, BLK), BF)])(
-        slide_output_gradient.T
-    )
+    grads = call(
+        order_kernel,
+        [((HD, BLK), BF)] * 4,
+        [pltpu.VMEM((192, BLK), BF), dma((4,))],
+        n_hbm_out=4,
+    )(slide_output_gradient.T)
     grads = [grads[0]] + [swap(grads[d], d, seq_count) for d in range(1, 4)]
+    slots = device_count * SLOTS
     table, table_col = call(
         table_kernel,
-        [((8, device_count * SLOTS), I32), ((device_count * SLOTS, 8), I32)],
+        [((8, slots), I32), ((slots, 8), I32)],
+        [pltpu.VMEM((8, slots), I32), pltpu.VMEM((slots, 8), I32), dma((2,))],
+        n_hbm_out=2,
     )(all_pos)
-
-    a1, a2, wqp = call(
-        between_kernel,
-        [((rows, ff), F32), ((rows, ff), F32), ((slide_width, 4 * slide_width), BF)],
-    )(gate_proj, up_proj, query_key_value_weight)
 
     y, yt, y2 = call(
         place_kernel,
         [((4, BLK, 192), BF), ((4, 192, BLK), BF), ((128, 192), BF)],
+        [pltpu.VMEM((8, slots), I32), dma],
         n_smem=1,
-        n_after=1,
-    )(dilation_shift, arrived, table, a1)
+        n_hbm=1,
+    )(dilation_shift, arrived, table)
     y2_in = [swap(y2, 4 * e, seq_count) for e in range(1, 4)]
     e0, m0, e1, m1, u, l = call(
         forward_kernel,
@@ -632,26 +749,27 @@
         ],
         n_smem=1,
     )(dilation_shift, y, yt)
-    *parts, gs, ds, own, send, dq2 = call(
+    *parts, gs, ds, own, send1, send2, send3, dq2 = call(
         wide_kernel,
         [((HD, BLK), BF)] * 4
-        + [
-            ((4, HD, BLK), BF),
-            ((4, 1, BLK), F32),
-            ((96, 128), F32),
-            ((3, 96, 128), BF),
-            ((HD, 128), F32),
-        ],
+        + [((4, HD, BLK), BF), ((4, 1, BLK), F32), ((96, 128), F32)]
+        + [((96, 128), BF)] * 3
+        + [((HD, 128), F32)],
         [
             pltpu.VMEM((BLK, 128), BF),
             pltpu.VMEM((BLK, 128), BF),
             pltpu.VMEM((HD, BLK), F32),
             pltpu.VMEM((1, BLK), F32),
+            pltpu.VMEM((4, HD, BLK), BF),
+            pltpu.VMEM((4, HD, BLK), BF),
+            dma((4,)),
+            dma((4,)),
         ],
         n_smem=1,
+        n_any=4,
+        n_hbm_out=4,
     )(dilation_shift, yt, y2, *y2_in, u, l, *grads)
-    back = [swap(send[e - 1], 4 * e, seq_count) for e in range(1, 4)]
-    parts = [parts[0]] + [swap(parts[d], d, seq_count) for d in range(1, 4)]
+    back = [swap(send, 4 * e, seq_count) for e, send in ((1, send1), (2, send2), (3, send3))]
     (dall,) = call(
         backward_kernel,
         [((4, 144, BLK), F32)],
@@ -660,43 +778,49 @@
     )(dilation_shift, y, yt, e0, m0, e1, m1, gs, ds)
     (returning,) = call(
         return_kernel,
-        [((device_count * SLOTS, slide_width), BF)],
+        [((slots, slide_width), BF)],
         [
             pltpu.VMEM((144, BLK), F32),
-            pltpu.VMEM((device_count * SLOTS, slide_width), BF),
-            pltpu.SemaphoreType.DMA((2,)),
+            pltpu.VMEM((slots, slide_width), BF),
+            pltpu.VMEM((4, HD, BLK), BF),
+            pltpu.VMEM((slots, 8), I32),
+            dma((2,)),
+            dma((5,)),
         ],
         n_smem=1,
-        n_any_out=1,
+        n_any=4,
+        n_hbm=1,
+        n_hbm_out=1,
         limit=6,
     )(dilation_shift, dall, own, dq2, *back, *grads, table_col)
     returned = exchange(returning)
+    parts = [parts[0]] + [swap(parts[d], d, seq_count) for d in range(1, 4)]
+
     (tile_grad,) = call(
         backward_mlp_kernel,
         [((rows, width), BF)],
         [
-            pltpu.VMEM((width, ff), BF),
-            pltpu.VMEM((width, ff), BF),
-            pltpu.VMEM((ff, width), BF),
-            pltpu.VMEM((width, slide_width), BF),
-            pltpu.VMEM((rows, 4 * slide_width), BF),
+            pltpu.VMEM((device_count, rows), I32),
+            pltpu.VMEM((rows, width), BF),
             pltpu.VMEM((rows, slide_width), BF),
-            pltpu.SemaphoreType.DMA((13,)),
+            pltpu.VMEM((rows, ff), BF),
+            pltpu.VMEM((rows, ff), BF),
+        ]
+        + stored
+        + [
+            pltpu.VMEM((rows, 3 * slide_width), BF),
+            pltpu.VMEM((rows, slide_width), BF),
+            dma((19,)),
         ],
+        n_hbm=10,
+        limit=48,
+    )(returned.reshape(8, 16 * SLOTS, slide_width), all_pos, tile_features, x, a1, a2, *weights)
+    (slide_out,) = call(
+        out_kernel,
+        [((192, BLK), BF)],
+        [pltpu.VMEM((192, BLK), BF), dma((4,))],
         n_any=4,
-        limit=32,
-    )(
-        returned.reshape(8, 16 * SLOTS, slide_width),
-        all_pos,
-        tile_features,
-        x,
-        a1,
-        a2,
-        wqp,
-        *weights[:4],
-    )
-    (slide_out,) = call(
-        out_kernel, [((192, BLK), BF)], [pltpu.VMEM((192, BLK), BF)], n_after=1
+        n_hbm=1,
     )(*parts, tile_grad)
     return (slide_out.T, tile_grad)
 

time: 152 us -> 126 us (0.83)
  local copies, waits for them, and re-layouts: 36.9 us -> 0.04 us
  waiting for transfers between devices: 26.8 us -> 42.2 us
  Pallas kernels: 53.9 us -> 49.9 us
    unnamed x76 -> x16, local copies, waits for them, and re-layouts: 36.9 us -> 0.04 us
    all_to_all x2, waiting for transfers between devices: 26.7 us -> 42.2 us  [exchange(): lax.all_to_all(block.reshape(device_count, SLOTS, slide_width), ('seq', '...]
    pallas_call x11 -> x10, Pallas kernels: 53.9 us -> 49.9 us  [run(): pl.pallas_call(kernel, out_shape=shapes, in_specs=specs, out_specs=out_sp...]
  transfers between devices with their start and end apart: 14 -> 14, of which waited for: 2 -> 2; matrix products, arithmetic and copies ran while one was open for 0% -> 0% of each run, Pallas kernels for 23% -> 24%
where the time goes in v3:
time: 126 us; the launch traced here: 125 us
  Pallas kernels  49.9 us (40%)
  waiting for transfers between devices  42.2 us (33%)
  starting transfers between devices  31.9 us (25%)
    pallas_call x10, Pallas kernels, run(): pl.pallas_call(kernel, out_shape=shapes, in_specs=specs, out_specs=out_sp...  49.9 us
    all_to_all x2, waiting for transfers between devices, exchange(): lax.all_to_all(block.reshape(device_count, SLOTS, slide_width), ('seq', '...  42.2 us
    all_to_all x2, starting transfers between devices, exchange(): lax.all_to_all(block.reshape(device_count, SLOTS, slide_width), ('seq', '...  17.6 us
    ppermute x12, starting transfers between devices, swap(): return lax.ppermute(value, 'seq', [(i, i ^ distance) for i in range(count)])  14.2 us
  transfers between devices with their start and end apart: 14, of which 2 were waited for; matrix products, arithmetic and copies ran while one was open for 0% of the time, Pallas kernels for 24%

profile of v3, /device:TPU:1, one launch (start us, length us, event | category | flops | bytes accessed | tf_op | source)
XLA Modules:
  0.0 125.1 jit_solution(13498982765998139458)
XLA Ops:
  0.6 11.7 %shard_map.104 = (bf16[8,128,768]{2,1,0:T(8,128)(2,1)}, bf16[128,768]{1,0:T(8,128)(2,1)}, bf16[128,2048]{1,0:T(8,128)(2,1)}, bf16[128,2048]{1,0:T(8,128)(2,1)}) custom-call(bf16[128,1536]{1,0:T(8,128)(2,1)} %feat_hbm.3, s32[128,128]{1,0:T(8,128)} %bitcast.9, bf16[1536,2048]{1,0:T(8,128)(2,1)} %gate_hbm.3, bf16[1536,2048]{1,0:T(8,128)(2,1)} %up_hbm.3, ...), custom_call_target="tpu_custom_call" | custom-call | tf_op jit(solution)/shard_map/pallas_call | solution.py:65
  12.3 0.0 copy-start.2
  12.3 0.0 copy-start
  12.3 0.0 copy-start.4
  12.3 11.5 %all-to-all-start = ((bf16[128,8,768]{2,1,0:T(8,128)(2,1)}), bf16[128,8,768]{2,1,0:T(8,128)(2,1)S(1)}, u32[]{:S(2)}, u32[]{:S(2)}) async-start(bf16[128,8,768]{2,1,0:T(8,128)(2,1)} %bitcast.14), calls=%async_computation | async-start | bytes 3145728 | tf_op jit(solution)/shard_map/all_to_all | solution.py:679
  23.9 1.0 shard_map.108
  24.9 0.0 copy-start.1
  24.9 1.1 collective-permute-start.3
  26.0 0.8 collective-permute-start.4
  26.8 0.9 collective-permute-start.5
  27.7 1.7 %shard_map.105 = (s32[8,1024]{1,0:T(8,128)}, s32[1024,8]{1,0:T(8,128)}) custom-call(s32[128,128]{1,0:T(8,128)S(1)} %bitcast.11), custom_call_target="tpu_custom_call" | custom-call | tf_op jit(solution)/shard_map/pallas_call | solution.py:65
  29.5 19.7 %all-to-all-done = bf16[128,8,768]{2,1,0:T(8,128)(2,1)S(1)} async-done(((bf16[128,8,768]{2,1,0:T(8,128)(2,1)}), bf16[128,8,768]{2,1,0:T(8,128)(2,1)S(1)}, u32[]{:S(2)}, u32[]{:S(2)}) %all-to-all-start) | async-done | bytes 1572896 | tf_op jit(solution)/shard_map/all_to_all | solution.py:679
  49.2 2.7 %shard_map.106 = (bf16[4,512,192]{2,1,0:T(8,128)(2,1)S(1)}, bf16[4,192,512]{2,1,0:T(8,128)(2,1)S(1)}, bf16[128,192]{1,0:T(8,128)(2,1)S(1)}) custom-call(s32[2,16]{1,0:T(2,128)S(1)} %copy-done.4, bf16[1024,768]{1,0:T(8,128)(2,1)S(1)} %bitcast.7, s32[8,1024]{1,0:T(8,128)} %get-tuple-element.33.tab_hbm), custom_call_target="tpu_custom_call" | custom-call | tf_op jit(solution)/shard_map/pallas_call | solution.py:65
  52.0 0.1 collective-permute-start.2
  52.0 1.0 collective-permute-start.1
  53.0 0.0 collective-permute-done.3.g1_hbm
  53.0 3.2 %collective-permute-start = (bf16[128,192]{1,0:T(8,128)(2,1)S(1)}, bf16[128,192]{1,0:T(8,128)(2,1)S(1)}, u32[]{:S(2)}, u32[]{:S(2)}) collective-permute-start(bf16[128,192]{1,0:T(8,128)(2,1)S(1)} %get-tuple-element.35.a0_ref), channel_id=1, source_target_pairs={{0,16},{4,20},{8,24},{12,28},{16,0},{20,4},{24,8},{28,12},{32,48},... | collective-permute-start | bytes 147464 | tf_op jit(solution)/shard_map/ppermute | solution.py:655
  56.2 4.3 %shard_map.107 = (bf16[4,512,512]{2,1,0:T(8,128)(2,1)S(1)}, bf16[4,512,512]{2,1,0:T(8,128)(2,1)S(1)}, bf16[512,512]{1,0:T(8,128)(2,1)S(1)}, bf16[512,512]{1,0:T(...) custom-call(s32[2,16]{1,0:T(2,128)S(1)} %copy-done.4, ...), custom_call_target="tpu_custom_call" | custom-call | tf_op jit(solution)/shard_map/pallas_call | solution.py:65
  60.6 2.4 %shard_map.109 = (bf16[48,512]{1,0:T(8,128)(2,1)}, bf16[48,512]{1,0:T(8,128)(2,1)}, bf16[48,512]{1,0:T(8,128)(2,1)}, bf16[48,512]{1,0:T(8,128)(2,1)}, bf16[4,48,...) custom-call(s32[2,16]{1,0:T(2,128)S(1)} %copy-done.4, ...), custom_call_target="tpu_custom_call" | custom-call | tf_op jit(solution)/shard_map/pallas_call | solution.py:65
  63.0 0.3 collective-permute-start.9
  63.3 0.3 collective-permute-start.10
  63.6 3.6 %collective-permute-start.11 = (bf16[96,128]{1,0:T(8,128)(2,1)S(1)}, bf16[96,128]{1,0:T(8,128)(2,1)S(1)}, u32[]{:S(2)}, u32[]{:S(2)}) collective-permute-start(bf16[96,128]{1,0:T(8,128)(2,1)S(1)} %get-tuple-element.57), channel_id=1, source_target_pairs={{0,48},{4,52},{8,56},{12,60},{16,32},{20,36},{24,40},{28,44},{32,1... | collective-permute-start | bytes 73736 | tf_op jit(solution)/shard_map/ppermute | solution.py:655
  67.2 4.4 %shard_map.110.dall_ref = f32[4,144,512]{2,1,0:T(8,128)S(1)} custom-call(s32[2,16]{1,0:T(2,128)S(1)} %copy-done.4, bf16[4,512,192]{2,1,0:T(8,128)(2,1)S(1)} %get-tuple-element.36.y_ref, bf16[4,192,512]{2,1,0:T(8,128)(2,1)S(1)} %get-tuple-element.34.yt_ref, bf16[4,512,512]{2,1,0:T(8,128)(2,1)S(1)} %get-tuple-element.47.e0_ref, ...), custom_call_target="tpu_custom_call" | custom-call | tf_op jit(solution)/shard_map/pallas_call | solution.py:65
  71.7 4.3 %shard_map.111 = bf16[1024,768]{1,0:T(8,128)(2,1)} custom-call(s32[2,16]{1,0:T(2,128)S(1)} %copy-done.4, f32[4,144,512]{2,1,0:T(8,128)S(1)} %shard_map.110.dall_ref, f32[96,128]{1,0:T(8,128)S(1)} %get-tuple-element.53.own_ref, f32[48,128]{1,0:T(8,128)S(1)} %get-tuple-element.54.dq_ref, bf16[96,128]{1,0:T(8,128)(2,1)S(1)} %collective-permute-done.9.r1_ref, ...), custom_call_target="tpu_custom_call" | custom-call | tf_op jit(solution)/shard_map/pallas_call | solution.py:65
  76.0 0.0 copy-start.7
  76.0 6.1 %all-to-all-start.1 = ((bf16[128,8,768]{2,1,0:T(8,128)(2,1)}), bf16[128,8,768]{2,1,0:T(8,128)(2,1)S(1)}, u32[]{:S(2)}, u32[]{:S(2)}) async-start(bf16[128,8,768]{2,1,0:T(8,128)(2,1)} %bitcast.13), calls=%async_computation.1 | async-start | bytes 3145728 | tf_op jit(solution)/shard_map/all_to_all | solution.py:679
  82.2 1.1 collective-permute-start.6
  83.3 0.8 collective-permute-start.7
  84.1 0.9 collective-permute-start.8
  85.1 22.5 %all-to-all-done.1 = bf16[128,8,768]{2,1,0:T(8,128)(2,1)S(1)} async-done(((bf16[128,8,768]{2,1,0:T(8,128)(2,1)}), bf16[128,8,768]{2,1,0:T(8,128)(2,1)S(1)}, u32[]{:S(2)}, u32[]{:S(2)}) %all-to-all-start.1) | async-done | bytes 1572896 | tf_op jit(solution)/shard_map/all_to_all | solution.py:679
  107.6 16.0 %shard_map.112._after_hbm = bf16[128,1536]{1,0:T(8,128)(2,1)} custom-call(bf16[8,128,768]{2,1,0:T(8,128)(2,1)S(1)} %bitcast.8, s32[128,128]{1,0:T(8,128)} %bitcast.10, bf16[128,1536]{1,0:T(8,128)(2,1)} %feat_hbm.3, bf16[128,768]{1,0:T(8,128)(2,1)} %get-tuple-element.59.x_hbm, bf16[128,2048]{1,0:T(8,128)(2,1)} %get-tuple-element.60.a1_hbm, ...), custom_call_target="tpu_custom_call" | custom-call | tf_op jit(solution)/shard_map/pallas_call | solution.py:65
  123.6 1.4 %shard_map.113 = bf16[192,512]{1,0:T(8,128)(2,1)} custom-call(bf16[48,512]{1,0:T(8,128)(2,1)S(1)} %copy-done.3, bf16[48,512]{1,0:T(8,128)(2,1)S(1)} %collective-permute-done.6.s1_hbm, bf16[48,512]{1,0:T(8,128)(2,1)S(1)} %collective-permute-done.7.s2_hbm, bf16[48,512]{1,0:T(8,128)(2,1)S(1)} %collective-permute-done.8.s3_hbm, ...), custom_call_target="tpu_custom_call" | custom-call | tf_op jit(solution)/shard_map/pallas_call | solution.py:65
  (22 shorter events, 0.1 us)
Async XLA Ops:
  12.3 11.6 %copy-start.2 = (bf16[512,192]{0,1:T(8,128)(2,1)S(1)}, bf16[512,192]{0,1:T(8,128)(2,1)}, u32[]{:S(2)}) copy-start(bf16[512,192]{0,1:T(8,128)(2,1)} %param.17) | copy-start | bytes 589828
  12.3 15.4 %copy-start = (s32[16384]{0:T(1024)S(1)}, s32[16384]{0:T(1024)}, u32[]{:S(2)}) copy-start(s32[16384]{0:T(1024)} %param.15) | copy-start | bytes 196612
  12.3 36.9 %copy-start.4 = (s32[2,16]{1,0:T(2,128)S(1)}, s32[2,16]{1,0:T(2,128)}, u32[]{:S(2)}) copy-start(s32[2,16]{1,0:T(2,128)} %shift_ref.9) | copy-start | bytes 388
  12.3 36.9 %all-to-all-start = ((bf16[128,8,768]{2,1,0:T(8,128)(2,1)}), bf16[128,8,768]{2,1,0:T(8,128)(2,1)S(1)}, u32[]{:S(2)}, u32[]{:S(2)}) async-start(bf16[128,8,768]{2,1,0:T(8,128)(2,1)} %bitcast.14), calls=%async_computation | async-start | bytes 3145728 | tf_op jit(solution)/shard_map/all_to_all | solution.py:679
  24.9 35.7 %copy-start.1 = (bf16[48,512]{1,0:T(8,128)(2,1)S(1)}, bf16[48,512]{1,0:T(8,128)(2,1)}, u32[]{:S(2)}) copy-start(bf16[48,512]{1,0:T(8,128)(2,1)} %get-tuple-element.39.g0_hbm) | copy-start | bytes 147460
  24.9 28.2 %collective-permute-start.3 = (bf16[48,512]{1,0:T(8,128)(2,1)}, bf16[48,512]{1,0:T(8,128)(2,1)S(1)}, u32[]{:S(2)}, u32[]{:S(2)}) collective-permute-start(bf16[48,512]{1,0:T(8,128)(2,1)} %get-tuple-element.40), channel_id=1, source_target_pairs={{0,4},{4,0},{8,12},{12,8},{16,20},{20,16},{24,28},{28,24},{32,36},... | collective-permute-start | bytes 147464 | tf_op jit(solution)/shard_map/ppermute | solution.py:655
  26.0 34.5 %collective-permute-start.4 = (bf16[48,512]{1,0:T(8,128)(2,1)}, bf16[48,512]{1,0:T(8,128)(2,1)S(1)}, u32[]{:S(2)}, u32[]{:S(2)}) collective-permute-start(bf16[48,512]{1,0:T(8,128)(2,1)} %get-tuple-element.41), channel_id=1, source_target_pairs={{0,8},{4,12},{8,0},{12,4},{16,24},{20,28},{24,16},{28,20},{32,40},... | collective-permute-start | bytes 147464 | tf_op jit(solution)/shard_map/ppermute | solution.py:655
  26.8 33.7 %collective-permute-start.5 = (bf16[48,512]{1,0:T(8,128)(2,1)}, bf16[48,512]{1,0:T(8,128)(2,1)S(1)}, u32[]{:S(2)}, u32[]{:S(2)}) collective-permute-start(bf16[48,512]{1,0:T(8,128)(2,1)} %get-tuple-element.42), channel_id=1, source_target_pairs={{0,12},{4,8},{8,4},{12,0},{16,28},{20,24},{24,20},{28,16},{32,44},... | collective-permute-start | bytes 147464 | tf_op jit(solution)/shard_map/ppermute | solution.py:655
  52.0 8.6 %collective-permute-start.2 = (bf16[128,192]{1,0:T(8,128)(2,1)S(1)}, bf16[128,192]{1,0:T(8,128)(2,1)S(1)}, u32[]{:S(2)}, u32[]{:S(2)}) collective-permute-start(bf16[128,192]{1,0:T(8,128)(2,1)S(1)} %get-tuple-element.35.a0_ref), channel_id=1, source_target_pairs={{0,48},{4,52},{8,56},{12,60},{16,32},{20,36},{24,40},{28,44},{32,1... | collective-permute-start | bytes 147464 | tf_op jit(solution)/shard_map/ppermute | solution.py:655
  52.0 8.5 %collective-permute-start.1 = (bf16[128,192]{1,0:T(8,128)(2,1)S(1)}, bf16[128,192]{1,0:T(8,128)(2,1)S(1)}, u32[]{:S(2)}, u32[]{:S(2)}) collective-permute-start(bf16[128,192]{1,0:T(8,128)(2,1)S(1)} %get-tuple-element.35.a0_ref), channel_id=1, source_target_pairs={{0,32},{4,36},{8,40},{12,44},{16,48},{20,52},{24,56},{28,60},{32,0... | collective-permute-start | bytes 147464 | tf_op jit(solution)/shard_map/ppermute | solution.py:655
  53.0 7.5 %collective-permute-start = (bf16[128,192]{1,0:T(8,128)(2,1)S(1)}, bf16[128,192]{1,0:T(8,128)(2,1)S(1)}, u32[]{:S(2)}, u32[]{:S(2)}) collective-permute-start(bf16[128,192]{1,0:T(8,128)(2,1)S(1)} %get-tuple-element.35.a0_ref), channel_id=1, source_target_pairs={{0,16},{4,20},{8,24},{12,28},{16,0},{20,4},{24,8},{28,12},{32,48},... | collective-permute-start | bytes 147464 | tf_op jit(solution)/shard_map/ppermute | solution.py:655
  63.0 8.7 %collective-permute-start.9 = (bf16[96,128]{1,0:T(8,128)(2,1)S(1)}, bf16[96,128]{1,0:T(8,128)(2,1)S(1)}, u32[]{:S(2)}, u32[]{:S(2)}) collective-permute-start(bf16[96,128]{1,0:T(8,128)(2,1)S(1)} %get-tuple-element.55), channel_id=1, source_target_pairs={{0,16},{4,20},{8,24},{12,28},{16,0},{20,4},{24,8},{28,12},{32,48},... | collective-permute-start | bytes 73736 | tf_op jit(solution)/shard_map/ppermute | solution.py:655
  63.3 8.4 %collective-permute-start.10 = (bf16[96,128]{1,0:T(8,128)(2,1)S(1)}, bf16[96,128]{1,0:T(8,128)(2,1)S(1)}, u32[]{:S(2)}, u32[]{:S(2)}) collective-permute-start(bf16[96,128]{1,0:T(8,128)(2,1)S(1)} %get-tuple-element.56), channel_id=1, source_target_pairs={{0,32},{4,36},{8,40},{12,44},{16,48},{20,52},{24,56},{28,60},{32,0... | collective-permute-start | bytes 73736 | tf_op jit(solution)/shard_map/ppermute | solution.py:655
  63.6 8.0 %collective-permute-start.11 = (bf16[96,128]{1,0:T(8,128)(2,1)S(1)}, bf16[96,128]{1,0:T(8,128)(2,1)S(1)}, u32[]{:S(2)}, u32[]{:S(2)}) collective-permute-start(bf16[96,128]{1,0:T(8,128)(2,1)S(1)} %get-tuple-element.57), channel_id=1, source_target_pairs={{0,48},{4,52},{8,56},{12,60},{16,32},{20,36},{24,40},{28,44},{32,1... | collective-permute-start | bytes 73736 | tf_op jit(solution)/shard_map/ppermute | solution.py:655
  76.0 6.2 %copy-start.7 = (bf16[48,512]{1,0:T(8,128)(2,1)S(1)}, bf16[48,512]{1,0:T(8,128)(2,1)}, u32[]{:S(2)}) copy-start(bf16[48,512]{1,0:T(8,128)(2,1)} %get-tuple-element.44) | copy-start | bytes 147460
  76.0 7.3 %copy-start.6 = (bf16[48,512]{1,0:T(8,128)(2,1)S(1)}, bf16[48,512]{1,0:T(8,128)(2,1)}, u32[]{:S(2)}) copy-start(bf16[48,512]{1,0:T(8,128)(2,1)} %get-tuple-element.45) | copy-start | bytes 147460
  76.0 8.1 %copy-start.5 = (bf16[48,512]{1,0:T(8,128)(2,1)S(1)}, bf16[48,512]{1,0:T(8,128)(2,1)}, u32[]{:S(2)}) copy-start(bf16[48,512]{1,0:T(8,128)(2,1)} %get-tuple-element.46) | copy-start | bytes 147460
  76.0 31.5 %all-to-all-start.1 = ((bf16[128,8,768]{2,1,0:T(8,128)(2,1)}), bf16[128,8,768]{2,1,0:T(8,128)(2,1)S(1)}, u32[]{:S(2)}, u32[]{:S(2)}) async-start(bf16[128,8,768]{2,1,0:T(8,128)(2,1)} %bitcast.13), calls=%async_computation.1 | async-start | bytes 3145728 | tf_op jit(solution)/shard_map/all_to_all | solution.py:679
  82.2 41.3 %collective-permute-start.6 = (bf16[48,512]{1,0:T(8,128)(2,1)S(1)}, bf16[48,512]{1,0:T(8,128)(2,1)S(1)}, u32[]{:S(2)}, u32[]{:S(2)}) collective-permute-start(bf16[48,512]{1,0:T(8,128)(2,1)S(1)} %copy-done.7), channel_id=1, source_target_pairs={{0,4},{4,0},{8,12},{12,8},{16,20},{20,16},{24,28},{28,24},{32,36},... | collective-permute-start | bytes 147464 | tf_op jit(solution)/shard_map/ppermute | solution.py:655
  83.3 40.2 %collective-permute-start.7 = (bf16[48,512]{1,0:T(8,128)(2,1)S(1)}, bf16[48,512]{1,0:T(8,128)(2,1)S(1)}, u32[]{:S(2)}, u32[]{:S(2)}) collective-permute-start(bf16[48,512]{1,0:T(8,128)(2,1)S(1)} %copy-done.6), channel_id=1, source_target_pairs={{0,8},{4,12},{8,0},{12,4},{16,24},{20,28},{24,16},{28,20},{32,40},... | collective-permute-start | bytes 147464 | tf_op jit(solution)/shard_map/ppermute | solution.py:655
  84.1 39.4 %collective-permute-start.8 = (bf16[48,512]{1,0:T(8,128)(2,1)S(1)}, bf16[48,512]{1,0:T(8,128)(2,1)S(1)}, u32[]{:S(2)}, u32[]{:S(2)}) collective-permute-start(bf16[48,512]{1,0:T(8,128)(2,1)S(1)} %copy-done.5), channel_id=1, source_target_pairs={{0,12},{4,8},{8,4},{12,0},{16,28},{20,24},{24,20},{28,16},{32,44},... | collective-permute-start | bytes 147464 | tf_op jit(solution)/shard_map/ppermute | solution.py:655
  107.6 16.0 %copy-start.3 = (bf16[48,512]{1,0:T(8,128)(2,1)S(1)}, bf16[48,512]{1,0:T(8,128)(2,1)}, u32[]{:S(2)}) copy-start(bf16[48,512]{1,0:T(8,128)(2,1)} %get-tuple-element.43.s0_hbm) | copy-start | bytes 147460

commit v4 on v3

--- a/solution.py
+++ b/solution.py
@@ -1,3 +1,5 @@
+import functools
+
 import jax
 import jax.numpy as jnp
 from jax import lax
@@ -85,19 +87,11 @@
         copy.wait()
 
 
-def order_kernel(grad_ref, g0_hbm, g1_hbm, g2_hbm, g3_hbm, tmp_ref, sems):
+def order_kernel(grad_ref, g0_ref, g1_ref, g2_ref, g3_ref, tmp_ref):
     j = lax.axis_index("seq") & 3
     tmp_ref[...] = mm(grad_ref[...], order_matrix()).astype(BF)
-    finish(
-        started(
-            [
-                pltpu.make_async_copy(
-                    tmp_ref.at[pl.ds(pl.multiple_of((j ^ d) * HD, 16), HD), :], out, sems.at[d]
-                )
-                for d, out in enumerate((g0_hbm, g1_hbm, g2_hbm, g3_hbm))
-            ]
-        )
-    )
+    for d, out_ref in enumerate((g0_ref, g1_ref, g2_ref, g3_ref)):
+        out_ref[...] = tmp_ref[pl.ds(pl.multiple_of((j ^ d) * HD, 16), HD), :]
 
 
 def offsets(shift_ref):
@@ -107,7 +101,7 @@
     return (o1 * 128, (o2 & 3) * 128, o2 >> 2)
 
 
-def table_kernel(pos_ref, row_hbm, col_hbm, row_ref, col_ref, sems):
+def table_kernel(pos_ref, row_ref, col_ref):
     s = lax.axis_index("seq")
     pos = pos_ref[...].T
     n = pos.shape[0]
@@ -136,14 +130,6 @@
     table = jnp.concatenate(rows + rows, axis=0) - 1.0
     row_ref[...] = table.astype(I32)
     col_ref[...] = table.T.astype(I32)
-    finish(
-        started(
-            [
-                pltpu.make_async_copy(row_ref, row_hbm, sems.at[0]),
-                pltpu.make_async_copy(col_ref, col_hbm, sems.at[1]),
-            ]
-        )
-    )
 
 
 def forward_mlp_kernel(
@@ -274,6 +260,72 @@
     finish(outs)
 
 
+def turn_steps(shapes):
+    steps = []
+    for which, (rows, columns) in enumerate(shapes):
+        band = 384 if columns == 2048 else 512 if columns == 1536 else 256 if columns == 2304 else 768
+        steps += [(which, at, band) for at in range(0, rows, band)]
+    return steps
+
+
+def turn_kernel(shapes, *refs):
+    count = len(shapes)
+    given = refs[:count]
+    made = refs[count + 1 : 2 * count + 1]
+    in_ref, out_ref, in_sems, out_sems = refs[2 * count + 1 :]
+    steps = turn_steps(shapes)
+
+    def load(i):
+        which, at, band = steps[i]
+        columns = shapes[which][1]
+        return pltpu.make_async_copy(
+            given[which].at[pl.ds(at, band), :],
+            in_ref.at[i % 2, pl.ds(0, band), pl.ds(0, columns)],
+            in_sems.at[i % 2],
+        )
+
+    def store(i):
+        which, at, band = steps[i]
+        columns = shapes[which][1]
+        return pltpu.make_async_copy(
+            out_ref.at[i % 2, pl.ds(0, columns), pl.ds(0, band)],
+            made[which].at[:, pl.ds(at, band)],
+            out_sems.at[i % 2],
+        )
+
+    load(0).start()
+    for i, (which, _, band) in enumerate(steps):
+        columns = shapes[which][1]
+        if i + 1 < len(steps):
+            load(i + 1).start()
+        load(i).wait()
+        if i >= 2:
+            store(i - 2).wait()
+        out_ref[i % 2, 0:columns, 0:band] = in_ref[i % 2, 0:band, 0:columns].T
+        store(i).start()
+    for i in range(max(len(steps) - 2, 0), len(steps)):
+        store(i).wait()
+
+
+def turned_weights(weights, after):
+    shapes = [w.shape for w in weights]
+    bands = [band for _, _, band in turn_steps(shapes)]
+    widest = max(columns for _, columns in shapes)
+    return call(
+        functools.partial(turn_kernel, shapes),
+        [((columns, rows), BF) for rows, columns in shapes],
+        [
+            pltpu.VMEM((2, max(bands), widest), BF),
+            pltpu.VMEM((2, widest, max(bands)), BF),
+            pltpu.SemaphoreType.DMA((2,)),
+            pltpu.SemaphoreType.DMA((2,)),
+        ],
+        n_hbm=len(shapes) + 1,
+        n_hbm_out=len(shapes),
+        limit=20,
+    )(*weights, after)
+
+
 def backward_mlp_kernel(
     ret_ref,
     pos_hbm,
@@ -301,9 +353,9 @@
     grad_ref,
     sems,
 ):
-    ff = gate_hbm.shape[1]
-    step = 512
-    chunks = ff // step
+    ff = gate_hbm.shape[0]
+    cuts = [(at, 512) for at in range(0, ff - 512, 512)] + [(ff - 512, 256), (ff - 256, 256)]
+    chunks = len(cuts)
     pairs = (
         (pos_hbm, pos_ref),
         (x_hbm, x_ref),
@@ -320,14 +372,14 @@
         ]
     )
     waits = []
-    for c in range(chunks):
-        at = pl.ds(c * step, step)
+    for c, (start, size) in enumerate(cuts):
+        at = pl.ds(start, size)
         waits.append(
             started(
                 [
-                    pltpu.make_async_copy(down_hbm.at[at, :], wd_ref.at[at, :], sems.at[3 * c]),
-                    pltpu.make_async_copy(gate_hbm.at[:, at], wg_ref.at[:, at], sems.at[3 * c + 1]),
-                    pltpu.make_async_copy(up_hbm.at[:, at], wu_ref.at[:, at], sems.at[3 * c + 2]),
+                    pltpu.make_async_copy(down_hbm.at[:, at], wd_ref.at[:, at], sems.at[3 * c]),
+                    pltpu.make_async_copy(gate_hbm.at[at, :], wg_ref.at[at, :], sems.at[3 * c + 1]),
+                    pltpu.make_async_copy(up_hbm.at[at, :], wu_ref.at[at, :], sems.at[3 * c + 2]),
                 ]
             )
         )
@@ -362,30 +414,27 @@
     first[1].wait()
     slide_norm, slide_inv = normalize(x_ref[...].astype(F32))
     first[2].wait()
-    dnorm = mm(dqkv_ref[...], wq_ref[...], NT)
+    dnorm = mm(dqkv_ref[...], wq_ref[...])
     dslide = (grad_ref[...].astype(F32) + norm_back(slide_norm, slide_inv, dnorm)).astype(BF)
     first[3].wait()
-    dembed = mm(dslide, wp_ref[...], NT).astype(BF)
+    dembed = mm(dslide, wp_ref[...]).astype(BF)
     finish(first[4:])
     normed, inv = normalize(feat_ref[...].astype(F32))
     dfeat = jnp.zeros(feat_ref.shape, F32)
-    for c in range(chunks):
-        at = slice(c * step, c * step + step)
+    for c, (start, size) in enumerate(cuts):
+        at = slice(start, start + size)
         waits[c][0].wait()
-        dhidden = mm(dembed, wd_ref[at, :], NT)
+        dhidden = mm(dembed, wd_ref[:, at])
         dgate = (dhidden * a1_ref[:, at].astype(F32)).astype(BF)
         dup = (dhidden * a2_ref[:, at].astype(F32)).astype(BF)
         waits[c][1].wait()
-        dfeat = dfeat + mm(dgate, wg_ref[:, at], NT)
+        dfeat = dfeat + mm(dgate, wg_ref[at, :])
         waits[c][2].wait()
-        dfeat = dfeat + mm(dup, wu_ref[:, at], NT)
+        dfeat = dfeat + mm(dup, wu_ref[at, :])
     out_ref[...] = (dembed.astype(F32) + norm_back(normed, inv, dfeat)).astype(BF)
 
 
-def place_kernel(shift_ref, recv_ref, tab_hbm, y_ref, yt_ref, y2_ref, tab_ref, sem):
-    copy = pltpu.make_async_copy(tab_hbm, tab_ref, sem)
-    copy.start()
-    copy.wait()
+def place_kernel(shift_ref, recv_ref, tab_ref, _after_hbm, y_ref, yt_ref, y2_ref):
     _, base, part = offsets(shift_ref)
     o2 = pl.multiple_of(base + 32 * part, 32)
     for d in range(4):
@@ -456,10 +505,10 @@
     a3_ref,
     u_ref,
     l_ref,
-    g0_hbm,
-    g1_hbm,
-    g2_hbm,
-    g3_hbm,
+    g0_ref,
+    g1_ref,
+    g2_ref,
+    g3_ref,
     so0_hbm,
     so1_hbm,
     so2_hbm,
@@ -475,17 +524,9 @@
     m2_ref,
     usum_ref,
     lsum_ref,
-    g_ref,
     so_ref,
-    sems,
     so_sems,
 ):
-    grads = started(
-        [
-            pltpu.make_async_copy(g, g_ref.at[d], sems.at[d])
-            for d, g in enumerate((g0_hbm, g1_hbm, g2_hbm, g3_hbm))
-        ]
-    )
     outs = []
     _, base, part = offsets(shift_ref)
     base = pl.multiple_of(base, 128)
@@ -518,8 +559,8 @@
         so_ref[d] = (yt_ref[d, 144:192, :].astype(F32) + att).astype(BF)
         so = (so0_hbm, so1_hbm, so2_hbm, so3_hbm)[d]
         outs += started([pltpu.make_async_copy(so_ref.at[d], so, so_sems.at[d])])
-        grads[d].wait()
-        gs = (g_ref[d].astype(F32) * inv).astype(BF)
+        grad_ref = (g0_ref, g1_ref, g2_ref, g3_ref)[d]
+        gs = (grad_ref[...].astype(F32) * inv).astype(BF)
         gs_ref[d] = gs
         ds_ref[d] = jnp.sum(gs.astype(F32) * att, axis=0, keepdims=True)
         gs_wide = gs_ref[d, :, pl.ds(base, 128)].astype(F32)
@@ -587,26 +628,16 @@
     r1_ref,
     r2_ref,
     r3_ref,
-    g0_hbm,
-    g1_hbm,
-    g2_hbm,
-    g3_hbm,
-    tab_hbm,
+    g0_ref,
+    g1_ref,
+    g2_ref,
+    g3_ref,
+    tab_ref,
     out_hbm,
     sum_ref,
     out_ref,
-    g_ref,
-    tab_ref,
     sems,
-    in_sems,
 ):
-    loads = started(
-        [pltpu.make_async_copy(tab_hbm, tab_ref, in_sems.at[4])]
-        + [
-            pltpu.make_async_copy(g, g_ref.at[d], in_sems.at[d])
-            for d, g in enumerate((g0_hbm, g1_hbm, g2_hbm, g3_hbm))
-        ]
-    )
     _, base, part = offsets(shift_ref)
     base = pl.multiple_of(base, 128)
     dkv = (
@@ -619,13 +650,13 @@
     lane = iota((1, 128), 1) >> 5
     rows = tab_ref.shape[0]
     outs = []
-    finish(loads)
     for d in range(4):
+        grad_ref = (g0_ref, g1_ref, g2_ref, g3_ref)[d]
         sum_ref[...] = dall_ref[d]
         sum_ref[:, pl.ds(base, 128)] += jnp.where(
             lane == part, turned(extra, 32 * (part - d)), 0.0
         )
-        both = jnp.concatenate([sum_ref[...].astype(BF), g_ref[d]], axis=0)
+        both = jnp.concatenate([sum_ref[...].astype(BF), grad_ref[...]], axis=0)
         onehot = jnp.where(tab_ref[:, d : d + 1] == iota((rows, BLK), 1), 1.0, 0.0).astype(BF)
         out_ref[:, 192 * d : 192 * d + 192] = mm(onehot, both, NT).astype(BF)
         if d % 2:
@@ -713,29 +744,26 @@
         limit=48,
     )(tile_features, all_pos, *weights)
     arrived = exchange(outgoing)
+    turned_ff = turned_weights(weights[:3], x)
 
     grads = call(
         order_kernel,
         [((HD, BLK), BF)] * 4,
-        [pltpu.VMEM((192, BLK), BF), dma((4,))],
-        n_hbm_out=4,
+        [pltpu.VMEM((192, BLK), BF)],
     )(slide_output_gradient.T)
     grads = [grads[0]] + [swap(grads[d], d, seq_count) for d in range(1, 4)]
     slots = device_count * SLOTS
     table, table_col = call(
         table_kernel,
         [((8, slots), I32), ((slots, 8), I32)],
-        [pltpu.VMEM((8, slots), I32), pltpu.VMEM((slots, 8), I32), dma((2,))],
-        n_hbm_out=2,
     )(all_pos)
 
     y, yt, y2 = call(
         place_kernel,
         [((4, BLK, 192), BF), ((4, 192, BLK), BF), ((128, 192), BF)],
-        [pltpu.VMEM((8, slots), I32), dma],
         n_smem=1,
         n_hbm=1,
-    )(dilation_shift, arrived, table)
+    )(dilation_shift, arrived, table, turned_ff[0])
     y2_in = [swap(y2, 4 * e, seq_count) for e in range(1, 4)]
     e0, m0, e1, m1, u, l = call(
         forward_kernel,
@@ -761,12 +789,9 @@
             pltpu.VMEM((HD, BLK), F32),
             pltpu.VMEM((1, BLK), F32),
             pltpu.VMEM((4, HD, BLK), BF),
-            pltpu.VMEM((4, HD, BLK), BF),
-            dma((4,)),
             dma((4,)),
         ],
         n_smem=1,
-        n_any=4,
         n_hbm_out=4,
     )(dilation_shift, yt, y2, *y2_in, u, l, *grads)
     back = [swap(send, 4 * e, seq_count) for e, send in ((1, send1), (2, send2), (3, send3))]
@@ -782,18 +807,14 @@
         [
             pltpu.VMEM((144, BLK), F32),
             pltpu.VMEM((slots, slide_width), BF),
-            pltpu.VMEM((4, HD, BLK), BF),
-            pltpu.VMEM((slots, 8), I32),
             dma((2,)),
-            dma((5,)),
         ],
         n_smem=1,
-        n_any=4,
-        n_hbm=1,
         n_hbm_out=1,
         limit=6,
     )(dilation_shift, dall, own, dq2, *back, *grads, table_col)
     returned = exchange(returning)
+    turned_rest = turned_weights(weights[3:], returning)
     parts = [parts[0]] + [swap(parts[d], d, seq_count) for d in range(1, 4)]
 
     (tile_grad,) = call(
@@ -806,15 +827,24 @@
             pltpu.VMEM((rows, ff), BF),
             pltpu.VMEM((rows, ff), BF),
         ]
-        + stored
+        + [pltpu.VMEM(w.shape[::-1], BF) for w in weights]
         + [
             pltpu.VMEM((rows, 3 * slide_width), BF),
             pltpu.VMEM((rows, slide_width), BF),
-            dma((19,)),
+            dma((22,)),
         ],
         n_hbm=10,
         limit=48,
-    )(returned.reshape(8, 16 * SLOTS, slide_width), all_pos, tile_features, x, a1, a2, *weights)
+    )(
+        returned.reshape(8, 16 * SLOTS, slide_width),
+        all_pos,
+        tile_features,
+        x,
+        a1,
+        a2,
+        *turned_ff,
+        *turned_rest,
+    )
     (slide_out,) = call(
         out_kernel,
         [((192, BLK), BF)],

time: 126 us -> 119 us (0.944)
  waiting for transfers between devices: 42.2 us -> 19.2 us
  Pallas kernels: 49.9 us -> 66 us
    all_to_all x2, waiting for transfers between devices: 42.2 us -> 19.1 us  [exchange(): lax.all_to_all(block.reshape(device_count, SLOTS, slide_width), ('seq', '...]
    pallas_call x10 -> x12, Pallas kernels: 49.9 us -> 66 us  [run(): pl.pallas_call(kernel, out_shape=shapes, in_specs=specs, out_specs=out_sp...]
  transfers between devices with their start and end apart: 14 -> 14, of which waited for: 2 -> 2; matrix products, arithmetic and copies ran while one was open for 0% -> 0% of each run, Pallas kernels for 24% -> 40%
where the time goes in v4:
time: 119 us
  Pallas kernels  66 us (55%)
  starting transfers between devices  32.6 us (27%)
  waiting for transfers between devices  19.2 us (16%)
    pallas_call x12, Pallas kernels, run(): pl.pallas_call(kernel, out_shape=shapes, in_specs=specs, out_specs=out_sp...  66 us
    all_to_all x2, waiting for transfers between devices, exchange(): lax.all_to_all(block.reshape(device_count, SLOTS, slide_width), ('seq', '...  19.1 us
    all_to_all x2, starting transfers between devices, exchange(): lax.all_to_all(block.reshape(device_count, SLOTS, slide_width), ('seq', '...  18.4 us
    ppermute x12, starting transfers between devices, swap(): return lax.ppermute(value, 'seq', [(i, i ^ distance) for i in range(count)])  14.2 us
  transfers between devices with their start and end apart: 14, of which 2 were waited for; matrix products, arithmetic and copies ran while one was open for 0% of the time, Pallas kernels for 40%

profile of v4, /device:TPU:1, one launch (start us, length us, event | category | flops | bytes accessed | tf_op | source)
XLA Modules:
  0.0 118.9 jit_solution(9722749339634391446)
XLA Ops:
  0.6 11.6 %shard_map.104 = (bf16[8,128,768]{2,1,0:T(8,128)(2,1)}, bf16[128,768]{1,0:T(8,128)(2,1)}, bf16[128,2048]{1,0:T(8,128)(2,1)}, bf16[128,2048]{1,0:T(8,128)(2,1)}) custom-call(bf16[128,1536]{1,0:T(8,128)(2,1)} %feat_hbm.3, s32[128,128]{1,0:T(8,128)} %bitcast.9, bf16[1536,2048]{1,0:T(8,128)(2,1)} %refs_0_.2, bf16[1536,2048]{1,0:T(8,128)(2,1)} %refs_1_.2, ...), custom_call_target="tpu_custom_call" | custom-call | tf_op jit(solution)/shard_map/pallas_call | solution.py:67
  12.3 0.0 copy-start.1
  12.3 0.0 copy-start
  12.3 11.5 %all-to-all-start = ((bf16[128,8,768]{2,1,0:T(8,128)(2,1)}), bf16[128,8,768]{2,1,0:T(8,128)(2,1)S(1)}, u32[]{:S(2)}, u32[]{:S(2)}) async-start(bf16[128,8,768]{2,1,0:T(8,128)(2,1)} %bitcast.14), calls=%async_computation | async-start | bytes 3145728 | tf_op jit(solution)/shard_map/all_to_all | solution.py:710
  23.8 0.3 shard_map.109
  24.1 1.1 collective-permute-start.3
  25.3 0.8 collective-permute-start.4
  26.1 0.9 collective-permute-start.5
  27.0 0.9 shard_map.105
  27.9 0.0 copy-start.3
  28.0 17.6 %shard_map.106 = (bf16[2048,1536]{1,0:T(8,128)(2,1)}, bf16[2048,1536]{1,0:T(8,128)(2,1)}, bf16[1536,2048]{1,0:T(8,128)(2,1)}) custom-call(bf16[1536,2048]{1,0:T(8,128)(2,1)} %refs_0_.2, bf16[1536,2048]{1,0:T(8,128)(2,1)} %refs_1_.2, bf16[2048,1536]{1,0:T(8,128)(2,1)} %refs_2_.1, bf16[128,768]{1,0:T(8,128)(2,1)} %get-tuple-element.39.refs_3_.x_hbm), custom_call_target="tpu_custom_call" | custom-call | tf_op jit(solution)/shard_map/pallas_call | solution.py:67
  45.5 3.7 %all-to-all-done = bf16[128,8,768]{2,1,0:T(8,128)(2,1)S(1)} async-done(((bf16[128,8,768]{2,1,0:T(8,128)(2,1)}), bf16[128,8,768]{2,1,0:T(8,128)(2,1)S(1)}, u32[]{:S(2)}, u32[]{:S(2)}) %all-to-all-start) | async-done | bytes 1572896 | tf_op jit(solution)/shard_map/all_to_all | solution.py:710
  49.2 2.0 %shard_map.107 = (bf16[4,512,192]{2,1,0:T(8,128)(2,1)S(1)}, bf16[4,192,512]{2,1,0:T(8,128)(2,1)S(1)}, bf16[128,192]{1,0:T(8,128)(2,1)S(1)}) custom-call(s32[2,16]{1,0:T(2,128)S(1)} %copy-done.3, bf16[1024,768]{1,0:T(8,128)(2,1)S(1)} %bitcast.8, s32[8,1024]{1,0:T(8,128)S(1)} %get-tuple-element.38.tab_ref, bf16[2048,1536]{1,0:T(8,128)(2,1)} %get-tuple-element.40._after_hbm.gate_hbm), custom_call_target="tpu_custom_call" | custom-call | tf_op jit(solution)/shard_map/pallas_call | solution.py:67
  51.1 0.1 collective-permute-start.2
  51.2 1.0 collective-permute-start.1
  52.2 3.2 %collective-permute-start = (bf16[128,192]{1,0:T(8,128)(2,1)S(1)}, bf16[128,192]{1,0:T(8,128)(2,1)S(1)}, u32[]{:S(2)}, u32[]{:S(2)}) collective-permute-start(bf16[128,192]{1,0:T(8,128)(2,1)S(1)} %get-tuple-element.42.a0_ref), channel_id=1, source_target_pairs={{0,16},{4,20},{8,24},{12,28},{16,0},{20,4},{24,8},{28,12},{32,48},... | collective-permute-start | bytes 147464 | tf_op jit(solution)/shard_map/ppermute | solution.py:686
  55.4 4.3 %shard_map.108 = (bf16[4,512,512]{2,1,0:T(8,128)(2,1)S(1)}, bf16[4,512,512]{2,1,0:T(8,128)(2,1)S(1)}, bf16[512,512]{1,0:T(8,128)(2,1)S(1)}, bf16[512,512]{1,0:T(...) custom-call(s32[2,16]{1,0:T(2,128)S(1)} %copy-done.3, ...), custom_call_target="tpu_custom_call" | custom-call | tf_op jit(solution)/shard_map/pallas_call | solution.py:67
  59.7 2.0 %shard_map.110 = (bf16[48,512]{1,0:T(8,128)(2,1)}, bf16[48,512]{1,0:T(8,128)(2,1)}, bf16[48,512]{1,0:T(8,128)(2,1)}, bf16[48,512]{1,0:T(8,128)(2,1)}, bf16[4,48,...) custom-call(s32[2,16]{1,0:T(2,128)S(1)} %copy-done.3, ...), custom_call_target="tpu_custom_call" | custom-call | tf_op jit(solution)/shard_map/pallas_call | solution.py:67
  61.7 0.3 collective-permute-start.9
  62.0 0.3 collective-permute-start.10
  62.4 3.5 %collective-permute-start.11 = (bf16[96,128]{1,0:T(8,128)(2,1)S(1)}, bf16[96,128]{1,0:T(8,128)(2,1)S(1)}, u32[]{:S(2)}, u32[]{:S(2)}) collective-permute-start(bf16[96,128]{1,0:T(8,128)(2,1)S(1)} %get-tuple-element.64), channel_id=1, source_target_pairs={{0,48},{4,52},{8,56},{12,60},{16,32},{20,36},{24,40},{28,44},{32,1... | collective-permute-start | bytes 73736 | tf_op jit(solution)/shard_map/ppermute | solution.py:686
  65.9 4.4 %shard_map.111.dall_ref = f32[4,144,512]{2,1,0:T(8,128)S(1)} custom-call(s32[2,16]{1,0:T(2,128)S(1)} %copy-done.3, bf16[4,512,192]{2,1,0:T(8,128)(2,1)S(1)} %get-tuple-element.43.y_ref, bf16[4,192,512]{2,1,0:T(8,128)(2,1)S(1)} %get-tuple-element.41.yt_ref, bf16[4,512,512]{2,1,0:T(8,128)(2,1)S(1)} %get-tuple-element.54.e0_ref, ...), custom_call_target="tpu_custom_call" | custom-call | tf_op jit(solution)/shard_map/pallas_call | solution.py:67
  70.4 3.2 %shard_map.112.refs_2_ = bf16[1024,768]{1,0:T(8,128)(2,1)} custom-call(s32[2,16]{1,0:T(2,128)S(1)} %copy-done.3, f32[4,144,512]{2,1,0:T(8,128)S(1)} %shard_map.111.dall_ref, f32[96,128]{1,0:T(8,128)S(1)} %get-tuple-element.60.own_ref, f32[48,128]{1,0:T(8,128)S(1)} %get-tuple-element.61.dq_ref, bf16[96,128]{1,0:T(8,128)(2,1)S(1)} %collective-permute-done.9.r1_ref, ...), custom_call_target="tpu_custom_call" | custom-call | tf_op jit(solution)/shard_map/pallas_call | solution.py:67
  73.6 0.0 copy-start.6
  73.7 6.9 %all-to-all-start.1 = ((bf16[128,8,768]{2,1,0:T(8,128)(2,1)}), bf16[128,8,768]{2,1,0:T(8,128)(2,1)S(1)}, u32[]{:S(2)}, u32[]{:S(2)}) async-start(bf16[128,8,768]{2,1,0:T(8,128)(2,1)} %bitcast.13), calls=%async_computation.1 | async-start | bytes 3145728 | tf_op jit(solution)/shard_map/all_to_all | solution.py:710
  80.6 1.1 collective-permute-start.6
  81.7 0.8 collective-permute-start.7
  82.5 0.9 collective-permute-start.8
  83.4 7.0 %shard_map.113 = (bf16[768,1536]{1,0:T(8,128)(2,1)}, bf16[2304,768]{1,0:T(8,128)(2,1)}) custom-call(bf16[1536,768]{1,0:T(8,128)(2,1)} %refs_0_.3, bf16[768,2304]{1,0:T(8,128)(2,1)} %refs_1_.3, bf16[1024,768]{1,0:T(8,128)(2,1)} %shard_map.112.refs_2_), custom_call_target="tpu_custom_call" | custom-call | tf_op jit(solution)/shard_map/pallas_call | solution.py:67
  90.5 15.5 %all-to-all-done.1 = bf16[128,8,768]{2,1,0:T(8,128)(2,1)S(1)} async-done(((bf16[128,8,768]{2,1,0:T(8,128)(2,1)}), bf16[128,8,768]{2,1,0:T(8,128)(2,1)S(1)}, u32[]{:S(2)}, u32[]{:S(2)}) %all-to-all-start.1) | async-done | bytes 1572896 | tf_op jit(solution)/shard_map/all_to_all | solution.py:710
  105.9 11.4 %shard_map.114._after_hbm = bf16[128,1536]{1,0:T(8,128)(2,1)} custom-call(bf16[8,128,768]{2,1,0:T(8,128)(2,1)S(1)} %bitcast.7, s32[128,128]{1,0:T(8,128)} %bitcast.10, bf16[128,1536]{1,0:T(8,128)(2,1)} %feat_hbm.3, bf16[128,768]{1,0:T(8,128)(2,1)} %get-tuple-element.39.refs_3_.x_hbm, bf16[128,2048]{1,0:T(8,128)(2,1)} %get-tuple-element.66.a1_hbm, ...), custom_call_target="tpu_custom_call" | custom-call | tf_op jit(solution)/shard_map/pallas_call | solution.py:67
  117.3 1.3 %shard_map.115 = bf16[192,512]{1,0:T(8,128)(2,1)} custom-call(bf16[48,512]{1,0:T(8,128)(2,1)S(1)} %copy-done.2, bf16[48,512]{1,0:T(8,128)(2,1)S(1)} %collective-permute-done.6.s1_hbm, bf16[48,512]{1,0:T(8,128)(2,1)S(1)} %collective-permute-done.7.s2_hbm, bf16[48,512]{1,0:T(8,128)(2,1)S(1)} %collective-permute-done.8.s3_hbm, ...), custom_call_target="tpu_custom_call" | custom-call | tf_op jit(solution)/shard_map/pallas_call | solution.py:67
  (22 shorter events, 0.1 us)
Async XLA Ops:
  12.3 11.5 %copy-start.1 = (bf16[512,192]{0,1:T(8,128)(2,1)S(1)}, bf16[512,192]{0,1:T(8,128)(2,1)}, u32[]{:S(2)}) copy-start(bf16[512,192]{0,1:T(8,128)(2,1)} %param.17) | copy-start | bytes 589828
  12.3 14.7 %copy-start = (s32[16384]{0:T(1024)S(1)}, s32[16384]{0:T(1024)}, u32[]{:S(2)}) copy-start(s32[16384]{0:T(1024)} %param.15) | copy-start | bytes 196612
  12.3 36.9 %all-to-all-start = ((bf16[128,8,768]{2,1,0:T(8,128)(2,1)}), bf16[128,8,768]{2,1,0:T(8,128)(2,1)S(1)}, u32[]{:S(2)}, u32[]{:S(2)}) async-start(bf16[128,8,768]{2,1,0:T(8,128)(2,1)} %bitcast.14), calls=%async_computation | async-start | bytes 3145728 | tf_op jit(solution)/shard_map/all_to_all | solution.py:710
  24.1 28.1 %collective-permute-start.3 = (bf16[48,512]{1,0:T(8,128)(2,1)S(1)}, bf16[48,512]{1,0:T(8,128)(2,1)S(1)}, u32[]{:S(2)}, u32[]{:S(2)}) collective-permute-start(bf16[48,512]{1,0:T(8,128)(2,1)S(1)} %get-tuple-element.47), channel_id=1, source_target_pairs={{0,4},{4,0},{8,12},{12,8},{16,20},{20,16},{24,28},{28,24},{32,36},... | collective-permute-start | bytes 147464 | tf_op jit(solution)/shard_map/ppermute | solution.py:686
  25.3 34.4 %collective-permute-start.4 = (bf16[48,512]{1,0:T(8,128)(2,1)S(1)}, bf16[48,512]{1,0:T(8,128)(2,1)S(1)}, u32[]{:S(2)}, u32[]{:S(2)}) collective-permute-start(bf16[48,512]{1,0:T(8,128)(2,1)S(1)} %get-tuple-element.48), channel_id=1, source_target_pairs={{0,8},{4,12},{8,0},{12,4},{16,24},{20,28},{24,16},{28,20},{32,40},... | collective-permute-start | bytes 147464 | tf_op jit(solution)/shard_map/ppermute | solution.py:686
  26.1 33.6 %collective-permute-start.5 = (bf16[48,512]{1,0:T(8,128)(2,1)S(1)}, bf16[48,512]{1,0:T(8,128)(2,1)S(1)}, u32[]{:S(2)}, u32[]{:S(2)}) collective-permute-start(bf16[48,512]{1,0:T(8,128)(2,1)S(1)} %get-tuple-element.49), channel_id=1, source_target_pairs={{0,12},{4,8},{8,4},{12,0},{16,28},{20,24},{24,20},{28,16},{32,44},... | collective-permute-start | bytes 147464 | tf_op jit(solution)/shard_map/ppermute | solution.py:686
  27.9 21.2 %copy-start.3 = (s32[2,16]{1,0:T(2,128)S(1)}, s32[2,16]{1,0:T(2,128)}, u32[]{:S(2)}) copy-start(s32[2,16]{1,0:T(2,128)} %shift_ref.9) | copy-start | bytes 388
  51.1 8.5 %collective-permute-start.2 = (bf16[128,192]{1,0:T(8,128)(2,1)S(1)}, bf16[128,192]{1,0:T(8,128)(2,1)S(1)}, u32[]{:S(2)}, u32[]{:S(2)}) collective-permute-start(bf16[128,192]{1,0:T(8,128)(2,1)S(1)} %get-tuple-element.42.a0_ref), channel_id=1, source_target_pairs={{0,48},{4,52},{8,56},{12,60},{16,32},{20,36},{24,40},{28,44},{32,1... | collective-permute-start | bytes 147464 | tf_op jit(solution)/shard_map/ppermute | solution.py:686
  51.2 8.5 %collective-permute-start.1 = (bf16[128,192]{1,0:T(8,128)(2,1)S(1)}, bf16[128,192]{1,0:T(8,128)(2,1)S(1)}, u32[]{:S(2)}, u32[]{:S(2)}) collective-permute-start(bf16[128,192]{1,0:T(8,128)(2,1)S(1)} %get-tuple-element.42.a0_ref), channel_id=1, source_target_pairs={{0,32},{4,36},{8,40},{12,44},{16,48},{20,52},{24,56},{28,60},{32,0... | collective-permute-start | bytes 147464 | tf_op jit(solution)/shard_map/ppermute | solution.py:686
  52.2 7.5 %collective-permute-start = (bf16[128,192]{1,0:T(8,128)(2,1)S(1)}, bf16[128,192]{1,0:T(8,128)(2,1)S(1)}, u32[]{:S(2)}, u32[]{:S(2)}) collective-permute-start(bf16[128,192]{1,0:T(8,128)(2,1)S(1)} %get-tuple-element.42.a0_ref), channel_id=1, source_target_pairs={{0,16},{4,20},{8,24},{12,28},{16,0},{20,4},{24,8},{28,12},{32,48},... | collective-permute-start | bytes 147464 | tf_op jit(solution)/shard_map/ppermute | solution.py:686
  61.7 8.7 %collective-permute-start.9 = (bf16[96,128]{1,0:T(8,128)(2,1)S(1)}, bf16[96,128]{1,0:T(8,128)(2,1)S(1)}, u32[]{:S(2)}, u32[]{:S(2)}) collective-permute-start(bf16[96,128]{1,0:T(8,128)(2,1)S(1)} %get-tuple-element.62), channel_id=1, source_target_pairs={{0,16},{4,20},{8,24},{12,28},{16,0},{20,4},{24,8},{28,12},{32,48},... | collective-permute-start | bytes 73736 | tf_op jit(solution)/shard_map/ppermute | solution.py:686
  62.0 8.3 %collective-permute-start.10 = (bf16[96,128]{1,0:T(8,128)(2,1)S(1)}, bf16[96,128]{1,0:T(8,128)(2,1)S(1)}, u32[]{:S(2)}, u32[]{:S(2)}) collective-permute-start(bf16[96,128]{1,0:T(8,128)(2,1)S(1)} %get-tuple-element.63), channel_id=1, source_target_pairs={{0,32},{4,36},{8,40},{12,44},{16,48},{20,52},{24,56},{28,60},{32,0... | collective-permute-start | bytes 73736 | tf_op jit(solution)/shard_map/ppermute | solution.py:686
  62.4 8.0 %collective-permute-start.11 = (bf16[96,128]{1,0:T(8,128)(2,1)S(1)}, bf16[96,128]{1,0:T(8,128)(2,1)S(1)}, u32[]{:S(2)}, u32[]{:S(2)}) collective-permute-start(bf16[96,128]{1,0:T(8,128)(2,1)S(1)} %get-tuple-element.64), channel_id=1, source_target_pairs={{0,48},{4,52},{8,56},{12,60},{16,32},{20,36},{24,40},{28,44},{32,1... | collective-permute-start | bytes 73736 | tf_op jit(solution)/shard_map/ppermute | solution.py:686
  73.6 6.9 %copy-start.6 = (bf16[48,512]{1,0:T(8,128)(2,1)S(1)}, bf16[48,512]{1,0:T(8,128)(2,1)}, u32[]{:S(2)}) copy-start(bf16[48,512]{1,0:T(8,128)(2,1)} %get-tuple-element.51) | copy-start | bytes 147460
  73.6 8.1 %copy-start.5 = (bf16[48,512]{1,0:T(8,128)(2,1)S(1)}, bf16[48,512]{1,0:T(8,128)(2,1)}, u32[]{:S(2)}) copy-start(bf16[48,512]{1,0:T(8,128)(2,1)} %get-tuple-element.52) | copy-start | bytes 147460
  73.7 8.9 %copy-start.4 = (bf16[48,512]{1,0:T(8,128)(2,1)S(1)}, bf16[48,512]{1,0:T(8,128)(2,1)}, u32[]{:S(2)}) copy-start(bf16[48,512]{1,0:T(8,128)(2,1)} %get-tuple-element.53) | copy-start | bytes 147460
  73.7 32.3 %all-to-all-start.1 = ((bf16[128,8,768]{2,1,0:T(8,128)(2,1)}), bf16[128,8,768]{2,1,0:T(8,128)(2,1)S(1)}, u32[]{:S(2)}, u32[]{:S(2)}) async-start(bf16[128,8,768]{2,1,0:T(8,128)(2,1)} %bitcast.13), calls=%async_computation.1 | async-start | bytes 3145728 | tf_op jit(solution)/shard_map/all_to_all | solution.py:710
  80.6 36.7 %collective-permute-start.6 = (bf16[48,512]{1,0:T(8,128)(2,1)S(1)}, bf16[48,512]{1,0:T(8,128)(2,1)S(1)}, u32[]{:S(2)}, u32[]{:S(2)}) collective-permute-start(bf16[48,512]{1,0:T(8,128)(2,1)S(1)} %copy-done.6), channel_id=1, source_target_pairs={{0,4},{4,0},{8,12},{12,8},{16,20},{20,16},{24,28},{28,24},{32,36},... | collective-permute-start | bytes 147464 | tf_op jit(solution)/shard_map/ppermute | solution.py:686
  81.7 35.6 %collective-permute-start.7 = (bf16[48,512]{1,0:T(8,128)(2,1)S(1)}, bf16[48,512]{1,0:T(8,128)(2,1)S(1)}, u32[]{:S(2)}, u32[]{:S(2)}) collective-permute-start(bf16[48,512]{1,0:T(8,128)(2,1)S(1)} %copy-done.5), channel_id=1, source_target_pairs={{0,8},{4,12},{8,0},{12,4},{16,24},{20,28},{24,16},{28,20},{32,40},... | collective-permute-start | bytes 147464 | tf_op jit(solution)/shard_map/ppermute | solution.py:686
  82.5 34.8 %collective-permute-start.8 = (bf16[48,512]{1,0:T(8,128)(2,1)S(1)}, bf16[48,512]{1,0:T(8,128)(2,1)S(1)}, u32[]{:S(2)}, u32[]{:S(2)}) collective-permute-start(bf16[48,512]{1,0:T(8,128)(2,1)S(1)} %copy-done.4), channel_id=1, source_target_pairs={{0,12},{4,8},{8,4},{12,0},{16,28},{20,24},{24,20},{28,16},{32,44},... | collective-permute-start | bytes 147464 | tf_op jit(solution)/shard_map/ppermute | solution.py:686
  105.9 11.4 %copy-start.2 = (bf16[48,512]{1,0:T(8,128)(2,1)S(1)}, bf16[48,512]{1,0:T(8,128)(2,1)}, u32[]{:S(2)}) copy-start(bf16[48,512]{1,0:T(8,128)(2,1)} %get-tuple-element.50.s0_hbm) | copy-start | bytes 147460

commit v5 on v4

--- a/solution.py
+++ b/solution.py
@@ -12,6 +12,7 @@
 EPSILON = 1e-06
 SOFT_CAP = 50.0
 SCALE = HD**-0.5
+LOG2_E = 1.4426950408889634
 BLK = 512
 SLOTS = 8
 BF = jnp.bfloat16
@@ -154,7 +155,6 @@
     x_ref,
     a1_ref,
     a2_ref,
-    qkv_ref,
     heads_ref,
     picker_ref,
     tmp_ref,
@@ -162,6 +162,7 @@
     out_sems,
 ):
     ff = gate_hbm.shape[1]
+    width = HEADS * HD
     step = 512
     chunks = ff // step
     first = started(
@@ -185,7 +186,10 @@
     last = started(
         [
             pltpu.make_async_copy(proj_hbm, wp_ref, sems.at[3 * chunks + 2]),
-            pltpu.make_async_copy(qkvw_hbm, wq_ref, sems.at[3 * chunks + 3]),
+        ]
+        + [
+            pltpu.make_async_copy(qkvw_hbm.at[:, at], wq_ref.at[:, at], sems.at[3 * chunks + 3 + i])
+            for i, at in enumerate(pl.ds(width * part, width) for part in range(3))
         ]
     )
     finish(first)
@@ -230,20 +234,22 @@
     x_ref[...] = x
     outs += started([pltpu.make_async_copy(x_ref, x_hbm, out_sems.at[2])])
     slide_norm = normalize(x.astype(F32))[0].astype(BF)
-    last[1].wait()
-    qkv_ref[...] = mm(slide_norm, wq_ref[...]).astype(BF)
-
-    width = HEADS * HD
+
+    def deal(values, part):
+        for h in range(HEADS):
+            t, j = h // 4, h % 4
+            heads_ref[2 * j + t // 2, n * (t % 2) : n * (t % 2) + n, HD * part : HD * part + HD] = (
+                values[:, h * HD : h * HD + HD]
+            )
+
+    deal(x, 3)
+    for part in range(3):
+        last[1 + part].wait()
+        at = slice(width * part, width * part + width)
+        deal(mm(slide_norm, wq_ref[:, at]).astype(BF), part)
     for pair in range(HEADS // 2):
-        j, t = pair // 2, 2 * (pair % 2)
-        for tp in range(2):
-            h = 4 * (t + tp) + j
-            for part in range(3):
-                heads_ref[n * tp : n * tp + n, HD * part : HD * part + HD] = qkv_ref[
-                    :, part * width + h * HD : part * width + h * HD + HD
-                ]
-            heads_ref[n * tp : n * tp + n, 144:192] = x_ref[:, h * HD : h * HD + HD]
-        rows = mm(picker_ref[...], heads_ref[...]).astype(BF)
+        j = pair // 2
+        rows = mm(picker_ref[...], heads_ref[pair]).astype(BF)
         at = slice(16 * pair, 16 * pair + 16)
         for block in range(4):
             lane = (j ^ block) * 192
@@ -328,6 +334,10 @@
 
 def backward_mlp_kernel(
     ret_ref,
+    s0_any,
+    s1_any,
+    s2_any,
+    s3_any,
     pos_hbm,
     feat_hbm,
     x_hbm,
@@ -339,6 +349,7 @@
     proj_hbm,
     qkvw_hbm,
     out_ref,
+    slide_ref,
     pos_ref,
     feat_ref,
     x_ref,
@@ -351,6 +362,7 @@
     wq_ref,
     dqkv_ref,
     grad_ref,
+    tmp_ref,
     sems,
 ):
     ff = gate_hbm.shape[0]
@@ -383,6 +395,17 @@
                 ]
             )
         )
+    j = lax.axis_index("seq") & 3
+    pieces = started(
+        [
+            pltpu.make_async_copy(
+                so,
+                tmp_ref.at[pl.ds(pl.multiple_of((j ^ d) * HD, 16), HD), :],
+                sems.at[3 * chunks + len(pairs) + d],
+            )
+            for d, so in enumerate((s0_any, s1_any, s2_any, s3_any))
+        ]
+    )
     first[0].wait()
     me = lax.axis_index("seq") * 4 + lax.axis_index("tile")
     brow = pos_ref[pl.ds(me, 1), :] >> 9
@@ -420,6 +443,8 @@
     dembed = mm(dslide, wp_ref[...]).astype(BF)
     finish(first[4:])
     normed, inv = normalize(feat_ref[...].astype(F32))
+    finish(pieces)
+    slide_ref[...] = mm(tmp_ref[...], order_matrix(), NT).astype(BF)
     dfeat = jnp.zeros(feat_ref.shape, F32)
     for c, (start, size) in enumerate(cuts):
         at = slice(start, start + size)
@@ -447,23 +472,22 @@
 
 
 def score_rows(keys, queries_t, e_store, m_store):
-    scores = mm(keys, queries_t)
-    count, width = scores.shape
+    count, width = keys.shape[0], queries_t.shape[1]
     total = jnp.zeros((8, width), F32)
-    step = 64
+    step = 128
     for c in range(0, count, step):
-        t = jnp.tanh(scores[c : c + step] * (SCALE / SOFT_CAP))
-        e = jnp.exp(SOFT_CAP * t)
+        t = jnp.tanh(mm(keys[c : c + step], queries_t) * (SCALE / SOFT_CAP))
+        e = jnp.exp2((SOFT_CAP * LOG2_E) * t)
         total = total + jnp.sum(e.reshape(step // 8, 8, width), axis=0)
         e_store(c, step, e.astype(BF))
-        m_store(c, step, (e * (1.0 - t * t) * SCALE).astype(BF))
+        m_store(c, step, (e - e * (t * t)).astype(BF))
     return jnp.sum(total, axis=0, keepdims=True)
 
 
 def forward_kernel(shift_ref, y_ref, yt_ref, e0_ref, m0_ref, e1_ref, m1_ref, u_ref, l_ref):
     o1 = pl.multiple_of(offsets(shift_ref)[0], 128)
 
-    def block(d, carry):
+    def block(d):
         def e_store(c, n, v):
             e0_ref[d, c : c + n, :] = v
 
@@ -472,9 +496,9 @@
 
         l_ref[d] = score_rows(y_ref[d, :, 48:96], yt_ref[d, 0:48, :], e_store, m_store)
         u_ref[d] = mm(yt_ref[d, 96:144, :], e0_ref[d])
-        return carry
-
-    lax.fori_loop(0, 4, block, 0)
+
+    for d in range(4):
+        block(d)
 
     def e_store(c, n, v):
         e1_ref[c : c + n, :] = v
@@ -570,8 +594,8 @@
     gs2 = gs2.astype(BF)
     dp = mm(values, gs2)
     dscore = (m2_ref[...].astype(F32) * (dp - ds2[0:1])).astype(BF)
-    dq_ref[...] = mm(both_t[0:48], dscore)
-    dk = mm(query_t, dscore, NT)
+    dq_ref[...] = mm(both_t[0:48], dscore) * SCALE
+    dk = mm(query_t, dscore, NT) * SCALE
     dv = mm(gs2, e2_ref[...], NT)
     dkv = jnp.concatenate([dk, dv], axis=0)
     own_ref[...] = dkv[:, 0:128]
@@ -595,16 +619,16 @@
     def store(c, n, v):
         tmp_ref[c : c + n, :] = v
 
-    def block(d, carry):
+    def block(d):
         gs = gs_ref[d]
         dscores(y_ref[d, :, 96:144], gs, ds_ref[d], lambda c, n: m0_ref[d, c : c + n, :], store)
         dscore = tmp_ref[...]
-        out_ref[d, 0:48, :] = mm(yt_ref[d, 48:96, :], dscore)
-        out_ref[d, 48:96, :] = mm(yt_ref[d, 0:48, :], dscore, NT)
+        out_ref[d, 0:48, :] = mm(yt_ref[d, 48:96, :], dscore) * SCALE
+        out_ref[d, 48:96, :] = mm(yt_ref[d, 0:48, :], dscore, NT) * SCALE
         out_ref[d, 96:144, :] = mm(gs, e0_ref[d], NT)
-        return carry
-
-    lax.fori_loop(0, 4, block, 0)
+
+    for d in range(4):
+        block(d)
     values = jnp.concatenate([y_ref[d, pl.ds(o1, 128), 96:144] for d in range(4)], axis=0)
     queries = jnp.concatenate([yt_ref[d, 0:48, pl.ds(o1, 128)] for d in range(4)], axis=1)
     keys = jnp.concatenate([yt_ref[d, 48:96, pl.ds(o1, 128)] for d in range(4)], axis=1)
@@ -612,8 +636,8 @@
     ds = jnp.concatenate([ds_ref[d, :, pl.ds(o1, 128)] for d in range(4)], axis=1)
     dscores(values, gs, ds, lambda c, n: m1_ref[c : c + n, :], store)
     dscore = tmp_ref[...]
-    dq = mm(keys, dscore)
-    dk = mm(queries, dscore, NT)
+    dq = mm(keys, dscore) * SCALE
+    dk = mm(queries, dscore, NT) * SCALE
     dv = mm(gs, e1_ref[...], NT)
     dall = jnp.concatenate([dq, dk, dv], axis=0)
     for d in range(4):
@@ -649,37 +673,22 @@
     extra = jnp.concatenate([dq_ref[...], dkv], axis=0)
     lane = iota((1, 128), 1) >> 5
     rows = tab_ref.shape[0]
-    outs = []
+    step = rows // 4
+    outs, parts = [], []
     for d in range(4):
         grad_ref = (g0_ref, g1_ref, g2_ref, g3_ref)[d]
         sum_ref[...] = dall_ref[d]
         sum_ref[:, pl.ds(base, 128)] += jnp.where(
             lane == part, turned(extra, 32 * (part - d)), 0.0
         )
-        both = jnp.concatenate([sum_ref[...].astype(BF), grad_ref[...]], axis=0)
-        onehot = jnp.where(tab_ref[:, d : d + 1] == iota((rows, BLK), 1), 1.0, 0.0).astype(BF)
-        out_ref[:, 192 * d : 192 * d + 192] = mm(onehot, both, NT).astype(BF)
-        if d % 2:
-            at = pl.ds(384 * (d // 2), 384)
-            outs += started(
-                [pltpu.make_async_copy(out_ref.at[:, at], out_hbm.at[:, at], sems.at[d // 2])]
-            )
+        parts.append(jnp.concatenate([sum_ref[...].astype(BF), grad_ref[...]], axis=0).T)
+    for c in range(4):
+        at = slice(step * c, step * c + step)
+        for d in range(4):
+            onehot = jnp.where(tab_ref[at, d : d + 1] == iota((step, BLK), 1), 1.0, 0.0)
+            out_ref[at, 192 * d : 192 * d + 192] = mm(onehot.astype(BF), parts[d]).astype(BF)
+        outs += started([pltpu.make_async_copy(out_ref.at[at, :], out_hbm.at[at, :], sems.at[c])])
     finish(outs)
-
-
-def out_kernel(s0_hbm, s1_hbm, s2_hbm, s3_hbm, _after_hbm, out_ref, tmp_ref, sems):
-    j = lax.axis_index("seq") & 3
-    finish(
-        started(
-            [
-                pltpu.make_async_copy(
-                    so, tmp_ref.at[pl.ds(pl.multiple_of((j ^ d) * HD, 16), HD), :], sems.at[d]
-                )
-                for d, so in enumerate((s0_hbm, s1_hbm, s2_hbm, s3_hbm))
-            ]
-        )
-    )
-    out_ref[...] = mm(tmp_ref[...], order_matrix(), NT).astype(BF)
 
 
 def swap(value, distance, count):
@@ -732,11 +741,10 @@
             pltpu.VMEM((rows, slide_width), BF),
             pltpu.VMEM((rows, ff), BF),
             pltpu.VMEM((rows, ff), BF),
-            pltpu.VMEM((rows, 3 * slide_width), BF),
-            pltpu.VMEM((2 * rows, 192), BF),
+            pltpu.VMEM((HEADS // 2, 2 * rows, 192), BF),
             pltpu.VMEM((BLK, 2 * rows), BF),
             pltpu.VMEM((8, 16 * SLOTS, slide_width), BF),
-            dma((16,)),
+            dma((18,)),
             dma((3 + HEADS // 2,)),
         ],
         n_hbm=7,
@@ -744,7 +752,7 @@
         limit=48,
     )(tile_features, all_pos, *weights)
     arrived = exchange(outgoing)
-    turned_ff = turned_weights(weights[:3], x)
+    turned_ff = turned_weights(weights[:2], x)
 
     grads = call(
         order_kernel,
@@ -807,19 +815,19 @@
         [
             pltpu.VMEM((144, BLK), F32),
             pltpu.VMEM((slots, slide_width), BF),
-            dma((2,)),
+            dma((4,)),
         ],
         n_smem=1,
         n_hbm_out=1,
         limit=6,
     )(dilation_shift, dall, own, dq2, *back, *grads, table_col)
     returned = exchange(returning)
-    turned_rest = turned_weights(weights[3:], returning)
+    turned_rest = turned_weights(weights[2:], returning)
     parts = [parts[0]] + [swap(parts[d], d, seq_count) for d in range(1, 4)]
 
-    (tile_grad,) = call(
+    tile_grad, slide_out = call(
         backward_mlp_kernel,
-        [((rows, width), BF)],
+        [((rows, width), BF), ((192, BLK), BF)],
         [
             pltpu.VMEM((device_count, rows), I32),
             pltpu.VMEM((rows, width), BF),
@@ -831,12 +839,15 @@
         + [
             pltpu.VMEM((rows, 3 * slide_width), BF),
             pltpu.VMEM((rows, slide_width), BF),
-            dma((22,)),
+            pltpu.VMEM((192, BLK), BF),
+            dma((26,)),
         ],
+        n_any=4,
         n_hbm=10,
         limit=48,
     )(
         returned.reshape(8, 16 * SLOTS, slide_width),
+        *parts,
         all_pos,
         tile_features,
         x,
@@ -845,13 +856,6 @@
         *turned_ff,
         *turned_rest,
     )
-    (slide_out,) = call(
-        out_kernel,
-        [((192, BLK), BF)],
-        [pltpu.VMEM((192, BLK), BF), dma((4,))],
-        n_any=4,
-        n_hbm=1,
-    )(*parts, tile_grad)
     return (slide_out.T, tile_grad)
 
 

time: 119 us -> 117 us (0.983)
  Pallas kernels: 66 us -> 62.9 us
    ppermute x12, waiting for transfers between devices: 0.03 us -> 3.83 us  [swap(): return lax.ppermute(value, 'seq', [(i, i ^ distance) for i in range(count)])]
    all_to_all x2, waiting for transfers between devices: 19.1 us -> 15.7 us  [exchange(): lax.all_to_all(block.reshape(device_count, SLOTS, slide_width), ('seq', '...]
    pallas_call x12 -> x11, Pallas kernels: 66 us -> 62.9 us  [run(): pl.pallas_call(kernel, out_shape=shapes, in_specs=specs, out_specs=out_sp...]
  transfers between devices with their start and end apart: 14 -> 14, of which waited for: 2 -> 3; matrix products, arithmetic and copies ran while one was open for 0% -> 0% of each run, Pallas kernels for 40% -> 30%
where the time goes in v5:
time: 117 us; the launch traced here: 116 us
  Pallas kernels  62.9 us (54%)
  starting transfers between devices  32.6 us (28%)
  waiting for transfers between devices  19.6 us (17%)
    pallas_call x11, Pallas kernels, run(): pl.pallas_call(kernel, out_shape=shapes, in_specs=specs, out_specs=out_sp...  62.9 us
    all_to_all x2, starting transfers between devices, exchange(): lax.all_to_all(block.reshape(device_count, SLOTS, slide_width), ('seq', '...  18.4 us
    all_to_all x2, waiting for transfers between devices, exchange(): lax.all_to_all(block.reshape(device_count, SLOTS, slide_width), ('seq', '...  15.7 us
    ppermute x12, starting transfers between devices, swap(): return lax.ppermute(value, 'seq', [(i, i ^ distance) for i in range(count)])  14.2 us
    ppermute x12, waiting for transfers between devices, swap(): return lax.ppermute(value, 'seq', [(i, i ^ distance) for i in range(count)])  3.83 us
  transfers between devices with their start and end apart: 14, of which 3 were waited for; matrix products, arithmetic and copies ran while one was open for 0% of the time, Pallas kernels for 30%

profile of v5, /device:TPU:1, one launch (start us, length us, event | category | flops | bytes accessed | tf_op | source)
XLA Modules:
  0.0 116.1 jit_solution(12295286364775611590)
XLA Ops:
  0.6 11.8 %shard_map.104 = (bf16[8,128,768]{2,1,0:T(8,128)(2,1)}, bf16[128,768]{1,0:T(8,128)(2,1)}, bf16[128,2048]{1,0:T(8,128)(2,1)}, bf16[128,2048]{1,0:T(8,128)(2,1)}) custom-call(bf16[128,1536]{1,0:T(8,128)(2,1)} %feat_hbm.3, s32[128,128]{1,0:T(8,128)} %bitcast.9, bf16[1536,2048]{1,0:T(8,128)(2,1)} %refs_0_.2, bf16[1536,2048]{1,0:T(8,128)(2,1)} %refs_1_.2, ...), custom_call_target="tpu_custom_call" | custom-call | tf_op jit(solution)/shard_map/pallas_call | solution.py:68
  12.4 0.0 copy-start.1
  12.4 0.0 copy-start
  12.4 11.5 %all-to-all-start = ((bf16[128,8,768]{2,1,0:T(8,128)(2,1)}), bf16[128,8,768]{2,1,0:T(8,128)(2,1)S(1)}, u32[]{:S(2)}, u32[]{:S(2)}) async-start(bf16[128,8,768]{2,1,0:T(8,128)(2,1)} %bitcast.14), calls=%async_computation | async-start | bytes 3145728 | tf_op jit(solution)/shard_map/all_to_all | solution.py:719
  24.0 0.3 shard_map.109
  24.3 1.1 collective-permute-start.3
  25.4 0.8 collective-permute-start.4
  26.2 0.9 collective-permute-start.5
  27.2 0.9 shard_map.105
  28.1 0.0 copy-start.3
  28.1 11.9 %shard_map.106 = (bf16[2048,1536]{1,0:T(8,128)(2,1)}, bf16[2048,1536]{1,0:T(8,128)(2,1)}) custom-call(bf16[1536,2048]{1,0:T(8,128)(2,1)} %refs_0_.2, bf16[1536,2048]{1,0:T(8,128)(2,1)} %refs_1_.2, bf16[128,768]{1,0:T(8,128)(2,1)} %get-tuple-element.41.refs_2_.x_hbm), custom_call_target="tpu_custom_call" | custom-call | tf_op jit(solution)/shard_map/pallas_call | solution.py:68
  40.1 9.3 %all-to-all-done = bf16[128,8,768]{2,1,0:T(8,128)(2,1)S(1)} async-done(((bf16[128,8,768]{2,1,0:T(8,128)(2,1)}), bf16[128,8,768]{2,1,0:T(8,128)(2,1)S(1)}, u32[]{:S(2)}, u32[]{:S(2)}) %all-to-all-start) | async-done | bytes 1572896 | tf_op jit(solution)/shard_map/all_to_all | solution.py:719
  49.3 2.0 %shard_map.107 = (bf16[4,512,192]{2,1,0:T(8,128)(2,1)S(1)}, bf16[4,192,512]{2,1,0:T(8,128)(2,1)S(1)}, bf16[128,192]{1,0:T(8,128)(2,1)S(1)}) custom-call(s32[2,16]{1,0:T(2,128)S(1)} %copy-done.3, bf16[1024,768]{1,0:T(8,128)(2,1)S(1)} %bitcast.8, s32[8,1024]{1,0:T(8,128)S(1)} %get-tuple-element.40.tab_ref, bf16[2048,1536]{1,0:T(8,128)(2,1)} %get-tuple-element.42._after_hbm.gate_hbm), custom_call_target="tpu_custom_call" | custom-call | tf_op jit(solution)/shard_map/pallas_call | solution.py:68
  51.3 0.1 collective-permute-start.2
  51.4 1.0 collective-permute-start.1
  52.4 3.2 %collective-permute-start = (bf16[128,192]{1,0:T(8,128)(2,1)S(1)}, bf16[128,192]{1,0:T(8,128)(2,1)S(1)}, u32[]{:S(2)}, u32[]{:S(2)}) collective-permute-start(bf16[128,192]{1,0:T(8,128)(2,1)S(1)} %get-tuple-element.49.a0_ref), channel_id=1, source_target_pairs={{0,16},{4,20},{8,24},{12,28},{16,0},{20,4},{24,8},{28,12},{32,48},... | collective-permute-start | bytes 147464 | tf_op jit(solution)/shard_map/ppermute | solution.py:695
  55.5 3.2 %shard_map.108 = (bf16[4,512,512]{2,1,0:T(8,128)(2,1)S(1)}, bf16[4,512,512]{2,1,0:T(8,128)(2,1)S(1)}, bf16[512,512]{1,0:T(8,128)(2,1)S(1)}, bf16[512,512]{1,0:T(...) custom-call(s32[2,16]{1,0:T(2,128)S(1)} %copy-done.3, ...), custom_call_target="tpu_custom_call" | custom-call | tf_op jit(solution)/shard_map/pallas_call | solution.py:68
  58.8 2.0 %shard_map.110 = (bf16[48,512]{1,0:T(8,128)(2,1)}, bf16[48,512]{1,0:T(8,128)(2,1)}, bf16[48,512]{1,0:T(8,128)(2,1)}, bf16[48,512]{1,0:T(8,128)(2,1)}, bf16[4,48,...) custom-call(s32[2,16]{1,0:T(2,128)S(1)} %copy-done.3, ...), custom_call_target="tpu_custom_call" | custom-call | tf_op jit(solution)/shard_map/pallas_call | solution.py:68
  60.8 1.4 %collective-permute-start.6 = (bf16[96,128]{1,0:T(8,128)(2,1)S(1)}, bf16[96,128]{1,0:T(8,128)(2,1)S(1)}, u32[]{:S(2)}, u32[]{:S(2)}) collective-permute-start(bf16[96,128]{1,0:T(8,128)(2,1)S(1)} %get-tuple-element.60), channel_id=1, source_target_pairs={{0,16},{4,20},{8,24},{12,28},{16,0},{20,4},{24,8},{28,12},{32,48},... | collective-permute-start | bytes 73736 | tf_op jit(solution)/shard_map/ppermute | solution.py:695
  62.2 0.4 collective-permute-start.7
  62.6 2.5 %collective-permute-start.8 = (bf16[96,128]{1,0:T(8,128)(2,1)S(1)}, bf16[96,128]{1,0:T(8,128)(2,1)S(1)}, u32[]{:S(2)}, u32[]{:S(2)}) collective-permute-start(bf16[96,128]{1,0:T(8,128)(2,1)S(1)} %get-tuple-element.62), channel_id=1, source_target_pairs={{0,48},{4,52},{8,56},{12,60},{16,32},{20,36},{24,40},{28,44},{32,1... | collective-permute-start | bytes 73736 | tf_op jit(solution)/shard_map/ppermute | solution.py:695
  65.0 3.7 %shard_map.111.dall_ref = f32[4,144,512]{2,1,0:T(8,128)S(1)} custom-call(s32[2,16]{1,0:T(2,128)S(1)} %copy-done.3, bf16[4,512,192]{2,1,0:T(8,128)(2,1)S(1)} %get-tuple-element.43.y_ref, bf16[4,192,512]{2,1,0:T(8,128)(2,1)S(1)} %get-tuple-element.44.yt_ref, bf16[4,512,512]{2,1,0:T(8,128)(2,1)S(1)} %get-tuple-element.45.e0_ref, ...), custom_call_target="tpu_custom_call" | custom-call | tf_op jit(solution)/shard_map/pallas_call | solution.py:68
  68.8 3.0 %shard_map.112.refs_3_ = bf16[1024,768]{1,0:T(8,128)(2,1)} custom-call(s32[2,16]{1,0:T(2,128)S(1)} %copy-done.3, f32[4,144,512]{2,1,0:T(8,128)S(1)} %shard_map.111.dall_ref, f32[96,128]{1,0:T(8,128)S(1)} %get-tuple-element.58.own_ref, f32[48,128]{1,0:T(8,128)S(1)} %get-tuple-element.59.dq_ref, bf16[96,128]{1,0:T(8,128)(2,1)S(1)} %collective-permute-done.6.r1_ref, ...), custom_call_target="tpu_custom_call" | custom-call | tf_op jit(solution)/shard_map/pallas_call | solution.py:68
  71.8 0.0 copy-start.6
  71.9 6.9 %all-to-all-start.1 = ((bf16[128,8,768]{2,1,0:T(8,128)(2,1)}), bf16[128,8,768]{2,1,0:T(8,128)(2,1)S(1)}, u32[]{:S(2)}, u32[]{:S(2)}) async-start(bf16[128,8,768]{2,1,0:T(8,128)(2,1)} %bitcast.13), calls=%async_computation.1 | async-start | bytes 3145728 | tf_op jit(solution)/shard_map/all_to_all | solution.py:719
  78.8 1.1 collective-permute-start.9
  79.9 0.8 collective-permute-start.10
  80.7 0.9 collective-permute-start.11
  81.6 12.2 %shard_map.113 = (bf16[1536,2048]{1,0:T(8,128)(2,1)}, bf16[768,1536]{1,0:T(8,128)(2,1)}, bf16[2304,768]{1,0:T(8,128)(2,1)}) custom-call(bf16[2048,1536]{1,0:T(8,128)(2,1)} %refs_0_.3, bf16[1536,768]{1,0:T(8,128)(2,1)} %refs_1_.3, bf16[768,2304]{1,0:T(8,128)(2,1)} %refs_2_.1, bf16[1024,768]{1,0:T(8,128)(2,1)} %shard_map.112.refs_3_), custom_call_target="tpu_custom_call" | custom-call | tf_op jit(solution)/shard_map/pallas_call | solution.py:68
  93.9 3.8 %collective-permute-done.11.s3_any = bf16[48,512]{1,0:T(8,128)(2,1)S(1)} collective-permute-done((bf16[48,512]{1,0:T(8,128)(2,1)S(1)}, bf16[48,512]{1,0:T(8,128)(2,1)S(1)}, u32[]{:S(2)}, u32[]{:S(2)}) %collective-permute-start.11) | collective-permute-done | bytes 49184 | tf_op jit(solution)/shard_map/ppermute | solution.py:695
  97.6 6.5 %all-to-all-done.1 = bf16[128,8,768]{2,1,0:T(8,128)(2,1)S(1)} async-done(((bf16[128,8,768]{2,1,0:T(8,128)(2,1)}), bf16[128,8,768]{2,1,0:T(8,128)(2,1)S(1)}, u32[]{:S(2)}, u32[]{:S(2)}) %all-to-all-start.1) | async-done | bytes 1572896 | tf_op jit(solution)/shard_map/all_to_all | solution.py:719
  104.1 11.8 %shard_map.114 = (bf16[128,1536]{1,0:T(8,128)(2,1)}, bf16[192,512]{1,0:T(8,128)(2,1)}) custom-call(bf16[8,128,768]{2,1,0:T(8,128)(2,1)S(1)} %bitcast.7, bf16[48,512]{1,0:T(8,128)(2,1)S(1)} %copy-done.2, bf16[48,512]{1,0:T(8,128)(2,1)S(1)} %collective-permute-done.9.s1_any, bf16[48,512]{1,0:T(8,128)(2,1)S(1)} %collective-permute-done.10.s2_any, ...), custom_call_target="tpu_custom_call" | custom-call | tf_op jit(solution)/shard_map/pallas_call | solution.py:68
  (21 shorter events, 0.0 us)
Async XLA Ops:
  12.4 11.5 %copy-start.1 = (bf16[512,192]{0,1:T(8,128)(2,1)S(1)}, bf16[512,192]{0,1:T(8,128)(2,1)}, u32[]{:S(2)}) copy-start(bf16[512,192]{0,1:T(8,128)(2,1)} %param.17) | copy-start | bytes 589828
  12.4 14.7 %copy-start = (s32[16384]{0:T(1024)S(1)}, s32[16384]{0:T(1024)}, u32[]{:S(2)}) copy-start(s32[16384]{0:T(1024)} %param.15) | copy-start | bytes 196612
  12.4 36.9 %all-to-all-start = ((bf16[128,8,768]{2,1,0:T(8,128)(2,1)}), bf16[128,8,768]{2,1,0:T(8,128)(2,1)S(1)}, u32[]{:S(2)}, u32[]{:S(2)}) async-start(bf16[128,8,768]{2,1,0:T(8,128)(2,1)} %bitcast.14), calls=%async_computation | async-start | bytes 3145728 | tf_op jit(solution)/shard_map/all_to_all | solution.py:719
  24.3 28.1 %collective-permute-start.3 = (bf16[48,512]{1,0:T(8,128)(2,1)S(1)}, bf16[48,512]{1,0:T(8,128)(2,1)S(1)}, u32[]{:S(2)}, u32[]{:S(2)}) collective-permute-start(bf16[48,512]{1,0:T(8,128)(2,1)S(1)} %get-tuple-element.53), channel_id=1, source_target_pairs={{0,4},{4,0},{8,12},{12,8},{16,20},{20,16},{24,28},{28,24},{32,36},... | collective-permute-start | bytes 147464 | tf_op jit(solution)/shard_map/ppermute | solution.py:695
  25.4 33.3 %collective-permute-start.4 = (bf16[48,512]{1,0:T(8,128)(2,1)S(1)}, bf16[48,512]{1,0:T(8,128)(2,1)S(1)}, u32[]{:S(2)}, u32[]{:S(2)}) collective-permute-start(bf16[48,512]{1,0:T(8,128)(2,1)S(1)} %get-tuple-element.54), channel_id=1, source_target_pairs={{0,8},{4,12},{8,0},{12,4},{16,24},{20,28},{24,16},{28,20},{32,40},... | collective-permute-start | bytes 147464 | tf_op jit(solution)/shard_map/ppermute | solution.py:695
  26.2 32.5 %collective-permute-start.5 = (bf16[48,512]{1,0:T(8,128)(2,1)S(1)}, bf16[48,512]{1,0:T(8,128)(2,1)S(1)}, u32[]{:S(2)}, u32[]{:S(2)}) collective-permute-start(bf16[48,512]{1,0:T(8,128)(2,1)S(1)} %get-tuple-element.55), channel_id=1, source_target_pairs={{0,12},{4,8},{8,4},{12,0},{16,28},{20,24},{24,20},{28,16},{32,44},... | collective-permute-start | bytes 147464 | tf_op jit(solution)/shard_map/ppermute | solution.py:695
  28.1 21.2 %copy-start.3 = (s32[2,16]{1,0:T(2,128)S(1)}, s32[2,16]{1,0:T(2,128)}, u32[]{:S(2)}) copy-start(s32[2,16]{1,0:T(2,128)} %shift_ref.9) | copy-start | bytes 388
  51.3 7.5 %collective-permute-start.2 = (bf16[128,192]{1,0:T(8,128)(2,1)S(1)}, bf16[128,192]{1,0:T(8,128)(2,1)S(1)}, u32[]{:S(2)}, u32[]{:S(2)}) collective-permute-start(bf16[128,192]{1,0:T(8,128)(2,1)S(1)} %get-tuple-element.49.a0_ref), channel_id=1, source_target_pairs={{0,48},{4,52},{8,56},{12,60},{16,32},{20,36},{24,40},{28,44},{32,1... | collective-permute-start | bytes 147464 | tf_op jit(solution)/shard_map/ppermute | solution.py:695
  51.4 7.4 %collective-permute-start.1 = (bf16[128,192]{1,0:T(8,128)(2,1)S(1)}, bf16[128,192]{1,0:T(8,128)(2,1)S(1)}, u32[]{:S(2)}, u32[]{:S(2)}) collective-permute-start(bf16[128,192]{1,0:T(8,128)(2,1)S(1)} %get-tuple-element.49.a0_ref), channel_id=1, source_target_pairs={{0,32},{4,36},{8,40},{12,44},{16,48},{20,52},{24,56},{28,60},{32,0... | collective-permute-start | bytes 147464 | tf_op jit(solution)/shard_map/ppermute | solution.py:695
  52.4 6.4 %collective-permute-start = (bf16[128,192]{1,0:T(8,128)(2,1)S(1)}, bf16[128,192]{1,0:T(8,128)(2,1)S(1)}, u32[]{:S(2)}, u32[]{:S(2)}) collective-permute-start(bf16[128,192]{1,0:T(8,128)(2,1)S(1)} %get-tuple-element.49.a0_ref), channel_id=1, source_target_pairs={{0,16},{4,20},{8,24},{12,28},{16,0},{20,4},{24,8},{28,12},{32,48},... | collective-permute-start | bytes 147464 | tf_op jit(solution)/shard_map/ppermute | solution.py:695
  60.8 8.0 %collective-permute-start.6 = (bf16[96,128]{1,0:T(8,128)(2,1)S(1)}, bf16[96,128]{1,0:T(8,128)(2,1)S(1)}, u32[]{:S(2)}, u32[]{:S(2)}) collective-permute-start(bf16[96,128]{1,0:T(8,128)(2,1)S(1)} %get-tuple-element.60), channel_id=1, source_target_pairs={{0,16},{4,20},{8,24},{12,28},{16,0},{20,4},{24,8},{28,12},{32,48},... | collective-permute-start | bytes 73736 | tf_op jit(solution)/shard_map/ppermute | solution.py:695
  62.2 6.6 %collective-permute-start.7 = (bf16[96,128]{1,0:T(8,128)(2,1)S(1)}, bf16[96,128]{1,0:T(8,128)(2,1)S(1)}, u32[]{:S(2)}, u32[]{:S(2)}) collective-permute-start(bf16[96,128]{1,0:T(8,128)(2,1)S(1)} %get-tuple-element.61), channel_id=1, source_target_pairs={{0,32},{4,36},{8,40},{12,44},{16,48},{20,52},{24,56},{28,60},{32,0... | collective-permute-start | bytes 73736 | tf_op jit(solution)/shard_map/ppermute | solution.py:695
  62.6 6.2 %collective-permute-start.8 = (bf16[96,128]{1,0:T(8,128)(2,1)S(1)}, bf16[96,128]{1,0:T(8,128)(2,1)S(1)}, u32[]{:S(2)}, u32[]{:S(2)}) collective-permute-start(bf16[96,128]{1,0:T(8,128)(2,1)S(1)} %get-tuple-element.62), channel_id=1, source_target_pairs={{0,48},{4,52},{8,56},{12,60},{16,32},{20,36},{24,40},{28,44},{32,1... | collective-permute-start | bytes 73736 | tf_op jit(solution)/shard_map/ppermute | solution.py:695
  71.8 6.9 %copy-start.6 = (bf16[48,512]{1,0:T(8,128)(2,1)S(1)}, bf16[48,512]{1,0:T(8,128)(2,1)}, u32[]{:S(2)}) copy-start(bf16[48,512]{1,0:T(8,128)(2,1)} %get-tuple-element.65) | copy-start | bytes 147460
  71.9 8.0 %copy-start.5 = (bf16[48,512]{1,0:T(8,128)(2,1)S(1)}, bf16[48,512]{1,0:T(8,128)(2,1)}, u32[]{:S(2)}) copy-start(bf16[48,512]{1,0:T(8,128)(2,1)} %get-tuple-element.66) | copy-start | bytes 147460
  71.9 8.8 %copy-start.4 = (bf16[48,512]{1,0:T(8,128)(2,1)S(1)}, bf16[48,512]{1,0:T(8,128)(2,1)}, u32[]{:S(2)}) copy-start(bf16[48,512]{1,0:T(8,128)(2,1)} %get-tuple-element.67) | copy-start | bytes 147460
  71.9 32.2 %all-to-all-start.1 = ((bf16[128,8,768]{2,1,0:T(8,128)(2,1)}), bf16[128,8,768]{2,1,0:T(8,128)(2,1)S(1)}, u32[]{:S(2)}, u32[]{:S(2)}) async-start(bf16[128,8,768]{2,1,0:T(8,128)(2,1)} %bitcast.13), calls=%async_computation.1 | async-start | bytes 3145728 | tf_op jit(solution)/shard_map/all_to_all | solution.py:719
  78.8 15.1 %collective-permute-start.9 = (bf16[48,512]{1,0:T(8,128)(2,1)S(1)}, bf16[48,512]{1,0:T(8,128)(2,1)S(1)}, u32[]{:S(2)}, u32[]{:S(2)}) collective-permute-start(bf16[48,512]{1,0:T(8,128)(2,1)S(1)} %copy-done.6), channel_id=1, source_target_pairs={{0,4},{4,0},{8,12},{12,8},{16,20},{20,16},{24,28},{28,24},{32,36},... | collective-permute-start | bytes 147464 | tf_op jit(solution)/shard_map/ppermute | solution.py:695
  79.9 13.9 %collective-permute-start.10 = (bf16[48,512]{1,0:T(8,128)(2,1)S(1)}, bf16[48,512]{1,0:T(8,128)(2,1)S(1)}, u32[]{:S(2)}, u32[]{:S(2)}) collective-permute-start(bf16[48,512]{1,0:T(8,128)(2,1)S(1)} %copy-done.5), channel_id=1, source_target_pairs={{0,8},{4,12},{8,0},{12,4},{16,24},{20,28},{24,16},{28,20},{32,40},... | collective-permute-start | bytes 147464 | tf_op jit(solution)/shard_map/ppermute | solution.py:695
  80.7 23.4 %copy-start.2 = (bf16[48,512]{1,0:T(8,128)(2,1)S(1)}, bf16[48,512]{1,0:T(8,128)(2,1)}, u32[]{:S(2)}) copy-start(bf16[48,512]{1,0:T(8,128)(2,1)} %get-tuple-element.64.s0_any) | copy-start | bytes 147460
  80.7 16.9 %collective-permute-start.11 = (bf16[48,512]{1,0:T(8,128)(2,1)S(1)}, bf16[48,512]{1,0:T(8,128)(2,1)S(1)}, u32[]{:S(2)}, u32[]{:S(2)}) collective-permute-start(bf16[48,512]{1,0:T(8,128)(2,1)S(1)} %copy-done.4), channel_id=1, source_target_pairs={{0,12},{4,8},{8,4},{12,0},{16,28},{20,24},{24,20},{28,16},{32,44},... | collective-permute-start | bytes 147464 | tf_op jit(solution)/shard_map/ppermute | solution.py:695
